TPU v7x, 1024 devices: a whole 4x8x16 slice. The times are simulated.
1024 devices in a mesh: depth: 32 (over y, x_lo, core), rows: 32 (over z, x_hi).
Axes of the slice: x: 4 (x_hi: 2, x_lo: 2; x = x_hi * 2 + x_lo), y: 8, z: 16, core: 2. Of those that a mesh axis runs over, the one named last changes fastest.
Arguments:
- projections: bfloat16 [32, 1024, 4096], P('depth', 'rows'), may hold values from -6 to 6
- owner: int32 [4], replicated, may hold values from 0 to 31, as said below
- row_offset: int32 [4, 128], P(None, 'depth'), may hold values from -14 to 14
- band_start: int32 [4, 1024], P(None, 'rows'), may hold values from -16 to 12
- taps: bfloat16 [4, 128, 4], P(None, 'depth'), may hold values from 0.19921875 to 1
Outputs:
- volume: float32 [128, 1024, 4096], P('depth', 'rows')
Inputs may be any that keep to these rules, and one draw needn't show every extreme that they name: `owner`: the 4 entries are distinct slots.
All inputs are finite; a program needn't handle non-finite values.
Results may differ from a plain program's by a relative error of at most 0.0003.
Values may be sent and summed in bfloat16 or wider, within the bound.
No kernel may reach another device: no remote copies, remote signals or barrier semaphores. Data moves between devices by JAX's collectives and lax.ppermute only.
A program may use at most 32 MiB of HBM per device.

v0:
```python
import jax
import jax.numpy as jnp
from jax import lax
from jax.sharding import PartitionSpec as P

RATE = 0.14
INV_KAPPA2 = 0.25


def spread(block, axis, owner):
    block = jnp.where(lax.axis_index(axis) == owner, block, jnp.zeros_like(block))
    return lax.psum(block, axis)


def padded_2(cells, sides, width):
    for axis, dim in sides:
        count = lax.axis_size(axis)
        ends = count - 1
        head = lax.slice_in_dim(cells, 0, width, axis=dim)
        tail = lax.slice_in_dim(cells, cells.shape[dim] - width, cells.shape[dim], axis=dim)
        cells = jnp.concatenate(
            [
                lax.ppermute(tail, axis, [(i, (i + 1) % count) for i in range(ends)]),
                cells,
                lax.ppermute(head, axis, [((i + 1) % count, i) for i in range(ends)]),
            ],
            axis=dim,
        )
    return cells


def conduct(diff):
    return diff / (1.0 + diff * diff * INV_KAPPA2)


def sweep(padded, first_slice, first_row, all_slices, all_rows):
    center = padded[1:-1, 1:-1, :]
    count_s = center.shape[0]
    count_r = center.shape[1]
    slice_ids = first_slice + jnp.arange(count_s, dtype=jnp.int32)
    row_ids = first_row + jnp.arange(count_r, dtype=jnp.int32)
    lower = (slice_ids > 0)[:, None, None]
    upper = (slice_ids < all_slices - 1)[:, None, None]
    left = (row_ids > 0)[None, :, None]
    right = (row_ids < all_rows - 1)[None, :, None]
    total = jnp.where(lower, conduct(padded[:-2, 1:-1, :] - center), 0.0)
    total = total + jnp.where(upper, conduct(padded[2:, 1:-1, :] - center), 0.0)
    total = total + jnp.where(left, conduct(padded[1:-1, :-2, :] - center), 0.0)
    total = total + jnp.where(right, conduct(padded[1:-1, 2:, :] - center), 0.0)
    steps = conduct(center[:, :, 1:] - center[:, :, :-1])
    zero_col = jnp.zeros_like(center[:, :, :1])
    total = (
        total
        + jnp.concatenate([steps, zero_col], axis=2)
        - jnp.concatenate([zero_col, steps], axis=2)
    )
    return center + RATE * total


def backproject(stacked, offsets, bands, weights, rows_here):
    views = offsets.shape[0]
    band = weights.shape[2]
    count_r = bands.shape[1]
    span = 3 * rows_here
    row_ids = jnp.arange(count_r, dtype=jnp.int32)
    view_ids = jnp.arange(views, dtype=jnp.int32)
    tap_ids = jnp.arange(band, dtype=jnp.int32)
    target = (
        view_ids[None, None, :, None] * span
        + rows_here
        + row_ids[None, :, None, None]
        + jnp.transpose(offsets)[:, None, :, None]
        + jnp.transpose(bands)[None, :, :, None]
        + tap_ids[None, None, None, :]
    )
    columns = jnp.arange(views * span, dtype=jnp.int32)
    weight = jnp.transpose(weights, (1, 0, 2)).astype(jnp.float32)[:, None, :, :, None]
    matched = target[..., None] == columns
    interp = jnp.sum(jnp.where(matched, weight, 0.0), axis=(2, 3)).astype(jnp.bfloat16)
    return jnp.einsum("srj,jc->src", interp, stacked, preferred_element_type=jnp.float32)


def shards(projections, owner, row_offset, band_start, taps):
    stored = projections[0]
    rows_here = stored.shape[0]
    slices_here = row_offset.shape[1]
    views = owner.shape[0]
    tiles = []
    for view in range(views):
        single = spread(stored, "depth", owner[view])
        tiles.append(padded_2(single, (("rows", 0),), rows_here))
    stacked = jnp.concatenate(tiles, axis=0)
    first_slice = lax.axis_index("depth") * slices_here
    first_row = lax.axis_index("rows") * rows_here
    all_slices = lax.axis_size("depth") * slices_here
    all_rows = lax.axis_size("rows") * rows_here
    volume = backproject(stacked, row_offset, band_start, taps, rows_here)
    for sweep_no in range(2):
        padded = padded_2(volume, (("depth", 0), ("rows", 1)), 1)
        volume = sweep(padded, first_slice, first_row, all_slices, all_rows)
    return volume


def solution(mesh):
    placed = (
        P("depth", "rows", None),
        P(),
        P(None, "depth"),
        P(None, "rows"),
        P(None, "depth", None),
    )
    return jax.shard_map(
        shards, mesh=mesh, in_specs=placed, out_specs=P("depth", "rows", None), check_vma=False
    )
```

profile of v0, /device:TPU:1, one launch (start us, length us, event | category | flops | bytes accessed | tf_op | source)
XLA Modules:
  0.0 388.8 jit_solution(4934945050571242285)
XLA Ops:
  6.5 1.5 fusion.17
  10.6 2.0 select_bitcast_fusion
  12.9 252.3 %all-reduce.7.cloned.1.call-done = (bf16[32,4096]{1,0:T(8,128)(2,1)}, bf16[32,4096]{1,0:T(8,128)(2,1)}, bf16[32,4096]{1,0:T(8,128)(2,1)}, bf16[32,4096]{1,0:T(8,128)(2,1)}) async-done(((bf16[32,4096]{1,0:T(8,128)(2,1)}, bf16[32,4096]{1,0:T(8,128)(2,1)}, bf16[32,4096]{1,0:T(8,128)(2,1)}, bf16[32,4096]{1,0:T(8,128)(2,1)}), (bf16[32,4096]{1,0:T(8,128)(2,1)}, bf16[32,4096]{1,0:T(8,128)(2,1)}, ...) | async-done | bytes 1048592 | tf_op jit(solution)/shard_map/psum | solution.py:12
  265.2 4.5 %collective-permute-start = (bf16[32,4096]{1,0:T(8,128)(2,1)}, bf16[32,4096]{1,0:T(8,128)(2,1)S(1)}, u32[]{:S(2)}, u32[]{:S(2)}) collective-permute-start(bf16[32,4096]{1,0:T(8,128)(2,1)} %get-tuple-element.5), channel_id=1, source_target_pairs={{0,1},{1,2},{2,3},{3,4},{4,5},{5,6},{6,7},{7,8},{8,9},{9,10},{10,1... | collective-permute-start | bytes 786440 | tf_op jit(solution)/shard_map/ppermute | solution.py:23
  270.3 1.3 collective-permute-start.1
  271.6 5.5 %collective-permute-start.2 = (bf16[32,4096]{1,0:T(8,128)(2,1)}, bf16[32,4096]{1,0:T(8,128)(2,1)S(1)}, u32[]{:S(2)}, u32[]{:S(2)}) collective-permute-start(bf16[32,4096]{1,0:T(8,128)(2,1)} %get-tuple-element.6), channel_id=1, source_target_pairs={{0,1},{1,2},{2,3},{3,4},{4,5},{5,6},{6,7},{7,8},{8,9},{9,10},{10,1... | collective-permute-start | bytes 786440 | tf_op jit(solution)/shard_map/ppermute | solution.py:23
  277.2 1.3 collective-permute-start.3
  278.5 5.5 %collective-permute-start.4 = (bf16[32,4096]{1,0:T(8,128)(2,1)}, bf16[32,4096]{1,0:T(8,128)(2,1)S(1)}, u32[]{:S(2)}, u32[]{:S(2)}) collective-permute-start(bf16[32,4096]{1,0:T(8,128)(2,1)} %get-tuple-element.7), channel_id=1, source_target_pairs={{0,1},{1,2},{2,3},{3,4},{4,5},{5,6},{6,7},{7,8},{8,9},{9,10},{10,1... | collective-permute-start | bytes 786440 | tf_op jit(solution)/shard_map/ppermute | solution.py:23
  284.0 1.3 collective-permute-start.5
  285.3 1.0 constant_dynamic-update-slice_fusion.10
  286.3 6.1 %collective-permute-start.6 = (bf16[32,4096]{1,0:T(8,128)(2,1)}, bf16[32,4096]{1,0:T(8,128)(2,1)S(1)}, u32[]{:S(2)}, u32[]{:S(2)}) collective-permute-start(bf16[32,4096]{1,0:T(8,128)(2,1)} %get-tuple-element.8), channel_id=1, source_target_pairs={{0,1},{1,2},{2,3},{3,4},{4,5},{5,6},{6,7},{7,8},{8,9},{9,10},{10,1... | collective-permute-start | bytes 786440 | tf_op jit(solution)/shard_map/ppermute | solution.py:23
  292.5 5.8 %collective-permute-done.2 = bf16[32,4096]{1,0:T(8,128)(2,1)S(1)} collective-permute-done((bf16[32,4096]{1,0:T(8,128)(2,1)}, bf16[32,4096]{1,0:T(8,128)(2,1)S(1)}, u32[]{:S(2)}, u32[]{:S(2)}) %collective-permute-start.2) | collective-permute-done | bytes 262176 | tf_op jit(solution)/shard_map/ppermute | solution.py:23
  298.3 1.3 collective-permute-start.7
  299.7 4.2 %collective-permute-done.4 = bf16[32,4096]{1,0:T(8,128)(2,1)S(1)} collective-permute-done((bf16[32,4096]{1,0:T(8,128)(2,1)}, bf16[32,4096]{1,0:T(8,128)(2,1)S(1)}, u32[]{:S(2)}, u32[]{:S(2)}) %collective-permute-start.4) | collective-permute-done | bytes 262176 | tf_op jit(solution)/shard_map/ppermute | solution.py:23
  304.0 11.1 %collective-permute-done.6 = bf16[32,4096]{1,0:T(8,128)(2,1)S(1)} collective-permute-done((bf16[32,4096]{1,0:T(8,128)(2,1)}, bf16[32,4096]{1,0:T(8,128)(2,1)S(1)}, u32[]{:S(2)}, u32[]{:S(2)}) %collective-permute-start.6) | collective-permute-done | bytes 262176 | tf_op jit(solution)/shard_map/ppermute | solution.py:23
  315.2 0.7 fusion
  315.9 1.1 fusion.16
  317.0 1.9 collective-permute-start.8
  318.9 2.4 collective-permute-start.9
  321.4 10.3 %collective-permute-done.8 = f32[1,32,4096]{2,1,0:T(8,128)S(1)} collective-permute-done((f32[1,32,4096]{2,1,0:T(8,128)}, f32[1,32,4096]{2,1,0:T(8,128)S(1)}, u32[]{:S(2)}, u32[]{:S(2)}) %collective-permute-start.8) | collective-permute-done | bytes 524320 | tf_op jit(solution)/shard_map/ppermute | solution.py:23
  331.8 4.8 %collective-permute-start.10 = (f32[6,1,4096]{2,1,0:T(1,128)S(1)}, f32[6,1,4096]{2,1,0:T(1,128)S(1)}, u32[]{:S(2)}, u32[]{:S(2)}) collective-permute-start(f32[6,1,4096]{2,1,0:T(1,128)S(1)} %get-tuple-element.11), channel_id=1, source_target_pairs={{0,1},{1,2},{2,3},{3,4},{4,5},{5,6},{6,7},{7,8},{8,9},{9,10},{10,1... | collective-permute-start | bytes 294920 | tf_op jit(solution)/shard_map/ppermute | solution.py:23
  336.6 1.3 collective-permute-start.11
  338.6 5.8 %collective-permute-done.11 = f32[6,1,4096]{2,1,0:T(1,128)S(1)} collective-permute-done((f32[6,1,4096]{2,1,0:T(1,128)S(1)}, f32[6,1,4096]{2,1,0:T(1,128)S(1)}, u32[]{:S(2)}, u32[]{:S(2)}) %collective-permute-start.11) | collective-permute-done | bytes 98336 | tf_op jit(solution)/shard_map/ppermute | solution.py:25
  344.4 3.4 multiply_add_fusion.1
  347.9 5.4 %collective-permute-start.12 = (f32[1,32,4096]{2,1,0:T(8,128)S(1)}, f32[1,32,4096]{2,1,0:T(8,128)S(1)}, u32[]{:S(2)}, u32[]{:S(2)}) collective-permute-start(f32[1,32,4096]{2,1,0:T(8,128)S(1)} %get-tuple-element.13), channel_id=1, source_target_pairs={{0,32},{32,64},{64,96},{96,128},{128,160},{160,192},{192,224},{224... | collective-permute-start | bytes 1572872 | tf_op jit(solution)/shard_map/ppermute | solution.py:23
  353.3 1.9 collective-permute-start.13
  355.2 8.2 %collective-permute-done.12 = f32[1,32,4096]{2,1,0:T(8,128)S(1)} collective-permute-done((f32[1,32,4096]{2,1,0:T(8,128)S(1)}, f32[1,32,4096]{2,1,0:T(8,128)S(1)}, u32[]{:S(2)}, u32[]{:S(2)}) %collective-permute-start.12) | collective-permute-done | bytes 524320 | tf_op jit(solution)/shard_map/ppermute | solution.py:23
  364.0 6.9 %collective-permute-start.14 = (f32[6,1,4096]{2,1,0:T(1,128)S(1)}, f32[6,1,4096]{2,1,0:T(1,128)S(1)}, u32[]{:S(2)}, u32[]{:S(2)}) collective-permute-start(f32[6,1,4096]{2,1,0:T(1,128)S(1)} %get-tuple-element.9), channel_id=1, source_target_pairs={{0,1},{1,2},{2,3},{3,4},{4,5},{5,6},{6,7},{7,8},{8,9},{9,10},{10,1... | collective-permute-start | bytes 294920 | tf_op jit(solution)/shard_map/ppermute | solution.py:23
  370.9 1.3 collective-permute-start.15
  372.2 0.6 add_divide_fusion
  372.8 4.9 %collective-permute-done.15 = f32[6,1,4096]{2,1,0:T(1,128)S(1)} collective-permute-done((f32[6,1,4096]{2,1,0:T(1,128)S(1)}, f32[6,1,4096]{2,1,0:T(1,128)S(1)}, u32[]{:S(2)}, u32[]{:S(2)}) %collective-permute-start.15) | collective-permute-done | bytes 98336 | tf_op jit(solution)/shard_map/ppermute | solution.py:25
  377.8 4.2 %multiply_add_fusion = f32[4,32,4096]{2,1,0:T(8,128)} fusion(f32[4,32,4096]{2,1,0:T(8,128)S(1)} %multiply_add_fusion.1, f32[4,32,4095]{2,1,0:T(8,128)S(1)} %add_divide_fusion, f32[6,1,4096]{2,1,0:T(1,128)S(1)} %collective-permute-done.15, f32[1,32,4096]{2,1,0:T(8,128)S(1)} %collective-permute-done.13, f32[1,32,4096]{2,1,0:T(8,128)S(1)} %collective-permute-done.12, ...), kind=kLoop, calls=%fused_computation.30 | loop fusion | flops 20447232 | bytes 7536200 | tf_op jit(solution)/shard_map/add | solution.py:57
  (48 shorter events, 2.4 us)
Async XLA Ops:
  6.5 6.1 %copy-start.5 = (s32[4,4]{1,0:T(4,128)S(1)}, s32[4,4]{1,0:T(4,128)}, u32[]{:S(2)}) copy-start(s32[4,4]{1,0:T(4,128)} %param.7) | copy-start | bytes 196
  6.5 6.2 %copy-start.4 = (s32[4,32]{1,0:T(4,128)S(1)}, s32[4,32]{1,0:T(4,128)}, u32[]{:S(2)}) copy-start(s32[4,32]{1,0:T(4,128)} %param.8) | copy-start | bytes 1540
  6.5 263.2 %copy-start.3 = (bf16[4,4,4]{2,1,0:T(4,128)(2,1)S(1)}, bf16[4,4,4]{2,1,0:T(4,128)(2,1)}, u32[]{:S(2)}) copy-start(bf16[4,4,4]{2,1,0:T(4,128)(2,1)} %param.9) | copy-start | bytes 388
  6.5 258.7 %all-reduce.7.cloned.1.call-start = ((), (), s32[]{:S(2)}) async-start(), calls=%async_computation | async-start | bytes 2097152 | tf_op jit(solution)/shard_map/psum | solution.py:12
  265.2 34.4 %copy-start.2 = (bf16[32,4096]{1,0:T(8,128)(2,1)S(1)}, bf16[32,4096]{1,0:T(8,128)(2,1)}, u32[]{:S(2)}) copy-start(bf16[32,4096]{1,0:T(8,128)(2,1)} %get-tuple-element.6) | copy-start | bytes 786436
  265.2 38.7 %copy-start.1 = (bf16[32,4096]{1,0:T(8,128)(2,1)S(1)}, bf16[32,4096]{1,0:T(8,128)(2,1)}, u32[]{:S(2)}) copy-start(bf16[32,4096]{1,0:T(8,128)(2,1)} %get-tuple-element.7) | copy-start | bytes 786436
  265.2 18.8 %collective-permute-start = (bf16[32,4096]{1,0:T(8,128)(2,1)}, bf16[32,4096]{1,0:T(8,128)(2,1)S(1)}, u32[]{:S(2)}, u32[]{:S(2)}) collective-permute-start(bf16[32,4096]{1,0:T(8,128)(2,1)} %get-tuple-element.5), channel_id=1, source_target_pairs={{0,1},{1,2},{2,3},{3,4},{4,5},{5,6},{6,7},{7,8},{8,9},{9,10},{10,1... | collective-permute-start | bytes 786440 | tf_op jit(solution)/shard_map/ppermute | solution.py:23
  270.3 15.9 %collective-permute-start.1 = (bf16[32,4096]{1,0:T(8,128)(2,1)}, bf16[32,4096]{1,0:T(8,128)(2,1)S(1)}, u32[]{:S(2)}, u32[]{:S(2)}) collective-permute-start(bf16[32,4096]{1,0:T(8,128)(2,1)} %get-tuple-element.5), channel_id=1, source_target_pairs={{1,0},{2,1},{3,2},{4,3},{5,4},{6,5},{7,6},{8,7},{9,8},{10,9},{11,1... | collective-permute-start | bytes 786440 | tf_op jit(solution)/shard_map/ppermute | solution.py:25
  271.6 26.6 %collective-permute-start.2 = (bf16[32,4096]{1,0:T(8,128)(2,1)}, bf16[32,4096]{1,0:T(8,128)(2,1)S(1)}, u32[]{:S(2)}, u32[]{:S(2)}) collective-permute-start(bf16[32,4096]{1,0:T(8,128)(2,1)} %get-tuple-element.6), channel_id=1, source_target_pairs={{0,1},{1,2},{2,3},{3,4},{4,5},{5,6},{6,7},{7,8},{8,9},{9,10},{10,1... | collective-permute-start | bytes 786440 | tf_op jit(solution)/shard_map/ppermute | solution.py:23
  277.2 22.5 %collective-permute-start.3 = (bf16[32,4096]{1,0:T(8,128)(2,1)}, bf16[32,4096]{1,0:T(8,128)(2,1)S(1)}, u32[]{:S(2)}, u32[]{:S(2)}) collective-permute-start(bf16[32,4096]{1,0:T(8,128)(2,1)} %get-tuple-element.6), channel_id=1, source_target_pairs={{1,0},{2,1},{3,2},{4,3},{5,4},{6,5},{7,6},{8,7},{9,8},{10,9},{11,1... | collective-permute-start | bytes 786440 | tf_op jit(solution)/shard_map/ppermute | solution.py:25
  278.5 25.4 %collective-permute-start.4 = (bf16[32,4096]{1,0:T(8,128)(2,1)}, bf16[32,4096]{1,0:T(8,128)(2,1)S(1)}, u32[]{:S(2)}, u32[]{:S(2)}) collective-permute-start(bf16[32,4096]{1,0:T(8,128)(2,1)} %get-tuple-element.7), channel_id=1, source_target_pairs={{0,1},{1,2},{2,3},{3,4},{4,5},{5,6},{6,7},{7,8},{8,9},{9,10},{10,1... | collective-permute-start | bytes 786440 | tf_op jit(solution)/shard_map/ppermute | solution.py:23
  284.0 20.0 %collective-permute-start.5 = (bf16[32,4096]{1,0:T(8,128)(2,1)}, bf16[32,4096]{1,0:T(8,128)(2,1)S(1)}, u32[]{:S(2)}, u32[]{:S(2)}) collective-permute-start(bf16[32,4096]{1,0:T(8,128)(2,1)} %get-tuple-element.7), channel_id=1, source_target_pairs={{1,0},{2,1},{3,2},{4,3},{5,4},{6,5},{7,6},{8,7},{9,8},{10,9},{11,1... | collective-permute-start | bytes 786440 | tf_op jit(solution)/shard_map/ppermute | solution.py:25
  286.3 28.9 %copy-start = (bf16[32,4096]{1,0:T(8,128)(2,1)S(1)}, bf16[32,4096]{1,0:T(8,128)(2,1)}, u32[]{:S(2)}) copy-start(bf16[32,4096]{1,0:T(8,128)(2,1)} %get-tuple-element.8) | copy-start | bytes 786436
  286.3 28.8 %collective-permute-start.6 = (bf16[32,4096]{1,0:T(8,128)(2,1)}, bf16[32,4096]{1,0:T(8,128)(2,1)S(1)}, u32[]{:S(2)}, u32[]{:S(2)}) collective-permute-start(bf16[32,4096]{1,0:T(8,128)(2,1)} %get-tuple-element.8), channel_id=1, source_target_pairs={{0,1},{1,2},{2,3},{3,4},{4,5},{5,6},{6,7},{7,8},{8,9},{9,10},{10,1... | collective-permute-start | bytes 786440 | tf_op jit(solution)/shard_map/ppermute | solution.py:23
  298.3 16.9 %collective-permute-start.7 = (bf16[32,4096]{1,0:T(8,128)(2,1)}, bf16[32,4096]{1,0:T(8,128)(2,1)S(1)}, u32[]{:S(2)}, u32[]{:S(2)}) collective-permute-start(bf16[32,4096]{1,0:T(8,128)(2,1)} %get-tuple-element.8), channel_id=1, source_target_pairs={{1,0},{2,1},{3,2},{4,3},{5,4},{6,5},{7,6},{8,7},{9,8},{10,9},{11,1... | collective-permute-start | bytes 786440 | tf_op jit(solution)/shard_map/ppermute | solution.py:25
  317.0 14.7 %collective-permute-start.8 = (f32[1,32,4096]{2,1,0:T(8,128)}, f32[1,32,4096]{2,1,0:T(8,128)S(1)}, u32[]{:S(2)}, u32[]{:S(2)}) collective-permute-start(f32[1,32,4096]{2,1,0:T(8,128)} %get-tuple-element.15), channel_id=1, source_target_pairs={{0,32},{32,64},{64,96},{96,128},{128,160},{160,192},{192,224},{224... | collective-permute-start | bytes 1572872 | tf_op jit(solution)/shard_map/ppermute | solution.py:23
  318.9 12.7 %collective-permute-start.9 = (f32[1,32,4096]{2,1,0:T(8,128)}, f32[1,32,4096]{2,1,0:T(8,128)S(1)}, u32[]{:S(2)}, u32[]{:S(2)}) collective-permute-start(f32[1,32,4096]{2,1,0:T(8,128)} %get-tuple-element.16), channel_id=1, source_target_pairs={{32,0},{64,32},{96,64},{128,96},{160,128},{192,160},{224,192},{256... | collective-permute-start | bytes 1572872 | tf_op jit(solution)/shard_map/ppermute | solution.py:25
  331.8 6.7 %collective-permute-start.10 = (f32[6,1,4096]{2,1,0:T(1,128)S(1)}, f32[6,1,4096]{2,1,0:T(1,128)S(1)}, u32[]{:S(2)}, u32[]{:S(2)}) collective-permute-start(f32[6,1,4096]{2,1,0:T(1,128)S(1)} %get-tuple-element.11), channel_id=1, source_target_pairs={{0,1},{1,2},{2,3},{3,4},{4,5},{5,6},{6,7},{7,8},{8,9},{9,10},{10,1... | collective-permute-start | bytes 294920 | tf_op jit(solution)/shard_map/ppermute | solution.py:23
  336.6 7.7 %collective-permute-start.11 = (f32[6,1,4096]{2,1,0:T(1,128)S(1)}, f32[6,1,4096]{2,1,0:T(1,128)S(1)}, u32[]{:S(2)}, u32[]{:S(2)}) collective-permute-start(f32[6,1,4096]{2,1,0:T(1,128)S(1)} %get-tuple-element.12), channel_id=1, source_target_pairs={{1,0},{2,1},{3,2},{4,3},{5,4},{6,5},{7,6},{8,7},{9,8},{10,9},{11,1... | collective-permute-start | bytes 294920 | tf_op jit(solution)/shard_map/ppermute | solution.py:25
  347.9 15.6 %collective-permute-start.12 = (f32[1,32,4096]{2,1,0:T(8,128)S(1)}, f32[1,32,4096]{2,1,0:T(8,128)S(1)}, u32[]{:S(2)}, u32[]{:S(2)}) collective-permute-start(f32[1,32,4096]{2,1,0:T(8,128)S(1)} %get-tuple-element.13), channel_id=1, source_target_pairs={{0,32},{32,64},{64,96},{96,128},{128,160},{160,192},{192,224},{224... | collective-permute-start | bytes 1572872 | tf_op jit(solution)/shard_map/ppermute | solution.py:23
  353.3 10.5 %collective-permute-start.13 = (f32[1,32,4096]{2,1,0:T(8,128)S(1)}, f32[1,32,4096]{2,1,0:T(8,128)S(1)}, u32[]{:S(2)}, u32[]{:S(2)}) collective-permute-start(f32[1,32,4096]{2,1,0:T(8,128)S(1)} %get-tuple-element.14), channel_id=1, source_target_pairs={{32,0},{64,32},{96,64},{128,96},{160,128},{192,160},{224,192},{256... | collective-permute-start | bytes 1572872 | tf_op jit(solution)/shard_map/ppermute | solution.py:25
  364.0 8.9 %collective-permute-start.14 = (f32[6,1,4096]{2,1,0:T(1,128)S(1)}, f32[6,1,4096]{2,1,0:T(1,128)S(1)}, u32[]{:S(2)}, u32[]{:S(2)}) collective-permute-start(f32[6,1,4096]{2,1,0:T(1,128)S(1)} %get-tuple-element.9), channel_id=1, source_target_pairs={{0,1},{1,2},{2,3},{3,4},{4,5},{5,6},{6,7},{7,8},{8,9},{9,10},{10,1... | collective-permute-start | bytes 294920 | tf_op jit(solution)/shard_map/ppermute | solution.py:23
  370.9 6.9 %collective-permute-start.15 = (f32[6,1,4096]{2,1,0:T(1,128)S(1)}, f32[6,1,4096]{2,1,0:T(1,128)S(1)}, u32[]{:S(2)}, u32[]{:S(2)}) collective-permute-start(f32[6,1,4096]{2,1,0:T(1,128)S(1)} %get-tuple-element.10), channel_id=1, source_target_pairs={{1,0},{2,1},{3,2},{4,3},{5,4},{6,5},{7,6},{8,7},{9,8},{10,9},{11,1... | collective-permute-start | bytes 294920 | tf_op jit(solution)/shard_map/ppermute | solution.py:25
Sparse Core Ops, SparseCore 0:
  12.7 252.4 all-reduce.6
where the time goes:
time: 394 us; the launch traced here: 389 us
  waiting for transfers between devices  303 us (77%)
  starting transfers between devices  52.9 us (13%)
  between operations  16.4 us (4%)
  other arithmetic  11.8 us (3%)
    psum x1, waiting for transfers between devices, spread(): return lax.psum(block, axis)  252 us
    ppermute x8, starting transfers between devices, padded_2(): lax.ppermute(tail, axis, [(i, (i + 1) % count) for i in range(ends)])  40.8 us
    ppermute x8, waiting for transfers between devices, padded_2(): lax.ppermute(tail, axis, [(i, (i + 1) % count) for i in range(ends)])  39.7 us
    ppermute x8, starting transfers between devices, padded_2(): lax.ppermute(head, axis, [((i + 1) % count, i) for i in range(ends)])  12.1 us
    ppermute x8, waiting for transfers between devices, padded_2(): lax.ppermute(head, axis, [((i + 1) % count, i) for i in range(ends)])  11.1 us
  transfers between devices with their start and end apart: 17, of which 9 were waited for; matrix products, arithmetic and copies ran while one was open for 1% of the time, Pallas kernels for 0%

commit v1 on v0

v1 whole, which is shorter than its diff:
```python
import functools

import jax
import jax.numpy as jnp
from jax import lax
from jax.experimental import pallas as pl
from jax.experimental.pallas import tpu as pltpu
from jax.sharding import Mesh, PartitionSpec as P

RATE4 = 0.56
F32 = jnp.float32
BF16 = jnp.bfloat16
I32 = jnp.int32

TILE = 32
HERE = 4
VIEWS = 4
BAND = 4
LANES = 128
NC = 4096
SPAN = 3 * VIEWS * TILE
ROWS = 40
DEEP = HERE + 4
WIDE = 512
STEPS = NC // WIDE
DEPTH = ("y", "xl", "core")


def half_conduct(diff):
    return diff / (diff * diff + 4.0)


def interpolation(ids, prm_ref, bands_ref):
    depth, tile, z, xh = ids[0], ids[1], ids[2], ids[3]
    lane = lax.broadcasted_iota(I32, (1, LANES), 1)
    col = lax.broadcasted_iota(I32, (1, SPAN), 1)
    view_of_col = (col >> 5) & 3
    lane_c = lax.broadcasted_iota(I32, (LANES, SPAN), 0)
    view_c = (lax.broadcasted_iota(I32, (LANES, SPAN), 1) >> 5) & 3

    row = lax.broadcasted_iota(I32, (ROWS, 1), 0)
    row = tile * TILE + jnp.where(row < 36, row, row - ROWS)
    last = 32 * TILE - 1
    row = jnp.where(row < 0, -1 - row, jnp.where(row > last, 2 * last + 1 - row, row))
    row_tile = row >> 5
    first_half = xh == 0
    band_a, band_b, band_t = bands_ref[0:1, :], bands_ref[1:2, :], bands_ref[2:3, :]
    before = jnp.where(first_half, band_t, band_a)
    here = jnp.where(first_half, band_a, band_b)
    after = jnp.where(first_half, band_b, band_t)
    picked = jnp.where(row_tile == tile, here, jnp.where(row_tile < tile, before, after))
    picked = jnp.where((lane & 31) == (row & 31), picked, 0.0).astype(BF16)
    same_view = ((lane_c >> 5) == view_c).astype(F32).astype(BF16)
    bands = jnp.dot(picked, same_view, preferred_element_type=F32)

    slot = col >> 7
    third = jnp.where(first_half, 2 * z - 1, 2 * z + 2)
    source = jnp.where(slot == 2, third, 2 * z + slot)
    col_row = jnp.where((source >= 0) & (source < 32), source * TILE + (col & 31), -100000)
    reach = (col_row - row).astype(F32) - bands

    rest = lane - 4 * VIEWS
    lane_slice = jnp.where(rest < 0, lane & 3, (rest >> 2) & 3)
    rest_c = lane_c - 4 * VIEWS
    lane_view = jnp.where(rest_c < 0, lane_c >> 2, rest_c >> 4)
    last_slice = 32 * HERE - 1
    kinds = [rest < 0] + [(rest >= 0) & (rest < 64) & ((rest & 3) == k) for k in range(BAND)]
    held = []
    for i in range(DEEP):
        at = depth * HERE + (i - 2)
        at = jnp.where(at < 0, -1 - at, jnp.where(at > last_slice, 2 * last_slice + 1 - at, at))
        mine = prm_ref[pl.ds(at >> 2, 1), :]
        held.append(jnp.where(lane_slice == (at & 3), mine, 0.0))
    held = jnp.concatenate(held, axis=0)
    stacked = jnp.concatenate([jnp.where(kind, held, 0.0) for kind in kinds], axis=0)
    spread = ((lane_view == view_c) & (rest_c < 64)).astype(F32).astype(BF16)
    table = jnp.dot(stacked.astype(BF16), spread, preferred_element_type=F32)

    parts = []
    for i in range(DEEP):
        gap = reach - table[i : i + 1, :]
        weight = jnp.zeros((ROWS, SPAN), F32)
        for k in range(BAND):
            at = (k + 1) * DEEP + i
            weight = jnp.where(gap == float(k), table[at : at + 1, :], weight)
        parts.append(weight)
    return jnp.concatenate(parts, axis=0).astype(BF16)


def smooth(src, dst_store, first, count, rows, at):
    centre = src[first - 1, :, pl.ds(at, WIDE)]
    ahead = src[first, :, pl.ds(at, WIDE)]
    below = half_conduct(ahead[:rows] - centre[:rows])
    for i in range(count):
        centre = ahead
        ahead = src[first + i + 1, :, pl.ds(at, WIDE)]
        above = half_conduct(ahead[:rows] - centre[:rows])
        total = above - below
        below = above
        step = half_conduct(pltpu.roll(centre, ROWS - 1, 0) - centre)
        total = total + (step - pltpu.roll(step, 1, 0))[:rows]
        wide = src[first + i, :rows, pl.ds(at - LANES, WIDE + 2 * LANES)]
        step = half_conduct(pltpu.roll(wide, WIDE + 2 * LANES - 1, 1) - wide)
        step = step - pltpu.roll(step, 1, 1)
        total = total + step[:, LANES : LANES + WIDE]
        dst_store(i, centre[:rows] + RATE4 * total)


def kernel(ids, prm_ref, bands_ref, own_ref, other_ref, out_ref, weights, v0, v1):
    k = pl.program_id(0)
    core, xl = ids[5], ids[4]

    def block(n):
        return jnp.where(core == 0, n, STEPS - 1 - n)

    @pl.when(k == 0)
    def _():
        weights[...] = interpolation(ids, prm_ref, bands_ref)

    def project(pack, n):
        j = block(n)
        y0 = (j & 3) * 2
        columns = []
        for i in range(2):
            for x in range(2):
                third = pl.ds(4 + (xl ^ x), 1)
                columns.append(
                    jnp.concatenate(
                        [pack[x, y0 + i], pack[2 + x, y0 + i], pack[third, y0 + i][0]], axis=0
                    )
                )
        rows = jnp.concatenate(columns, axis=1)
        found = jnp.dot(weights[...], rows, preferred_element_type=F32)
        at = pl.multiple_of(LANES + j * WIDE, LANES)
        found = found.reshape(DEEP, ROWS, WIDE)
        v0[:, :, pl.ds(at, WIDE)] = found

        @pl.when(j == 0)
        def _():
            v0[:, :, :LANES] = jnp.broadcast_to(found[:, :, :1], (DEEP, ROWS, LANES))

        @pl.when(j == STEPS - 1)
        def _():
            v0[:, :, LANES + NC :] = jnp.broadcast_to(
                found[:, :, WIDE - 1 :], (DEEP, ROWS, LANES)
            )

    @pl.when(k < STEPS // 2)
    def _():
        project(own_ref, k)

    @pl.when((k >= STEPS // 2) & (k < STEPS))
    def _():
        project(other_ref, k)

    @pl.when((k >= 1) & (k <= STEPS))
    def _():
        j = block(k - 1)
        at = pl.multiple_of(LANES + j * WIDE, LANES)

        def store(i, value):
            v1[i, :, pl.ds(at, WIDE)] = value

            @pl.when(j == 0)
            def _():
                v1[i, :, :LANES] = jnp.broadcast_to(value[:, :1], (ROWS, LANES))

            @pl.when(j == STEPS - 1)
            def _():
                v1[i, :, LANES + NC :] = jnp.broadcast_to(value[:, WIDE - 1 :], (ROWS, LANES))

        smooth(v0, store, 1, HERE + 2, ROWS, at)

    @pl.when(k >= 2)
    def _():
        j = block(k - 2)
        at = pl.multiple_of(LANES + j * WIDE, LANES)

        def store(i, value):
            out_ref[i] = value

        smooth(v1, store, 1, HERE, TILE, at)


def finish(ids, prm, bands, own, other):
    def place(k, ids):
        n = jnp.maximum(k - 2, 0)
        return 0, 0, jnp.where(ids[5] == 0, n, STEPS - 1 - n)

    whole = pl.BlockSpec(memory_space=pltpu.VMEM)
    return pl.pallas_call(
        kernel,
        out_shape=jax.ShapeDtypeStruct((HERE, TILE, NC), F32),
        grid_spec=pltpu.PrefetchScalarGridSpec(
            num_scalar_prefetch=1,
            grid=(STEPS + 2,),
            in_specs=[whole] * 4,
            out_specs=pl.BlockSpec((HERE, TILE, WIDE), place),
            scratch_shapes=[
                pltpu.VMEM((DEEP * ROWS, SPAN), BF16),
                pltpu.VMEM((DEEP, ROWS, NC + 2 * LANES), F32),
                pltpu.VMEM((HERE + 2, ROWS, NC + 2 * LANES), F32),
            ],
        ),
        compiler_params=pltpu.CompilerParams(vmem_limit_bytes=32 * 1024 * 1024),
    )(ids, prm, bands, own, other)


def shards(projections, owner, row_offset, band_start, taps):
    stored = projections[0]
    z, xh, xl, core = (lax.axis_index(a) for a in ("z", "xh", "xl", "core"))
    depth, tile = lax.axis_index(DEPTH), lax.axis_index(("z", "xh"))
    ids = jnp.stack([depth, tile, z, xh, xl, core]).astype(I32)

    numbers = jnp.concatenate([row_offset.astype(BF16).reshape(16), taps.reshape(64)])
    numbers = jnp.pad(numbers[None], ((0, 7), (0, LANES - 80)))
    pieces = stored.reshape(TILE, 2, 8, 2, LANES).transpose(2, 3, 1, 0, 4)
    pieces = pieces.reshape(32, TILE, LANES)
    numbers = jnp.broadcast_to(numbers[None], (32, 8, LANES))
    got = lax.all_to_all(jnp.concatenate([pieces, numbers], axis=1), DEPTH, 0, 0, tiled=True)
    prm = got[:, TILE, :].astype(F32)
    views = jnp.concatenate(
        [lax.dynamic_index_in_dim(got, owner[v], keepdims=False)[:TILE] for v in range(VIEWS)]
    )

    band = jnp.pad(band_start.astype(BF16).reshape(1, LANES), ((0, 7), (0, 0)))
    away = [(2 * i + 1, (2 * i + 2) % 32) for i in range(16)]
    away += [(2 * i, (2 * i - 1) % 32) for i in range(16)]
    third = lax.ppermute(jnp.concatenate([views, band]), ("z", "xh"), away)
    both = jnp.concatenate([views, third[: VIEWS * TILE]])

    along = lax.all_to_all(
        jnp.broadcast_to(both[None], (8,) + both.shape), "y", 0, 0, tiled=True
    )
    far = along[:, VIEWS * TILE :]
    swap = [(0, 1), (1, 0)]
    far_pair = lax.ppermute(far, "xl", swap)
    near = jnp.concatenate([along[:, : VIEWS * TILE].reshape(8 * VIEWS * TILE, LANES), band])
    near = lax.all_to_all(
        jnp.broadcast_to(near[None], (4,) + near.shape), ("xh", "xl"), 0, 0, tiled=True
    )
    bands = jnp.stack(
        [near[0, 8 * VIEWS * TILE], near[2, 8 * VIEWS * TILE], third[VIEWS * TILE]]
    ).astype(F32)
    near = near[:, : 8 * VIEWS * TILE].reshape(4, 8, VIEWS * TILE, LANES)
    own = jnp.concatenate([near, far[None], far_pair[None]])
    other = lax.ppermute(own, "core", swap)
    return finish(ids, prm, bands, own, other)


def solution(mesh):
    parted = Mesh(mesh.devices.reshape(8, 2, 2, 16, 2), DEPTH + ("z", "xh"))
    rows = ("z", "xh")
    placed = (
        P(DEPTH, rows, None),
        P(),
        P(None, DEPTH),
        P(None, rows),
        P(None, DEPTH, None),
    )
    return jax.shard_map(
        shards, mesh=parted, in_specs=placed, out_specs=P(DEPTH, rows, None), check_vma=False
    )
```

time: 394 us -> 114 us (0.29); the launches traced: 389 us -> 113 us
  waiting for transfers between devices: 303 us -> 20.6 us
  blocking collectives: 0 us -> 17.9 us
  Pallas kernels: 0 us -> 17.5 us
  starting transfers between devices: 52.9 us -> 42.8 us
  other arithmetic: 11.8 us -> 1.75 us
  between operations: 16.4 us -> 7.61 us
    psum x1 -> x0, waiting for transfers between devices: 252 us -> none  [spread(): return lax.psum(block, axis)]
    ppermute x16 -> x3, waiting for transfers between devices: 50.8 us -> 7.91 us  [the longest x1 4.42 us: shards(): far_pair = lax.ppermute(far, 'xl', swap)]
    ppermute x16 -> x3, starting transfers between devices: 52.9 us -> 21.6 us  [the longest x1 12.1 us: shards(): third = lax.ppermute(jnp.concatenate([views, band]), ('z', 'xh'), away)]
    all_to_all x0 -> x2, starting transfers between devices: none -> 21.2 us  [the longest x1 17.7 us: shards(): lax.all_to_all(jnp.concatenate([pieces, numbers], axis=1), DEPTH, 0, 0, t...]
    all_to_all x0 -> x1, blocking collectives: none -> 17.9 us  [shards(): lax.all_to_all(jnp.broadcast_to(both[None], (8,) + both.shape), 'y', 0, 0...]
    pallas_call x0 -> x1, Pallas kernels: none -> 17.5 us  [finish(): pl.pallas_call(kernel, out_shape=jax.ShapeDtypeStruct((HERE, TILE, NC), F...]
    all_to_all x0 -> x2, waiting for transfers between devices: none -> 12.7 us  [the longest x1 8.14 us: shards(): lax.all_to_all(jnp.broadcast_to(near[None], (4,) + near.shape), ('xh', 'x...]
    add x6 -> x0, other arithmetic: 7.78 us -> none  [the longest x2 7.62 us: sweep(): return center + RATE * total]
  transfers between devices with their start and end apart: 17 -> 5, of which waited for: 9 -> 5; matrix products, arithmetic and copies ran while one was open for 1% -> 1% of each run, Pallas kernels for 0% -> 0%
where the time goes in v1:
time: 114 us; the launch traced here: 113 us
  starting transfers between devices  42.8 us (38%)
  waiting for transfers between devices  20.6 us (18%)
  blocking collectives  17.9 us (16%)
  Pallas kernels  17.5 us (15%)
  between operations  7.61 us (7%)
  local copies, waits for them, and re-layouts  5.09 us (4%)
  other arithmetic  1.75 us (2%)
    all_to_all x1, blocking collectives, shards(): lax.all_to_all(jnp.broadcast_to(both[None], (8,) + both.shape), 'y', 0, 0...  17.9 us
    all_to_all x1, starting transfers between devices, shards(): lax.all_to_all(jnp.concatenate([pieces, numbers], axis=1), DEPTH, 0, 0, t...  17.7 us
    pallas_call x1, Pallas kernels, finish(): pl.pallas_call(kernel, out_shape=jax.ShapeDtypeStruct((HERE, TILE, NC), F...  17.5 us
    ppermute x1, starting transfers between devices, shards(): third = lax.ppermute(jnp.concatenate([views, band]), ('z', 'xh'), away)  12.1 us
    all_to_all x1, waiting for transfers between devices, shards(): lax.all_to_all(jnp.broadcast_to(near[None], (4,) + near.shape), ('xh', 'x...  8.14 us
    ppermute x1, starting transfers between devices, shards(): other = lax.ppermute(own, 'core', swap)  6.2 us
    all_to_all x1, waiting for transfers between devices, shards(): lax.all_to_all(jnp.concatenate([pieces, numbers], axis=1), DEPTH, 0, 0, t...  4.53 us
    ppermute x1, waiting for transfers between devices, shards(): far_pair = lax.ppermute(far, 'xl', swap)  4.42 us
  transfers between devices with their start and end apart: 5, of which 5 were waited for; matrix products, arithmetic and copies ran while one was open for 1% of the time, Pallas kernels for 0%

profile of v1, /device:TPU:1, one launch (start us, length us, event | category | flops | bytes accessed | tf_op | source)
XLA Modules:
  0.0 113.2 jit_solution(5652564381897621790)
XLA Ops:
  0.0 0.0 copy-start.1
  0.0 0.8 reshape.29
  0.8 0.7 convert_element_type.18
  1.5 0.1 reshape.28
  1.6 1.1 reshape_squeeze.3
  2.7 0.1 copy.6
  2.8 0.1 maximum_bitcast_fusion
  2.9 0.8 pad_maximum_fusion.1
  3.7 17.7 %all-to-all-start = ((bf16[32,40,128]{2,1,0:T(8,128)(2,1)}), bf16[32,40,128]{2,1,0:T(8,128)(2,1)S(1)}, u32[]{:S(2)}, u32[]{:S(2)}) async-start(bf16[32,40,128]{2,1,0:T(8,128)(2,1)} %pad_maximum_fusion.1), calls=%async_computation | async-start | bytes 655360 | tf_op jit(solution)/shard_map/all_to_all | solution.py:220
  21.4 0.0 copy-done.1
  21.4 0.7 fusion.1
  27.0 0.0 copy-done.2
  27.0 0.1 reshape.30
  29.6 4.5 %all-to-all-done = bf16[32,40,128]{2,1,0:T(8,128)(2,1)S(1)} async-done(((bf16[32,40,128]{2,1,0:T(8,128)(2,1)}), bf16[32,40,128]{2,1,0:T(8,128)(2,1)S(1)}, u32[]{:S(2)}, u32[]{:S(2)}) %all-to-all-start) | async-done | bytes 327712 | tf_op jit(solution)/shard_map/all_to_all | solution.py:220
  34.2 12.1 %collective-permute-start = (bf16[136,128]{1,0:T(8,128)(2,1)S(1)}, bf16[136,128]{1,0:T(8,128)(2,1)S(1)}, u32[]{:S(2)}, u32[]{:S(2)}) collective-permute-start(bf16[136,128]{1,0:T(8,128)(2,1)S(1)} %get-tuple-element.19), channel_id=1, source_target_pairs={{1,2},{3,4},{5,6},{7,8},{9,10},{11,12},{13,14},{15,16},{17,18},{19... | collective-permute-start | bytes 104456 | tf_op jit(solution)/shard_map/ppermute | solution.py:229
  46.3 1.3 %collective-permute-done = bf16[136,128]{1,0:T(8,128)(2,1)S(1)} collective-permute-done((bf16[136,128]{1,0:T(8,128)(2,1)S(1)}, bf16[136,128]{1,0:T(8,128)(2,1)S(1)}, u32[]{:S(2)}, u32[]{:S(2)}) %collective-permute-start) | collective-permute-done | bytes 34848 | tf_op jit(solution)/shard_map/ppermute | solution.py:229
  47.6 0.1 broadcast_in_dim.14
  47.7 17.9 %all_to_all.15 = bf16[8,256,128]{2,1,0:T(8,128)(2,1)S(1)} all-to-all(bf16[8,256,128]{2,1,0:T(8,128)(2,1)S(1)} %broadcast_in_dim.14), channel_id=1, replica_groups=mesh['y'=8,'xl'=2,'core'=2,'z'=16,'xh'=2] {'y'}, dimensions={0} | all-to-all | bytes 1048576 | tf_op jit(solution)/shard_map/all_to_all | solution.py:232
  65.6 0.1 slice_bitcast_fusion.2
  65.7 1.1 broadcast_in_dim.30
  66.8 3.5 %all-to-all-start.2 = ((bf16[4,1032,128]{2,1,0:T(8,128)(2,1)}), bf16[4,1032,128]{2,1,0:T(8,128)(2,1)S(1)}, u32[]{:S(2)}, u32[]{:S(2)}) async-start(bf16[4,1032,128]{2,1,0:T(8,128)(2,1)} %broadcast_in_dim.30), calls=%async_computation.2 | async-start | bytes 2113536 | tf_op jit(solution)/shard_map/all_to_all | solution.py:239
  70.4 3.3 %collective-permute-start.1 = (bf16[8,128,128]{2,1,0:T(8,128)(2,1)S(1)}, bf16[8,128,128]{2,1,0:T(8,128)(2,1)S(1)}, u32[]{:S(2)}, u32[]{:S(2)}) collective-permute-start(bf16[8,128,128]{2,1,0:T(8,128)(2,1)S(1)} %get-tuple-element.8), channel_id=1, source_target_pairs={{0,64},{64,0},{1,65},{65,1},{2,66},{66,2},{3,67},{67,3},{4,68},{68... | collective-permute-start | bytes 786440 | tf_op jit(solution)/shard_map/ppermute | solution.py:237
  73.7 8.1 %all-to-all-done.2 = bf16[4,1032,128]{2,1,0:T(8,128)(2,1)S(1)} async-done(((bf16[4,1032,128]{2,1,0:T(8,128)(2,1)}), bf16[4,1032,128]{2,1,0:T(8,128)(2,1)S(1)}, u32[]{:S(2)}, u32[]{:S(2)}) %all-to-all-start.2) | async-done | bytes 1056800 | tf_op jit(solution)/shard_map/all_to_all | solution.py:239
  81.8 0.1 slice.86
  81.9 4.4 %collective-permute-done.1 = bf16[8,128,128]{2,1,0:T(8,128)(2,1)S(1)} collective-permute-done((bf16[8,128,128]{2,1,0:T(8,128)(2,1)S(1)}, bf16[8,128,128]{2,1,0:T(8,128)(2,1)S(1)}, u32[]{:S(2)}, u32[]{:S(2)}) %collective-permute-start.1) | collective-permute-done | bytes 262176 | tf_op jit(solution)/shard_map/ppermute | solution.py:237
  86.3 0.0 copy-done
  86.3 0.2 pad_maximum_fusion.own_ref
  86.5 6.2 %collective-permute-start.2 = (bf16[6,8,128,128]{3,2,1,0:T(8,128)(2,1)S(1)}, bf16[6,8,128,128]{3,2,1,0:T(8,128)(2,1)S(1)}, u32[]{:S(2)}, u32[]{:S(2)}) collective-permute-start(bf16[6,8,128,128]{3,2,1,0:T(8,128)(2,1)S(1)} %pad_maximum_fusion.own_ref), channel_id=1, source_target_pairs={{0,32},{32,0},{1,33},{33,1},{2,34},{34,2},{3,35},{35,3},{4,36},{36... | collective-permute-start | bytes 4718600 | tf_op jit(solution)/shard_map/ppermute | solution.py:247
  92.8 0.1 stack.30.ids
  92.9 0.7 slice_bitcast_fusion.1
  93.6 2.2 %collective-permute-done.2.other_ref = bf16[6,8,128,128]{3,2,1,0:T(8,128)(2,1)S(1)} collective-permute-done((bf16[6,8,128,128]{3,2,1,0:T(8,128)(2,1)S(1)}, bf16[6,8,128,128]{3,2,1,0:T(8,128)(2,1)S(1)}, u32[]{:S(2)}, u32[]{:S(2)}) %collective-permute-start.2) | collective-permute-done | bytes 1572896 | tf_op jit(solution)/shard_map/ppermute | solution.py:247
  95.8 17.5 %shard_map.55 = f32[4,32,4096]{2,1,0:T(8,128)} custom-call(s32[6]{0:T(128)S(1)} %stack.30.ids, f32[32,128]{1,0:T(8,128)S(1)} %bitcast.49, f32[3,128]{1,0:T(4,128)S(1)} %maximum_convert_fusion.bands_ref, bf16[6,8,128,128]{3,2,1,0:T(8,128)(2,1)S(1)} %pad_maximum_fusion.own_ref, bf16[6,8,128,128]{3,2,1,0:T(8,128)(2,1)S(1)} %collective-permute-done.2.other_ref), custom_call_target="tpu_custom_call" | custom-call | tf_op jit(solution)/shard_map/pallas_call | solution.py:191
  (15 shorter events, 0.1 us)
Async XLA Ops:
  0.0 21.4 %copy-start.1 = (s32[4]{0:T(128)S(1)}, s32[4]{0:T(128)}, u32[]{:S(2)}) copy-start(s32[4]{0:T(128)} %param.6) | copy-start | bytes 52
  0.0 27.0 %copy-start.2 = (s32[4,32]{1,0:T(4,128)S(1)}, s32[4,32]{1,0:T(4,128)}, u32[]{:S(2)}) copy-start(s32[4,32]{1,0:T(4,128)} %param.8) | copy-start | bytes 1540
  3.7 30.5 %all-to-all-start = ((bf16[32,40,128]{2,1,0:T(8,128)(2,1)}), bf16[32,40,128]{2,1,0:T(8,128)(2,1)S(1)}, u32[]{:S(2)}, u32[]{:S(2)}) async-start(bf16[32,40,128]{2,1,0:T(8,128)(2,1)} %pad_maximum_fusion.1), calls=%async_computation | async-start | bytes 655360 | tf_op jit(solution)/shard_map/all_to_all | solution.py:220
  34.2 13.4 %collective-permute-start = (bf16[136,128]{1,0:T(8,128)(2,1)S(1)}, bf16[136,128]{1,0:T(8,128)(2,1)S(1)}, u32[]{:S(2)}, u32[]{:S(2)}) collective-permute-start(bf16[136,128]{1,0:T(8,128)(2,1)S(1)} %get-tuple-element.19), channel_id=1, source_target_pairs={{1,2},{3,4},{5,6},{7,8},{9,10},{11,12},{13,14},{15,16},{17,18},{19... | collective-permute-start | bytes 104456 | tf_op jit(solution)/shard_map/ppermute | solution.py:229
  66.8 15.0 %all-to-all-start.2 = ((bf16[4,1032,128]{2,1,0:T(8,128)(2,1)}), bf16[4,1032,128]{2,1,0:T(8,128)(2,1)S(1)}, u32[]{:S(2)}, u32[]{:S(2)}) async-start(bf16[4,1032,128]{2,1,0:T(8,128)(2,1)} %broadcast_in_dim.30), calls=%async_computation.2 | async-start | bytes 2113536 | tf_op jit(solution)/shard_map/all_to_all | solution.py:239
  70.4 16.0 %collective-permute-start.1 = (bf16[8,128,128]{2,1,0:T(8,128)(2,1)S(1)}, bf16[8,128,128]{2,1,0:T(8,128)(2,1)S(1)}, u32[]{:S(2)}, u32[]{:S(2)}) collective-permute-start(bf16[8,128,128]{2,1,0:T(8,128)(2,1)S(1)} %get-tuple-element.8), channel_id=1, source_target_pairs={{0,64},{64,0},{1,65},{65,1},{2,66},{66,2},{3,67},{67,3},{4,68},{68... | collective-permute-start | bytes 786440 | tf_op jit(solution)/shard_map/ppermute | solution.py:237
  81.8 4.5 %copy-start = (bf16[4,1032,128]{2,1,0:T(8,128)(2,1)}, bf16[4,1032,128]{2,1,0:T(8,128)(2,1)S(1)}, u32[]{:S(2)}) copy-start(bf16[4,1032,128]{2,1,0:T(8,128)(2,1)S(1)} %all-to-all-done.2) | copy-start | bytes 3170308
  86.5 9.2 %collective-permute-start.2 = (bf16[6,8,128,128]{3,2,1,0:T(8,128)(2,1)S(1)}, bf16[6,8,128,128]{3,2,1,0:T(8,128)(2,1)S(1)}, u32[]{:S(2)}, u32[]{:S(2)}) collective-permute-start(bf16[6,8,128,128]{3,2,1,0:T(8,128)(2,1)S(1)} %pad_maximum_fusion.own_ref), channel_id=1, source_target_pairs={{0,32},{32,0},{1,33},{33,1},{2,34},{34,2},{3,35},{35,3},{4,36},{36... | collective-permute-start | bytes 4718600 | tf_op jit(solution)/shard_map/ppermute | solution.py:247

commit v2 on v1

v2 whole, which is shorter than its diff:
```python
import functools

import jax
import jax.numpy as jnp
from jax import lax
from jax.experimental import pallas as pl
from jax.experimental.pallas import tpu as pltpu
from jax.sharding import Mesh, PartitionSpec as P

RATE4 = 0.56
F32 = jnp.float32
BF16 = jnp.bfloat16
I32 = jnp.int32

TILE = 32
HERE = 4
VIEWS = 4
BAND = 4
LANES = 128
NC = 4096
SPAN = 3 * VIEWS * TILE
ROWS = 40
DEEP = HERE + 4
WIDE = 1024
BATCH = 16
DEPTH = ("y", "xl", "core")


def half_conduct(diff):
    return diff / (diff * diff + 4.0)


def interpolation(ids, prm_ref, bands_ref):
    depth, tile, xh = ids[0], ids[1], ids[2]
    lane = lax.broadcasted_iota(I32, (1, LANES), 1)
    col = lax.broadcasted_iota(I32, (1, SPAN), 1)
    view_of_col = (col >> 5) & 3
    lane_c = lax.broadcasted_iota(I32, (LANES, SPAN), 0)
    view_c = (lax.broadcasted_iota(I32, (LANES, SPAN), 1) >> 5) & 3

    row = lax.broadcasted_iota(I32, (ROWS, 1), 0)
    row = tile * TILE + jnp.where(row < 36, row, row - ROWS)
    last = 32 * TILE - 1
    row = jnp.where(row < 0, -1 - row, jnp.where(row > last, 2 * last + 1 - row, row))
    row_tile = row >> 5
    first_half = xh == 0
    here, pair, away = bands_ref[0:1, :], bands_ref[1:2, :], bands_ref[2:3, :]
    before = jnp.where(first_half, away, pair)
    after = jnp.where(first_half, pair, away)
    picked = jnp.where(row_tile == tile, here, jnp.where(row_tile < tile, before, after))
    picked = jnp.where((lane & 31) == (row & 31), picked, 0.0).astype(BF16)
    same_view = ((lane_c >> 5) == view_c).astype(F32).astype(BF16)
    bands = jnp.dot(picked, same_view, preferred_element_type=F32)

    slot = col >> 7
    third = jnp.where(first_half, tile - 1, tile + 1)
    pair = jnp.where(first_half, tile + 1, tile - 1)
    source = jnp.where(slot == 0, tile, jnp.where(slot == 1, pair, third))
    col_row = jnp.where((source >= 0) & (source < 32), source * TILE + (col & 31), -100000)
    reach = (col_row - row).astype(F32) - bands

    rest = lane - 4 * VIEWS
    lane_slice = jnp.where(rest < 0, lane & 3, (rest >> 2) & 3)
    rest_c = lane_c - 4 * VIEWS
    lane_view = jnp.where(rest_c < 0, lane_c >> 2, rest_c >> 4)
    last_slice = 32 * HERE - 1
    kinds = [rest < 0] + [(rest >= 0) & (rest < 64) & ((rest & 3) == k) for k in range(BAND)]
    held = []
    for i in range(DEEP):
        at = depth * HERE + (i - 2)
        at = jnp.where(at < 0, -1 - at, jnp.where(at > last_slice, 2 * last_slice + 1 - at, at))
        mine = prm_ref[pl.ds(at >> 2, 1), :]
        held.append(jnp.where(lane_slice == (at & 3), mine, 0.0))
    held = jnp.concatenate(held, axis=0)
    stacked = jnp.concatenate([jnp.where(kind, held, 0.0) for kind in kinds], axis=0)
    spread = ((lane_view == view_c) & (rest_c < 64)).astype(F32).astype(BF16)
    table = jnp.dot(stacked.astype(BF16), spread, preferred_element_type=F32)

    parts = []
    for i in range(DEEP):
        gap = reach - table[i : i + 1, :]
        weight = jnp.zeros((ROWS, SPAN), F32)
        for k in range(BAND):
            at = (k + 1) * DEEP + i
            weight = jnp.where(gap == float(k), table[at : at + 1, :], weight)
        parts.append(weight)
    return jnp.concatenate(parts, axis=0).astype(BF16)


def sweep(src, flow, count, rows, store):
    lane = lax.broadcasted_iota(I32, (rows, LANES), 1)
    first, last = lane == 0, lane == LANES - 1
    tiles = NC // LANES

    def at(t):
        return slice(t * LANES, (t + 1) * LANES)

    for t in range(tiles):
        flow[:rows, at(t)] = half_conduct(src[1, :rows, at(t)] - src[0, :rows, at(t)])

    def one(i, carry):
        came = 0.0
        for t0 in range(0, tiles, BATCH):
            batch = range(t0, t0 + BATCH)
            tall = [src[i + 1, :, at(t)] for t in batch]
            ahead = [src[i + 2, :rows, at(t)] for t in batch]
            behind = [flow[:rows, at(t)] for t in batch]
            centre = [x[:rows] for x in tall]
            turned = [pltpu.roll(x, LANES - 1, 1) for x in centre]
            if t0 + BATCH < tiles:
                turned.append(pltpu.roll(src[i + 1, :rows, at(t0 + BATCH)], LANES - 1, 1))
            ahead = [half_conduct(x - c) for x, c in zip(ahead, centre)]
            total = [x - y for x, y in zip(ahead, behind)]
            step = [half_conduct(pltpu.roll(x, ROWS - 1, 0) - x) for x in tall]
            step = [(x - pltpu.roll(x, 1, 0))[:rows] for x in step]
            total = [x + y for x, y in zip(total, step)]
            step = []
            for n in range(BATCH):
                if n + 1 < len(turned):
                    right = jnp.where(last, turned[n + 1], turned[n])
                    step.append(half_conduct(right - centre[n]))
                else:
                    step.append(jnp.where(last, 0.0, half_conduct(turned[n] - centre[n])))
            goes = [pltpu.roll(x, 1, 1) for x in step]
            total = [x + y for x, y in zip(total, step)]
            left = [jnp.where(first, x, y) for x, y in zip([came] + goes, goes)]
            came = goes[-1]
            total = [c + RATE4 * (x - y) for c, x, y in zip(centre, total, left)]
            for n, t in enumerate(batch):
                flow[:rows, at(t)] = ahead[n]
            for n, t in enumerate(batch):
                store(i, at(t), total[n])
        return carry

    lax.fori_loop(0, count, one, 0)


def kernel(
    ids, prm_ref, bands_ref, own_ref, own_third_ref, other_ref, other_third_ref, out_ref,
    weights, v0, v1, flow, done, sems,
):
    xl, core = ids[3], ids[4]
    weights[...] = interpolation(ids, prm_ref, bands_ref)

    def project(pieces, thirds, first):
        def part(j, carry):
            columns = []
            for i in range(4):
                for x in range(2):
                    at = pl.multiple_of(((x ^ xl) * 8 + 4 * j + i) * LANES, LANES)
                    columns.append(
                        jnp.concatenate(
                            [
                                pieces[pl.ds(at, LANES)],
                                pieces[pl.ds(16 * LANES + at, LANES)],
                                thirds[pl.ds(at, LANES)],
                            ],
                            axis=0,
                        )
                    )
            rows = jnp.concatenate(columns, axis=1)
            found = jnp.dot(weights[...], rows, preferred_element_type=F32)
            at = pl.multiple_of(first + j * WIDE, LANES)
            v0[:, :, pl.ds(at, WIDE)] = found.reshape(DEEP, ROWS, WIDE)
            return carry

        lax.fori_loop(0, NC // 2 // WIDE, part, 0)

    project(own_ref, own_third_ref, core * (NC // 2))
    project(other_ref, other_third_ref, (1 - core) * (NC // 2))

    def keep(i, at, value):
        v1[i, :, at] = value

    sweep(v0, flow, HERE + 2, ROWS, keep)

    def put(i, at, value):
        done[i, :, at] = value

        if at.stop == NC:
            pltpu.make_async_copy(done.at[i], out_ref.at[i], sems.at[i]).start()

    sweep(v1, flow, HERE, TILE, put)
    for i in range(HERE):
        pltpu.make_async_copy(done.at[i], out_ref.at[i], sems.at[i]).wait()


def finish(ids, prm, bands, *pieces):
    whole = pl.BlockSpec(memory_space=pltpu.VMEM)
    return pl.pallas_call(
        kernel,
        out_shape=jax.ShapeDtypeStruct((HERE, TILE, NC), F32),
        in_specs=[pl.BlockSpec(memory_space=pltpu.SMEM)] + [whole] * 6,
        out_specs=pl.BlockSpec(memory_space=pl.ANY),
        scratch_shapes=[
            pltpu.VMEM((DEEP * ROWS, SPAN), BF16),
            pltpu.VMEM((DEEP, ROWS, NC), F32),
            pltpu.VMEM((HERE + 2, ROWS, NC), F32),
            pltpu.VMEM((ROWS, NC), F32),
            pltpu.VMEM((HERE, TILE, NC), F32),
            pltpu.SemaphoreType.DMA((HERE,)),
        ],
        compiler_params=pltpu.CompilerParams(vmem_limit_bytes=32 * 1024 * 1024),
    )(ids, prm, bands, *pieces)


def pack(stored_ref, offset_ref, taps_ref, out_ref):
    lane = lax.broadcasted_iota(I32, (1, LANES), 1)
    rest = lane - 4 * VIEWS
    line = lax.broadcasted_iota(I32, (HERE, LANES), 0)
    pick = (line == (lane & 3)).astype(F32)
    spread = jnp.dot(offset_ref[...].astype(F32), pick, preferred_element_type=F32)
    mine = (line == (lane >> 2)) & (lane < 4 * VIEWS)
    numbers = jnp.sum(jnp.where(mine, spread, 0.0), axis=0, keepdims=True)
    for v in range(VIEWS):
        spread = jnp.dot(taps_ref[v].astype(F32), pick, preferred_element_type=F32)
        mine = (line == ((rest >> 2) & 3)) & (rest >= 0) & ((rest >> 4) == v)
        numbers += jnp.sum(jnp.where(mine, spread, 0.0), axis=0, keepdims=True)
    numbers = jnp.broadcast_to(numbers, (8, LANES)).astype(BF16)
    for y in range(8):
        for xl in range(2):
            for core in range(2):
                at = ((core * 8 + y) * 2 + xl) * LANES
                piece = stored_ref[:, at : at + LANES]
                out_ref[(y * 2 + xl) * 2 + core] = jnp.concatenate([piece, numbers], axis=0)


def shards(projections, owner, row_offset, band_start, taps):
    xh, xl, core = (lax.axis_index(a) for a in ("xh", "xl", "core"))
    depth, tile = lax.axis_index(DEPTH), lax.axis_index(("z", "xh"))
    ids = jnp.stack([depth, tile, xh, xl, core]).astype(I32)

    whole = pl.BlockSpec(memory_space=pltpu.VMEM)
    pieces = pl.pallas_call(
        pack,
        out_shape=jax.ShapeDtypeStruct((32, TILE + 8, LANES), BF16),
        in_specs=[whole] * 3,
        out_specs=whole,
    )(projections[0], row_offset, taps)
    got = lax.all_to_all(pieces, DEPTH, 0, 0, tiled=True)
    prm = got[:, TILE, :].astype(F32)
    views = jnp.concatenate(
        [lax.dynamic_index_in_dim(got, owner[v], keepdims=False)[:TILE] for v in range(VIEWS)]
    )

    size = VIEWS * TILE
    near = lax.all_to_all(jnp.broadcast_to(views[None], (8, size, LANES)), "y", 0, 0, tiled=True)
    near = near.reshape(8 * size, LANES)

    band = jnp.pad(band_start.astype(BF16).reshape(1, LANES), ((0, 7), (0, 0)))
    swap = [(0, 1), (1, 0)]
    cross = [(0, 3), (1, 2), (2, 1), (3, 0)]
    pair = lax.ppermute(jnp.concatenate([near, band]), "xh", swap)
    pair_far = lax.ppermute(near, ("xl", "xh"), cross)
    near_late, pair_far = lax.optimization_barrier((near, pair_far))
    near_far = lax.ppermute(near_late, "xl", swap)

    along = [(2 * i, (2 * i + 2) % 32) for i in range(16)]
    along += [(2 * i + 1, (2 * i - 1) % 32) for i in range(16)]
    pairs = jnp.concatenate([pair[: 8 * size], pair_far, pair[8 * size :]])
    own_third = lax.ppermute(pairs, ("z", "xh"), along)

    own = jnp.concatenate([near, near_far, pair[: 8 * size], pair_far])
    other = lax.ppermute(own, "core", swap)
    other_third = lax.ppermute(own_third, "core", swap)
    bands = jnp.stack([band[0], pairs[16 * size], own_third[16 * size]]).astype(F32)
    return finish(ids, prm, bands, own, own_third, other, other_third)


def solution(mesh):
    parted = Mesh(mesh.devices.reshape(8, 2, 2, 16, 2), DEPTH + ("z", "xh"))
    rows = ("z", "xh")
    placed = (
        P(DEPTH, rows, None),
        P(),
        P(None, DEPTH),
        P(None, rows),
        P(None, DEPTH, None),
    )
    return jax.shard_map(
        shards, mesh=parted, in_specs=placed, out_specs=P(DEPTH, rows, None), check_vma=False
    )
```

time: 114 us -> 104 us (0.912)
  waiting for transfers between devices: 20.6 us -> 39.3 us
  blocking collectives: 17.9 us -> 0 us
  Pallas kernels: 17.5 us -> 11.7 us
  starting transfers between devices: 42.8 us -> 41.1 us
  other arithmetic: 1.75 us -> 0.15 us
  local copies, waits for them, and re-layouts: 5.09 us -> 3.78 us
    ppermute x2 -> x5, waiting for transfers between devices: 5.74 us -> 25.4 us  [the longest x1 12.5 us: shards(): own_third = lax.ppermute(pairs, ('z', 'xh'), along)]
    all_to_all x1 -> x0, blocking collectives: 17.9 us -> none  [shards(): lax.all_to_all(jnp.broadcast_to(both[None], (8,) + both.shape), 'y', 0, 0...]
    pallas_call x1, Pallas kernels: 17.5 us -> 9.82 us  [finish(): pl.pallas_call(kernel, out_shape=jax.ShapeDtypeStruct((HERE, TILE, NC), F...]
    ppermute x1, starting transfers between devices: 6.2 us -> 3.69 us  [shards(): other = lax.ppermute(own, 'core', swap)]
    ppermute x1, waiting for transfers between devices: 2.17 us -> 0.01 us  [shards(): other = lax.ppermute(own, 'core', swap)]
    another operation x4 -> x1, local copies, waits for them, and re-layouts: 2.01 us -> 0.09 us  [shards(): ids = jnp.stack([depth, tile, xh, xl, core]).astype(I32)]
    pallas_call x0 -> x1, Pallas kernels: none -> 1.85 us  [shards(): pl.pallas_call(pack, out_shape=jax.ShapeDtypeStruct((32, TILE + 8, LANES)...]
    all_to_all x2, waiting for transfers between devices: 12.7 us -> 13.9 us  [the longest x1 9.9 us: shards(): lax.all_to_all(jnp.broadcast_to(views[None], (8, size, LANES)), 'y', 0, 0...]
  transfers between devices with their start and end apart: 5 -> 8, of which waited for: 5 -> 6; matrix products, arithmetic and copies ran while one was open for 1% -> 2% of each run, Pallas kernels for 0% -> 0%
where the time goes in v2:
time: 104 us; the launch traced here: 103 us
  starting transfers between devices  41.1 us (40%)
  waiting for transfers between devices  39.3 us (38%)
  Pallas kernels  11.7 us (11%)
  between operations  7.5 us (7%)
  local copies, waits for them, and re-layouts  3.78 us (4%)
    all_to_all x1, starting transfers between devices, shards(): got = lax.all_to_all(pieces, DEPTH, 0, 0, tiled=True)  17.7 us
    ppermute x1, waiting for transfers between devices, shards(): own_third = lax.ppermute(pairs, ('z', 'xh'), along)  12.5 us
    all_to_all x1, waiting for transfers between devices, shards(): lax.all_to_all(jnp.broadcast_to(views[None], (8, size, LANES)), 'y', 0, 0...  9.9 us
    pallas_call x1, Pallas kernels, finish(): pl.pallas_call(kernel, out_shape=jax.ShapeDtypeStruct((HERE, TILE, NC), F...  9.82 us
    ppermute x1, waiting for transfers between devices, shards(): pair_far = lax.ppermute(near, ('xl', 'xh'), cross)  9.37 us
    ppermute x1, starting transfers between devices, shards(): pair_far = lax.ppermute(near, ('xl', 'xh'), cross)  5.59 us
    all_to_all x1, waiting for transfers between devices, shards(): got = lax.all_to_all(pieces, DEPTH, 0, 0, tiled=True)  3.98 us
    ppermute x1, starting transfers between devices, shards(): other = lax.ppermute(own, 'core', swap)  3.69 us
  transfers between devices with their start and end apart: 8, of which 6 were waited for; matrix products, arithmetic and copies ran while one was open for 2% of the time, Pallas kernels for 0%

profile of v2, /device:TPU:1, one launch (start us, length us, event | category | flops | bytes accessed | tf_op | source)
XLA Modules:
  0.0 103.5 jit_solution(18299783623550563354)
XLA Ops:
  0.0 0.0 copy-start.1
  0.0 1.8 %shard_map.55 = bf16[32,40,128]{2,1,0:T(8,128)(2,1)} custom-call(bf16[32,4096]{1,0:T(8,128)(2,1)} %bitcast.28, s32[4,4]{1,0:T(4,128)} %offset_ref.1, bf16[4,4,4]{2,1,0:T(4,128)(2,1)} %taps_ref.1), custom_call_target="tpu_custom_call" | custom-call | tf_op jit(solution)/shard_map/pallas_call | solution.py:234
  1.8 17.7 %all-to-all-start = ((bf16[32,40,128]{2,1,0:T(8,128)(2,1)}), bf16[32,40,128]{2,1,0:T(8,128)(2,1)S(1)}, u32[]{:S(2)}, u32[]{:S(2)}) async-start(bf16[32,40,128]{2,1,0:T(8,128)(2,1)} %shard_map.55), calls=%async_computation | async-start | bytes 655360 | tf_op jit(solution)/shard_map/all_to_all | solution.py:240
  19.5 1.5 %fusion.3 = (s32[1]{0:T(128)}, s32[1]{0:T(128)}, s32[1]{0:T(128)}, s32[1]{0:T(128)}) fusion(s32[4]{0:T(128)} %param.6), kind=kLoop, calls=%fused_computation.13 | loop fusion | bytes 32 | tf_op jit(solution)/shard_map/slice | solution.py:243
  28.3 4.0 %all-to-all-done = bf16[32,40,128]{2,1,0:T(8,128)(2,1)S(1)} async-done(((bf16[32,40,128]{2,1,0:T(8,128)(2,1)}), bf16[32,40,128]{2,1,0:T(8,128)(2,1)S(1)}, u32[]{:S(2)}, u32[]{:S(2)}) %all-to-all-start) | async-done | bytes 327712 | tf_op jit(solution)/shard_map/all_to_all | solution.py:240
  32.3 0.7 broadcast_in_dim.2
  33.1 3.4 %all-to-all-start.1 = ((bf16[8,128,128]{2,1,0:T(8,128)(2,1)}), bf16[8,128,128]{2,1,0:T(8,128)(2,1)S(1)}, u32[]{:S(2)}, u32[]{:S(2)}) async-start(bf16[8,128,128]{2,1,0:T(8,128)(2,1)} %broadcast_in_dim.2), calls=%async_computation.1 | async-start | bytes 524288 | tf_op jit(solution)/shard_map/all_to_all | solution.py:247
  36.5 0.0 copy-done.1
  36.5 0.1 reshape.13
  36.6 9.9 %all-to-all-done.1 = bf16[8,128,128]{2,1,0:T(8,128)(2,1)S(1)} async-done(((bf16[8,128,128]{2,1,0:T(8,128)(2,1)}), bf16[8,128,128]{2,1,0:T(8,128)(2,1)S(1)}, u32[]{:S(2)}, u32[]{:S(2)}) %all-to-all-start.1) | async-done | bytes 262176 | tf_op jit(solution)/shard_map/all_to_all | solution.py:247
  46.5 1.9 %collective-permute-start = (bf16[1032,128]{1,0:T(8,128)(2,1)S(1)}, bf16[1032,128]{1,0:T(8,128)(2,1)S(1)}, u32[]{:S(2)}, u32[]{:S(2)}) collective-permute-start(bf16[1032,128]{1,0:T(8,128)(2,1)S(1)} %fusion.1), channel_id=1, source_target_pairs={{0,1},{1,0},{2,3},{3,2},{4,5},{5,4},{6,7},{7,6},{8,9},{9,8},{10,11... | collective-permute-start | bytes 792584 | tf_op jit(solution)/shard_map/ppermute | solution.py:253
  48.4 5.6 %collective-permute-start.1 = (bf16[1024,128]{1,0:T(8,128)(2,1)S(1)}, bf16[1024,128]{1,0:T(8,128)(2,1)S(1)}, u32[]{:S(2)}, u32[]{:S(2)}) collective-permute-start(bf16[1024,128]{1,0:T(8,128)(2,1)S(1)} %bitcast.25), channel_id=1, source_target_pairs={{0,65},{1,64},{64,1},{65,0},{2,67},{3,66},{66,3},{67,2},{4,69},{5,... | collective-permute-start | bytes 786440 | tf_op jit(solution)/shard_map/ppermute | solution.py:254
  54.0 9.4 %collective-permute-done.1 = bf16[1024,128]{1,0:T(8,128)(2,1)S(1)} collective-permute-done((bf16[1024,128]{1,0:T(8,128)(2,1)S(1)}, bf16[1024,128]{1,0:T(8,128)(2,1)S(1)}, u32[]{:S(2)}, u32[]{:S(2)}) %collective-permute-start.1) | collective-permute-done | bytes 262176 | tf_op jit(solution)/shard_map/ppermute | solution.py:254
  63.4 3.2 %collective-permute-start.3 = (bf16[1024,128]{1,0:T(8,128)(2,1)S(1)}, bf16[1024,128]{1,0:T(8,128)(2,1)S(1)}, u32[]{:S(2)}, u32[]{:S(2)}) collective-permute-start(bf16[1024,128]{1,0:T(8,128)(2,1)S(1)} %bitcast.26), channel_id=1, source_target_pairs={{0,64},{64,0},{1,65},{65,1},{2,66},{66,2},{3,67},{67,3},{4,68},{68... | collective-permute-start | bytes 786440 | tf_op jit(solution)/shard_map/ppermute | solution.py:256
  66.7 0.0 collective-permute-done
  66.7 0.0 copy-start
  66.7 0.7 copy-done
  67.4 1.9 %collective-permute-start.2 = (bf16[2056,128]{1,0:T(8,128)(2,1)S(1)}, bf16[2056,128]{1,0:T(8,128)(2,1)S(1)}, u32[]{:S(2)}, u32[]{:S(2)}) collective-permute-start(bf16[2056,128]{1,0:T(8,128)(2,1)S(1)} %pad_maximum_fusion.1), channel_id=1, source_target_pairs={{0,2},{2,4},{4,6},{6,8},{8,10},{10,12},{12,14},{14,16},{16,18},{18... | collective-permute-start | bytes 1579016 | tf_op jit(solution)/shard_map/ppermute | solution.py:261
  69.4 2.9 %collective-permute-done.3 = bf16[1024,128]{1,0:T(8,128)(2,1)S(1)} collective-permute-done((bf16[1024,128]{1,0:T(8,128)(2,1)S(1)}, bf16[1024,128]{1,0:T(8,128)(2,1)S(1)}, u32[]{:S(2)}, u32[]{:S(2)}) %collective-permute-start.3) | collective-permute-done | bytes 262176 | tf_op jit(solution)/shard_map/ppermute | solution.py:256
  72.2 0.1 pad_maximum_fusion.own_ref
  72.3 3.7 %collective-permute-start.4 = (bf16[4096,128]{1,0:T(8,128)(2,1)S(1)}, bf16[4096,128]{1,0:T(8,128)(2,1)S(1)}, u32[]{:S(2)}, u32[]{:S(2)}) collective-permute-start(bf16[4096,128]{1,0:T(8,128)(2,1)S(1)} %pad_maximum_fusion.own_ref), channel_id=1, source_target_pairs={{0,32},{32,0},{1,33},{33,1},{2,34},{34,2},{3,35},{35,3},{4,36},{36... | collective-permute-start | bytes 3145736 | tf_op jit(solution)/shard_map/ppermute | solution.py:264
  76.0 12.5 %collective-permute-done.2.own_third_ref = bf16[2056,128]{1,0:T(8,128)(2,1)S(1)} collective-permute-done((bf16[2056,128]{1,0:T(8,128)(2,1)S(1)}, bf16[2056,128]{1,0:T(8,128)(2,1)S(1)}, u32[]{:S(2)}, u32[]{:S(2)}) %collective-permute-start.2) | collective-permute-done | bytes 526368 | tf_op jit(solution)/shard_map/ppermute | solution.py:261
  88.5 3.6 %collective-permute-start.5 = (bf16[2056,128]{1,0:T(8,128)(2,1)S(1)}, bf16[2056,128]{1,0:T(8,128)(2,1)S(1)}, u32[]{:S(2)}, u32[]{:S(2)}) collective-permute-start(bf16[2056,128]{1,0:T(8,128)(2,1)S(1)} %collective-permute-done.2.own_third_ref), channel_id=1, source_target_pairs={{0,32},{32,0},{1,33},{33,1},{2,34},{34,2},{3,35},{35,3},{4,36},{36... | collective-permute-start | bytes 1579016 | tf_op jit(solution)/shard_map/ppermute | solution.py:265
  92.2 0.1 stack.26.ids
  92.3 0.7 slice.72
  93.0 0.7 collective-permute-done.5.other_third_ref
  93.7 0.0 collective-permute-done.4.other_ref
  93.7 9.8 %shard_map.56 = f32[4,32,4096]{2,1,0:T(8,128)} custom-call(s32[5]{0:T(128)S(1)} %stack.26.ids, f32[32,128]{1,0:T(8,128)S(1)} %fusion.2.prm_ref, f32[3,128]{1,0:T(4,128)S(1)} %maximum_convert_fusion.bands_ref, bf16[4096,128]{1,0:T(8,128)(2,1)S(1)} %pad_maximum_fusion.own_ref, bf16[2056,128]{1,0:T(8,128)(2,1)S(1)} %collective-permute-done.2.own_third_ref, ...), custom_call_target="tpu_custom_call" | custom-call | tf_op jit(solution)/shard_map/pallas_call | solution.py:190
  (11 shorter events, 0.1 us)
Async XLA Ops:
  0.0 36.5 %copy-start.1 = (s32[4,32]{1,0:T(4,128)S(1)}, s32[4,32]{1,0:T(4,128)}, u32[]{:S(2)}) copy-start(s32[4,32]{1,0:T(4,128)} %param.8) | copy-start | bytes 1540
  1.8 30.5 %all-to-all-start = ((bf16[32,40,128]{2,1,0:T(8,128)(2,1)}), bf16[32,40,128]{2,1,0:T(8,128)(2,1)S(1)}, u32[]{:S(2)}, u32[]{:S(2)}) async-start(bf16[32,40,128]{2,1,0:T(8,128)(2,1)} %shard_map.55), calls=%async_computation | async-start | bytes 655360 | tf_op jit(solution)/shard_map/all_to_all | solution.py:240
  33.1 13.4 %all-to-all-start.1 = ((bf16[8,128,128]{2,1,0:T(8,128)(2,1)}), bf16[8,128,128]{2,1,0:T(8,128)(2,1)S(1)}, u32[]{:S(2)}, u32[]{:S(2)}) async-start(bf16[8,128,128]{2,1,0:T(8,128)(2,1)} %broadcast_in_dim.2), calls=%async_computation.1 | async-start | bytes 524288 | tf_op jit(solution)/shard_map/all_to_all | solution.py:247
  46.5 20.1 %collective-permute-start = (bf16[1032,128]{1,0:T(8,128)(2,1)S(1)}, bf16[1032,128]{1,0:T(8,128)(2,1)S(1)}, u32[]{:S(2)}, u32[]{:S(2)}) collective-permute-start(bf16[1032,128]{1,0:T(8,128)(2,1)S(1)} %fusion.1), channel_id=1, source_target_pairs={{0,1},{1,0},{2,3},{3,2},{4,5},{5,4},{6,7},{7,6},{8,9},{9,8},{10,11... | collective-permute-start | bytes 792584 | tf_op jit(solution)/shard_map/ppermute | solution.py:253
  48.4 15.0 %collective-permute-start.1 = (bf16[1024,128]{1,0:T(8,128)(2,1)S(1)}, bf16[1024,128]{1,0:T(8,128)(2,1)S(1)}, u32[]{:S(2)}, u32[]{:S(2)}) collective-permute-start(bf16[1024,128]{1,0:T(8,128)(2,1)S(1)} %bitcast.25), channel_id=1, source_target_pairs={{0,65},{1,64},{64,1},{65,0},{2,67},{3,66},{66,3},{67,2},{4,69},{5,... | collective-permute-start | bytes 786440 | tf_op jit(solution)/shard_map/ppermute | solution.py:254
  63.4 8.8 %collective-permute-start.3 = (bf16[1024,128]{1,0:T(8,128)(2,1)S(1)}, bf16[1024,128]{1,0:T(8,128)(2,1)S(1)}, u32[]{:S(2)}, u32[]{:S(2)}) collective-permute-start(bf16[1024,128]{1,0:T(8,128)(2,1)S(1)} %bitcast.26), channel_id=1, source_target_pairs={{0,64},{64,0},{1,65},{65,1},{2,66},{66,2},{3,67},{67,3},{4,68},{68... | collective-permute-start | bytes 786440 | tf_op jit(solution)/shard_map/ppermute | solution.py:256
  66.7 0.7 copy-start
  67.4 21.1 %collective-permute-start.2 = (bf16[2056,128]{1,0:T(8,128)(2,1)S(1)}, bf16[2056,128]{1,0:T(8,128)(2,1)S(1)}, u32[]{:S(2)}, u32[]{:S(2)}) collective-permute-start(bf16[2056,128]{1,0:T(8,128)(2,1)S(1)} %pad_maximum_fusion.1), channel_id=1, source_target_pairs={{0,2},{2,4},{4,6},{6,8},{8,10},{10,12},{12,14},{14,16},{16,18},{18... | collective-permute-start | bytes 1579016 | tf_op jit(solution)/shard_map/ppermute | solution.py:261
  72.3 21.4 %collective-permute-start.4 = (bf16[4096,128]{1,0:T(8,128)(2,1)S(1)}, bf16[4096,128]{1,0:T(8,128)(2,1)S(1)}, u32[]{:S(2)}, u32[]{:S(2)}) collective-permute-start(bf16[4096,128]{1,0:T(8,128)(2,1)S(1)} %pad_maximum_fusion.own_ref), channel_id=1, source_target_pairs={{0,32},{32,0},{1,33},{33,1},{2,34},{34,2},{3,35},{35,3},{4,36},{36... | collective-permute-start | bytes 3145736 | tf_op jit(solution)/shard_map/ppermute | solution.py:264
  88.5 5.2 %collective-permute-start.5 = (bf16[2056,128]{1,0:T(8,128)(2,1)S(1)}, bf16[2056,128]{1,0:T(8,128)(2,1)S(1)}, u32[]{:S(2)}, u32[]{:S(2)}) collective-permute-start(bf16[2056,128]{1,0:T(8,128)(2,1)S(1)} %collective-permute-done.2.own_third_ref), channel_id=1, source_target_pairs={{0,32},{32,0},{1,33},{33,1},{2,34},{34,2},{3,35},{35,3},{4,36},{36... | collective-permute-start | bytes 1579016 | tf_op jit(solution)/shard_map/ppermute | solution.py:265

commit v3 on v2

--- a/solution.py
+++ b/solution.py
@@ -18,10 +18,11 @@
 BAND = 4
 LANES = 128
 NC = 4096
+SIZE = VIEWS * TILE
+TILES = NC // LANES // 2
 SPAN = 3 * VIEWS * TILE
 ROWS = 40
 DEEP = HERE + 4
-WIDE = 1024
 BATCH = 16
 DEPTH = ("y", "xl", "core")
 
@@ -30,7 +31,7 @@
     return diff / (diff * diff + 4.0)
 
 
-def interpolation(ids, prm_ref, bands_ref):
+def interpolation(ids, prm_ref, here, pair, away):
     depth, tile, xh = ids[0], ids[1], ids[2]
     lane = lax.broadcasted_iota(I32, (1, LANES), 1)
     col = lax.broadcasted_iota(I32, (1, SPAN), 1)
@@ -44,7 +45,6 @@
     row = jnp.where(row < 0, -1 - row, jnp.where(row > last, 2 * last + 1 - row, row))
     row_tile = row >> 5
     first_half = xh == 0
-    here, pair, away = bands_ref[0:1, :], bands_ref[1:2, :], bands_ref[2:3, :]
     before = jnp.where(first_half, away, pair)
     after = jnp.where(first_half, pair, away)
     picked = jnp.where(row_tile == tile, here, jnp.where(row_tile < tile, before, after))
@@ -87,10 +87,9 @@
     return jnp.concatenate(parts, axis=0).astype(BF16)
 
 
-def sweep(src, flow, count, rows, store):
+def sweep(src, flow, count, rows, tiles, store):
     lane = lax.broadcasted_iota(I32, (rows, LANES), 1)
     first, last = lane == 0, lane == LANES - 1
-    tiles = NC // LANES
 
     def at(t):
         return slice(t * LANES, (t + 1) * LANES)
@@ -101,7 +100,7 @@
     def one(i, carry):
         came = 0.0
         for t0 in range(0, tiles, BATCH):
-            batch = range(t0, t0 + BATCH)
+            batch = range(t0, min(t0 + BATCH, tiles))
             tall = [src[i + 1, :, at(t)] for t in batch]
             ahead = [src[i + 2, :rows, at(t)] for t in batch]
             behind = [flow[:rows, at(t)] for t in batch]
@@ -115,7 +114,7 @@
             step = [(x - pltpu.roll(x, 1, 0))[:rows] for x in step]
             total = [x + y for x, y in zip(total, step)]
             step = []
-            for n in range(BATCH):
+            for n in range(len(batch)):
                 if n + 1 < len(turned):
                     right = jnp.where(last, turned[n + 1], turned[n])
                     step.append(half_conduct(right - centre[n]))
@@ -135,73 +134,106 @@
     lax.fori_loop(0, count, one, 0)
 
 
-def kernel(
-    ids, prm_ref, bands_ref, own_ref, own_third_ref, other_ref, other_third_ref, out_ref,
-    weights, v0, v1, flow, done, sems,
-):
-    xl, core = ids[3], ids[4]
-    weights[...] = interpolation(ids, prm_ref, bands_ref)
-
-    def project(pieces, thirds, first):
-        def part(j, carry):
-            columns = []
-            for i in range(4):
-                for x in range(2):
-                    at = pl.multiple_of(((x ^ xl) * 8 + 4 * j + i) * LANES, LANES)
-                    columns.append(
-                        jnp.concatenate(
-                            [
-                                pieces[pl.ds(at, LANES)],
-                                pieces[pl.ds(16 * LANES + at, LANES)],
-                                thirds[pl.ds(at, LANES)],
-                            ],
-                            axis=0,
-                        )
-                    )
-            rows = jnp.concatenate(columns, axis=1)
-            found = jnp.dot(weights[...], rows, preferred_element_type=F32)
-            at = pl.multiple_of(first + j * WIDE, LANES)
-            v0[:, :, pl.ds(at, WIDE)] = found.reshape(DEEP, ROWS, WIDE)
-            return carry
-
-        lax.fori_loop(0, NC // 2 // WIDE, part, 0)
-
-    project(own_ref, own_third_ref, core * (NC // 2))
-    project(other_ref, other_third_ref, (1 - core) * (NC // 2))
+def half(second, ids, prm_ref, band_ref, own_ref, own_a_ref, own_b_ref, *rest):
+    if second:
+        other_ref, other_a_ref, other_b_ref, _, out_ref, weights, v0, v1, flow, done, sems = rest
+    else:
+        out_ref, weights, v0, v1, flow, done, sems = rest
+    xh, core = ids[2], ids[3]
+    tiles = TILES + 2 if second else TILES
+
+    def band(ref):
+        return ref[8 * SIZE :, :].astype(F32)[:1, :]
+
+    pair_band = band(own_ref.at[2 * (1 - xh)])
+    weights[...] = interpolation(ids, prm_ref, band_ref[...], pair_band, band(own_a_ref))
+
+    def project(pieces, third, x, y, count, first):
+        columns = []
+        for i in range(count):
+            at = pl.ds(pl.multiple_of((y + i) * SIZE, SIZE), SIZE)
+            near = pieces[2 * xh + x, at, :]
+            columns.append(
+                jnp.concatenate([near, pieces[2 * (1 - xh) + x, at, :], third(at)], axis=0)
+            )
+        found = jnp.dot(
+            weights[...], jnp.concatenate(columns, axis=1), preferred_element_type=F32
+        )
+        where = pl.ds(pl.multiple_of(first * LANES, LANES), count * LANES)
+        v0[:, :, where] = found.reshape(DEEP, ROWS, count * LANES)
+
+    if second:
+        before = (1 - core) * 2
+        project(other_ref, lambda at: other_a_ref[at, :], 0, 0, 8, before)
+        project(other_ref, lambda at: other_b_ref[at, :], 1, 0, 8, before + 8)
+        edge = jnp.where(core == 0, 0, TILES)
+        project(
+            own_ref,
+            lambda at: jnp.where(core == 0, own_b_ref[at, :], own_a_ref[at, :]),
+            1 - core,
+            6 * (1 - core),
+            2,
+            edge,
+        )
+    else:
+        project(own_ref, lambda at: own_a_ref[at, :], 0, 0, 8, 0)
+        project(own_ref, lambda at: own_b_ref[at, :], 1, 0, 8, 8)
 
     def keep(i, at, value):
         v1[i, :, at] = value
 
-    sweep(v0, flow, HERE + 2, ROWS, keep)
+    sweep(v0, flow, HERE + 2, ROWS, tiles, keep)
+
+    count = (tiles - 1 if second else tiles) * LANES
+    source, target = 0, pl.multiple_of(core * (NC // 2), LANES)
+    if second:
+        source = pl.multiple_of((1 - core) * LANES, LANES)
+        target = pl.multiple_of((1 - core) * (TILES - 1) * LANES, LANES)
+
+    def copy(i):
+        return pltpu.make_async_copy(
+            done.at[i, :, pl.ds(source, count)],
+            out_ref.at[i, :, pl.ds(target, count)],
+            sems.at[i],
+        )
 
     def put(i, at, value):
         done[i, :, at] = value
-
-        if at.stop == NC:
-            pltpu.make_async_copy(done.at[i], out_ref.at[i], sems.at[i]).start()
-
-    sweep(v1, flow, HERE, TILE, put)
+        if at.stop == tiles * LANES:
+            copy(i).start()
+
+    sweep(v1, flow, HERE, TILE, tiles, put)
     for i in range(HERE):
-        pltpu.make_async_copy(done.at[i], out_ref.at[i], sems.at[i]).wait()
-
-
-def finish(ids, prm, bands, *pieces):
+        copy(i).wait()
+
+
+def smooth(second, *operands):
+    wide = (TILES + 2 if second else TILES) * LANES
     whole = pl.BlockSpec(memory_space=pltpu.VMEM)
+    specs = [pl.BlockSpec(memory_space=pltpu.SMEM)] + [whole] * (8 if second else 5)
+    if second:
+        specs.append(pl.BlockSpec(memory_space=pl.ANY))
     return pl.pallas_call(
-        kernel,
+        functools.partial(half, second),
         out_shape=jax.ShapeDtypeStruct((HERE, TILE, NC), F32),
-        in_specs=[pl.BlockSpec(memory_space=pltpu.SMEM)] + [whole] * 6,
+        in_specs=specs,
         out_specs=pl.BlockSpec(memory_space=pl.ANY),
         scratch_shapes=[
             pltpu.VMEM((DEEP * ROWS, SPAN), BF16),
-            pltpu.VMEM((DEEP, ROWS, NC), F32),
-            pltpu.VMEM((HERE + 2, ROWS, NC), F32),
-            pltpu.VMEM((ROWS, NC), F32),
-            pltpu.VMEM((HERE, TILE, NC), F32),
+            pltpu.VMEM((DEEP, ROWS, wide), F32),
+            pltpu.VMEM((HERE + 2, ROWS, wide), F32),
+            pltpu.VMEM((ROWS, wide), F32),
+            pltpu.VMEM((HERE, TILE, wide), F32),
             pltpu.SemaphoreType.DMA((HERE,)),
         ],
-        compiler_params=pltpu.CompilerParams(vmem_limit_bytes=32 * 1024 * 1024),
-    )(ids, prm, bands, *pieces)
+        input_output_aliases={9: 0} if second else {},
+        cost_estimate=pl.CostEstimate(
+            flops=2 * DEEP * ROWS * SPAN * wide,
+            bytes_accessed=24 * 1024 * 1024,
+            transcendentals=0,
+        ),
+        compiler_params=pltpu.CompilerParams(vmem_limit_bytes=24 * 1024 * 1024),
+    )(*operands)
 
 
 def pack(stored_ref, offset_ref, taps_ref, out_ref):
@@ -220,15 +252,15 @@
     for y in range(8):
         for xl in range(2):
             for core in range(2):
-                at = ((core * 8 + y) * 2 + xl) * LANES
+                at = ((core * 2 + xl) * 8 + y) * LANES
                 piece = stored_ref[:, at : at + LANES]
                 out_ref[(y * 2 + xl) * 2 + core] = jnp.concatenate([piece, numbers], axis=0)
 
 
 def shards(projections, owner, row_offset, band_start, taps):
-    xh, xl, core = (lax.axis_index(a) for a in ("xh", "xl", "core"))
+    xh, core = lax.axis_index("xh"), lax.axis_index("core")
     depth, tile = lax.axis_index(DEPTH), lax.axis_index(("z", "xh"))
-    ids = jnp.stack([depth, tile, xh, xl, core]).astype(I32)
+    ids = jnp.stack([depth, tile, xh, core]).astype(I32)
 
     whole = pl.BlockSpec(memory_space=pltpu.VMEM)
     pieces = pl.pallas_call(
@@ -243,28 +275,25 @@
         [lax.dynamic_index_in_dim(got, owner[v], keepdims=False)[:TILE] for v in range(VIEWS)]
     )
 
-    size = VIEWS * TILE
-    near = lax.all_to_all(jnp.broadcast_to(views[None], (8, size, LANES)), "y", 0, 0, tiled=True)
-    near = near.reshape(8 * size, LANES)
-
-    band = jnp.pad(band_start.astype(BF16).reshape(1, LANES), ((0, 7), (0, 0)))
-    swap = [(0, 1), (1, 0)]
-    cross = [(0, 3), (1, 2), (2, 1), (3, 0)]
-    pair = lax.ppermute(jnp.concatenate([near, band]), "xh", swap)
-    pair_far = lax.ppermute(near, ("xl", "xh"), cross)
-    near_late, pair_far = lax.optimization_barrier((near, pair_far))
-    near_far = lax.ppermute(near_late, "xl", swap)
+    near = lax.all_to_all(jnp.broadcast_to(views[None], (8, SIZE, LANES)), "y", 0, 0, tiled=True)
+
+    band = band_start.astype(BF16).reshape(1, SIZE)
+    near = jnp.concatenate([near.reshape(8 * SIZE, LANES), jnp.pad(band, ((0, 15), (0, 0)))])
+    own = lax.all_to_all(
+        jnp.broadcast_to(near[None], (4,) + near.shape), ("xh", "xl"), 0, 0, tiled=True
+    )
 
     along = [(2 * i, (2 * i + 2) % 32) for i in range(16)]
     along += [(2 * i + 1, (2 * i - 1) % 32) for i in range(16)]
-    pairs = jnp.concatenate([pair[: 8 * size], pair_far, pair[8 * size :]])
-    own_third = lax.ppermute(pairs, ("z", "xh"), along)
-
-    own = jnp.concatenate([near, near_far, pair[: 8 * size], pair_far])
-    other = lax.ppermute(own, "core", swap)
-    other_third = lax.ppermute(own_third, "core", swap)
-    bands = jnp.stack([band[0], pairs[16 * size], own_third[16 * size]]).astype(F32)
-    return finish(ids, prm, bands, own, own_third, other, other_third)
+    pair = [lax.dynamic_index_in_dim(own, 2 * (1 - xh) + x, keepdims=False) for x in range(2)]
+    thirds = [lax.ppermute(p, ("z", "xh"), along) for p in pair]
+
+    swap = [(0, 1), (1, 0)]
+    later, thirds[0] = lax.optimization_barrier((own, thirds[0]))
+    other = lax.ppermute(later, "core", swap)
+    other_thirds = [lax.ppermute(t, "core", swap) for t in thirds]
+    first = smooth(False, ids, prm, band.astype(F32), own, *thirds)
+    return smooth(True, ids, prm, band.astype(F32), own, *thirds, other, *other_thirds, first)
 
 
 def solution(mesh):

time: 104 us -> 110 us (1.058)
  waiting for transfers between devices: 39.3 us -> 45.8 us
  Pallas kernels: 11.7 us -> 13.3 us
  local copies, waits for them, and re-layouts: 3.78 us -> 2.66 us
  starting transfers between devices: 41.1 us -> 40 us
    all_to_all x1 -> x2, waiting for transfers between devices: 9.9 us -> 22.1 us  [the longest x1 12.2 us: shards(): lax.all_to_all(jnp.broadcast_to(near[None], (4,) + near.shape), ('xh', 'x...]
    ppermute x6 -> x5, waiting for transfers between devices: 25.4 us -> 19 us  [the longest x2 19 us: shards(): thirds = [lax.ppermute(p, ('z', 'xh'), along) for p in pair]]
    ppermute x6 -> x5, starting transfers between devices: 20 us -> 15.4 us  [the longest x1 6.97 us: shards(): other = lax.ppermute(later, 'core', swap)]
    all_to_all x1 -> x2, starting transfers between devices: 3.41 us -> 6.93 us  [the longest x1 3.52 us: shards(): lax.all_to_all(jnp.broadcast_to(near[None], (4,) + near.shape), ('xh', 'x...]
    pallas_call x1 -> x2, Pallas kernels: 9.82 us -> 11.4 us  [smooth(): pl.pallas_call(functools.partial(half, second), out_shape=jax.ShapeDtypeS...]
    broadcast_in_dim x1 -> x2, local copies, waits for them, and re-layouts: 0.74 us -> 1.85 us  [the longest x1 1.11 us: shards(): jnp.broadcast_to(near[None], (4,) + near.shape)]
  transfers between devices with their start and end apart: 8 -> 8, of which waited for: 6 -> 5; matrix products, arithmetic and copies ran while one was open for 2% -> 1% of each run, Pallas kernels for 0% -> 5%
where the time goes in v3:
time: 110 us
  waiting for transfers between devices  45.8 us (42%)
  starting transfers between devices  40 us (36%)
  Pallas kernels  13.3 us (12%)
  between operations  7.64 us (7%)
  local copies, waits for them, and re-layouts  2.66 us (2%)
    ppermute x2, waiting for transfers between devices, shards(): thirds = [lax.ppermute(p, ('z', 'xh'), along) for p in pair]  19 us
    all_to_all x1, starting transfers between devices, shards(): got = lax.all_to_all(pieces, DEPTH, 0, 0, tiled=True)  17.7 us
    all_to_all x1, waiting for transfers between devices, shards(): lax.all_to_all(jnp.broadcast_to(near[None], (4,) + near.shape), ('xh', 'x...  12.2 us
    pallas_call x2, Pallas kernels, smooth(): pl.pallas_call(functools.partial(half, second), out_shape=jax.ShapeDtypeS...  11.4 us
    all_to_all x1, waiting for transfers between devices, shards(): lax.all_to_all(jnp.broadcast_to(views[None], (8, SIZE, LANES)), 'y', 0, 0...  9.9 us
    ppermute x1, starting transfers between devices, shards(): other = lax.ppermute(later, 'core', swap)  6.97 us
    all_to_all x1, waiting for transfers between devices, shards(): got = lax.all_to_all(pieces, DEPTH, 0, 0, tiled=True)  4.64 us
    ppermute x2, starting transfers between devices, shards(): other_thirds = [lax.ppermute(t, 'core', swap) for t in thirds]  4.61 us
  transfers between devices with their start and end apart: 8, of which 5 were waited for; matrix products, arithmetic and copies ran while one was open for 1% of the time, Pallas kernels for 5%

profile of v3, /device:TPU:1, one launch (start us, length us, event | category | flops | bytes accessed | tf_op | source)
XLA Modules:
  0.0 109.5 jit_solution(14951874358659645541)
XLA Ops:
  0.0 0.0 copy-start
  0.0 0.0 copy-start.1
  0.0 1.9 %shard_map.55 = bf16[32,40,128]{2,1,0:T(8,128)(2,1)} custom-call(bf16[32,4096]{1,0:T(8,128)(2,1)} %bitcast.28, s32[4,4]{1,0:T(4,128)} %offset_ref.1, bf16[4,4,4]{2,1,0:T(4,128)(2,1)} %taps_ref.1), custom_call_target="tpu_custom_call" | custom-call | tf_op jit(solution)/shard_map/pallas_call | solution.py:266
  1.9 17.7 %all-to-all-start = ((bf16[32,40,128]{2,1,0:T(8,128)(2,1)}), bf16[32,40,128]{2,1,0:T(8,128)(2,1)S(1)}, u32[]{:S(2)}, u32[]{:S(2)}) async-start(bf16[32,40,128]{2,1,0:T(8,128)(2,1)} %shard_map.55), calls=%async_computation | async-start | bytes 655360 | tf_op jit(solution)/shard_map/all_to_all | solution.py:272
  19.6 0.0 copy-done
  19.6 0.7 fusion.3
  27.7 4.6 %all-to-all-done = bf16[32,40,128]{2,1,0:T(8,128)(2,1)S(1)} async-done(((bf16[32,40,128]{2,1,0:T(8,128)(2,1)}), bf16[32,40,128]{2,1,0:T(8,128)(2,1)S(1)}, u32[]{:S(2)}, u32[]{:S(2)}) %all-to-all-start) | async-done | bytes 327712 | tf_op jit(solution)/shard_map/all_to_all | solution.py:272
  32.3 0.7 broadcast_in_dim.4
  33.1 3.4 %all-to-all-start.1 = ((bf16[8,128,128]{2,1,0:T(8,128)(2,1)}), bf16[8,128,128]{2,1,0:T(8,128)(2,1)S(1)}, u32[]{:S(2)}, u32[]{:S(2)}) async-start(bf16[8,128,128]{2,1,0:T(8,128)(2,1)} %broadcast_in_dim.4), calls=%async_computation.1 | async-start | bytes 524288 | tf_op jit(solution)/shard_map/all_to_all | solution.py:278
  36.5 0.0 copy-done.1
  36.5 0.1 reshape.26
  36.6 9.9 %all-to-all-done.1 = bf16[8,128,128]{2,1,0:T(8,128)(2,1)S(1)} async-done(((bf16[8,128,128]{2,1,0:T(8,128)(2,1)}), bf16[8,128,128]{2,1,0:T(8,128)(2,1)S(1)}, u32[]{:S(2)}, u32[]{:S(2)}) %all-to-all-start.1) | async-done | bytes 262176 | tf_op jit(solution)/shard_map/all_to_all | solution.py:278
  46.5 1.1 %broadcast_in_dim.5 = bf16[4,1040,128]{2,1,0:T(8,128)(2,1)} broadcast(bf16[1040,128]{1,0:T(8,128)(2,1)S(1)} %fusion.1), dimensions={1,2} | broadcast | bytes 1331200 | tf_op jit(solution)/shard_map/broadcast_in_dim | solution.py:283
  47.6 3.5 %all-to-all-start.2 = ((bf16[4,1040,128]{2,1,0:T(8,128)(2,1)}), bf16[4,1040,128]{2,1,0:T(8,128)(2,1)S(1)}, u32[]{:S(2)}, u32[]{:S(2)}) async-start(bf16[4,1040,128]{2,1,0:T(8,128)(2,1)} %broadcast_in_dim.5), calls=%async_computation.2 | async-start | bytes 2129920 | tf_op jit(solution)/shard_map/all_to_all | solution.py:282
  51.2 12.2 %all-to-all-done.2.own_ref = bf16[4,1040,128]{2,1,0:T(8,128)(2,1)S(1)} async-done(((bf16[4,1040,128]{2,1,0:T(8,128)(2,1)}), bf16[4,1040,128]{2,1,0:T(8,128)(2,1)S(1)}, u32[]{:S(2)}, u32[]{:S(2)}) %all-to-all-start.2) | async-done | bytes 1064992 | tf_op jit(solution)/shard_map/all_to_all | solution.py:282
  63.4 1.9 %collective-permute-start = (bf16[1040,128]{1,0:T(8,128)(2,1)S(1)}, bf16[1040,128]{1,0:T(8,128)(2,1)S(1)}, u32[]{:S(2)}, u32[]{:S(2)}) collective-permute-start(bf16[1040,128]{1,0:T(8,128)(2,1)S(1)} %get-tuple-element.10), channel_id=1, source_target_pairs={{0,2},{2,4},{4,6},{6,8},{8,10},{10,12},{12,14},{14,16},{16,18},{18... | collective-permute-start | bytes 798728 | tf_op jit(solution)/shard_map/ppermute | solution.py:289
  65.4 11.9 %collective-permute-done.own_a_ref = bf16[1040,128]{1,0:T(8,128)(2,1)S(1)} collective-permute-done((bf16[1040,128]{1,0:T(8,128)(2,1)S(1)}, bf16[1040,128]{1,0:T(8,128)(2,1)S(1)}, u32[]{:S(2)}, u32[]{:S(2)}) %collective-permute-start) | collective-permute-done | bytes 266272 | tf_op jit(solution)/shard_map/ppermute | solution.py:289
  77.2 7.0 %collective-permute-start.2 = (bf16[4,1040,128]{2,1,0:T(8,128)(2,1)S(1)}, bf16[4,1040,128]{2,1,0:T(8,128)(2,1)S(1)}, u32[]{:S(2)}, u32[]{:S(2)}) collective-permute-start(bf16[4,1040,128]{2,1,0:T(8,128)(2,1)S(1)} %all-to-all-done.2.own_ref), channel_id=1, source_target_pairs={{0,32},{32,0},{1,33},{33,1},{2,34},{34,2},{3,35},{35,3},{4,36},{36... | collective-permute-start | bytes 3194888 | tf_op jit(solution)/shard_map/ppermute | solution.py:293
  84.2 1.9 %collective-permute-start.1 = (bf16[1040,128]{1,0:T(8,128)(2,1)S(1)}, bf16[1040,128]{1,0:T(8,128)(2,1)S(1)}, u32[]{:S(2)}, u32[]{:S(2)}) collective-permute-start(bf16[1040,128]{1,0:T(8,128)(2,1)S(1)} %get-tuple-element.9), channel_id=1, source_target_pairs={{0,2},{2,4},{4,6},{6,8},{8,10},{10,12},{12,14},{14,16},{16,18},{18... | collective-permute-start | bytes 798728 | tf_op jit(solution)/shard_map/ppermute | solution.py:289
  86.2 0.1 pad_add_fusion.ids
  86.3 1.9 %collective-permute-start.3 = (bf16[1040,128]{1,0:T(8,128)(2,1)S(1)}, bf16[1040,128]{1,0:T(8,128)(2,1)S(1)}, u32[]{:S(2)}, u32[]{:S(2)}) collective-permute-start(bf16[1040,128]{1,0:T(8,128)(2,1)S(1)} %collective-permute-done.own_a_ref), channel_id=1, source_target_pairs={{0,32},{32,0},{1,33},{33,1},{2,34},{34,2},{3,35},{35,3},{4,36},{36... | collective-permute-start | bytes 798728 | tf_op jit(solution)/shard_map/ppermute | solution.py:294
  88.2 7.1 %collective-permute-done.1.own_b_ref = bf16[1040,128]{1,0:T(8,128)(2,1)S(1)} collective-permute-done((bf16[1040,128]{1,0:T(8,128)(2,1)S(1)}, bf16[1040,128]{1,0:T(8,128)(2,1)S(1)}, u32[]{:S(2)}, u32[]{:S(2)}) %collective-permute-start.1) | collective-permute-done | bytes 266272 | tf_op jit(solution)/shard_map/ppermute | solution.py:289
  95.3 2.7 %collective-permute-start.4 = (bf16[1040,128]{1,0:T(8,128)(2,1)S(1)}, bf16[1040,128]{1,0:T(8,128)(2,1)S(1)}, u32[]{:S(2)}, u32[]{:S(2)}) collective-permute-start(bf16[1040,128]{1,0:T(8,128)(2,1)S(1)} %collective-permute-done.1.own_b_ref), channel_id=1, source_target_pairs={{0,32},{32,0},{1,33},{33,1},{2,34},{34,2},{3,35},{35,3},{4,36},{36... | collective-permute-start | bytes 798728 | tf_op jit(solution)/shard_map/ppermute | solution.py:294
  98.1 5.4 %shard_map.56.rest_3_ = f32[4,32,4096]{2,1,0:T(8,128)} custom-call(s32[4]{0:T(128)S(1)} %pad_add_fusion.ids, f32[32,128]{1,0:T(8,128)S(1)} %fusion.2.prm_ref, f32[1,128]{1,0:T(1,128)S(1)} %convert_element_type.17.band_ref, bf16[4,1040,128]{2,1,0:T(8,128)(2,1)S(1)} %all-to-all-done.2.own_ref, bf16[1040,128]{1,0:T(8,128)(2,1)S(1)} %collective-permute-done.own_a_ref, ...), custom_call_target="tpu_custom_call" | custom-call | flops 503316480 | bytes 25165824 | tf_op jit(solution)/shard_map/pallas_call | solution.py:216
  103.5 0.0 collective-permute-done.4.rest_2_
  103.5 0.0 collective-permute-done.3.rest_1_
  103.5 0.0 collective-permute-done.2.rest_0_
  103.5 6.1 %shard_map.57 = f32[4,32,4096]{2,1,0:T(8,128)} custom-call(s32[4]{0:T(128)S(1)} %pad_add_fusion.ids, f32[32,128]{1,0:T(8,128)S(1)} %fusion.2.prm_ref, f32[1,128]{1,0:T(1,128)S(1)} %convert_element_type.17.band_ref, bf16[4,1040,128]{2,1,0:T(8,128)(2,1)S(1)} %all-to-all-done.2.own_ref, ...), custom_call_target="tpu_custom_call", output_to_operand_aliasing={{}: (9, {})} | custom-call | flops 566231040 | bytes 25165824 | tf_op jit(solution)/shard_map/pallas_call | solution.py:216
  (8 shorter events, 0.1 us)
Async XLA Ops:
  0.0 19.6 %copy-start = (s32[4]{0:T(128)S(1)}, s32[4]{0:T(128)}, u32[]{:S(2)}) copy-start(s32[4]{0:T(128)} %param.6) | copy-start | bytes 52
  0.0 36.5 %copy-start.1 = (s32[4,32]{1,0:T(4,128)S(1)}, s32[4,32]{1,0:T(4,128)}, u32[]{:S(2)}) copy-start(s32[4,32]{1,0:T(4,128)} %param.8) | copy-start | bytes 1540
  1.9 30.5 %all-to-all-start = ((bf16[32,40,128]{2,1,0:T(8,128)(2,1)}), bf16[32,40,128]{2,1,0:T(8,128)(2,1)S(1)}, u32[]{:S(2)}, u32[]{:S(2)}) async-start(bf16[32,40,128]{2,1,0:T(8,128)(2,1)} %shard_map.55), calls=%async_computation | async-start | bytes 655360 | tf_op jit(solution)/shard_map/all_to_all | solution.py:272
  33.1 13.4 %all-to-all-start.1 = ((bf16[8,128,128]{2,1,0:T(8,128)(2,1)}), bf16[8,128,128]{2,1,0:T(8,128)(2,1)S(1)}, u32[]{:S(2)}, u32[]{:S(2)}) async-start(bf16[8,128,128]{2,1,0:T(8,128)(2,1)} %broadcast_in_dim.4), calls=%async_computation.1 | async-start | bytes 524288 | tf_op jit(solution)/shard_map/all_to_all | solution.py:278
  47.6 15.8 %all-to-all-start.2 = ((bf16[4,1040,128]{2,1,0:T(8,128)(2,1)}), bf16[4,1040,128]{2,1,0:T(8,128)(2,1)S(1)}, u32[]{:S(2)}, u32[]{:S(2)}) async-start(bf16[4,1040,128]{2,1,0:T(8,128)(2,1)} %broadcast_in_dim.5), calls=%async_computation.2 | async-start | bytes 2129920 | tf_op jit(solution)/shard_map/all_to_all | solution.py:282
  63.4 13.8 %collective-permute-start = (bf16[1040,128]{1,0:T(8,128)(2,1)S(1)}, bf16[1040,128]{1,0:T(8,128)(2,1)S(1)}, u32[]{:S(2)}, u32[]{:S(2)}) collective-permute-start(bf16[1040,128]{1,0:T(8,128)(2,1)S(1)} %get-tuple-element.10), channel_id=1, source_target_pairs={{0,2},{2,4},{4,6},{6,8},{8,10},{10,12},{12,14},{14,16},{16,18},{18... | collective-permute-start | bytes 798728 | tf_op jit(solution)/shard_map/ppermute | solution.py:289
  77.2 26.2 %collective-permute-start.2 = (bf16[4,1040,128]{2,1,0:T(8,128)(2,1)S(1)}, bf16[4,1040,128]{2,1,0:T(8,128)(2,1)S(1)}, u32[]{:S(2)}, u32[]{:S(2)}) collective-permute-start(bf16[4,1040,128]{2,1,0:T(8,128)(2,1)S(1)} %all-to-all-done.2.own_ref), channel_id=1, source_target_pairs={{0,32},{32,0},{1,33},{33,1},{2,34},{34,2},{3,35},{35,3},{4,36},{36... | collective-permute-start | bytes 3194888 | tf_op jit(solution)/shard_map/ppermute | solution.py:293
  84.2 11.1 %collective-permute-start.1 = (bf16[1040,128]{1,0:T(8,128)(2,1)S(1)}, bf16[1040,128]{1,0:T(8,128)(2,1)S(1)}, u32[]{:S(2)}, u32[]{:S(2)}) collective-permute-start(bf16[1040,128]{1,0:T(8,128)(2,1)S(1)} %get-tuple-element.9), channel_id=1, source_target_pairs={{0,2},{2,4},{4,6},{6,8},{8,10},{10,12},{12,14},{14,16},{16,18},{18... | collective-permute-start | bytes 798728 | tf_op jit(solution)/shard_map/ppermute | solution.py:289
  86.3 17.2 %collective-permute-start.3 = (bf16[1040,128]{1,0:T(8,128)(2,1)S(1)}, bf16[1040,128]{1,0:T(8,128)(2,1)S(1)}, u32[]{:S(2)}, u32[]{:S(2)}) collective-permute-start(bf16[1040,128]{1,0:T(8,128)(2,1)S(1)} %collective-permute-done.own_a_ref), channel_id=1, source_target_pairs={{0,32},{32,0},{1,33},{33,1},{2,34},{34,2},{3,35},{35,3},{4,36},{36... | collective-permute-start | bytes 798728 | tf_op jit(solution)/shard_map/ppermute | solution.py:294
  95.3 8.1 %collective-permute-start.4 = (bf16[1040,128]{1,0:T(8,128)(2,1)S(1)}, bf16[1040,128]{1,0:T(8,128)(2,1)S(1)}, u32[]{:S(2)}, u32[]{:S(2)}) collective-permute-start(bf16[1040,128]{1,0:T(8,128)(2,1)S(1)} %collective-permute-done.1.own_b_ref), channel_id=1, source_target_pairs={{0,32},{32,0},{1,33},{33,1},{2,34},{34,2},{3,35},{35,3},{4,36},{36... | collective-permute-start | bytes 798728 | tf_op jit(solution)/shard_map/ppermute | solution.py:294

commit v4 on v3

--- a/solution.py
+++ b/solution.py
@@ -134,28 +134,28 @@
     lax.fori_loop(0, count, one, 0)
 
 
-def half(second, ids, prm_ref, band_ref, own_ref, own_a_ref, own_b_ref, *rest):
+def half(second, ids, prm_ref, band_ref, own_ref, *rest):
     if second:
-        other_ref, other_a_ref, other_b_ref, _, out_ref, weights, v0, v1, flow, done, sems = rest
+        other_ref, _, out_ref, weights, v0, v1, flow, done, sems = rest
     else:
         out_ref, weights, v0, v1, flow, done, sems = rest
-    xh, core = ids[2], ids[3]
+    xh, core, xl = ids[2], ids[3], ids[4]
     tiles = TILES + 2 if second else TILES
 
     def band(ref):
         return ref[8 * SIZE :, :].astype(F32)[:1, :]
 
     pair_band = band(own_ref.at[2 * (1 - xh)])
-    weights[...] = interpolation(ids, prm_ref, band_ref[...], pair_band, band(own_a_ref))
-
-    def project(pieces, third, x, y, count, first):
+    weights[...] = interpolation(ids, prm_ref, band_ref[...], pair_band, band(own_ref.at[4]))
+
+    def project(pieces, x, y, count, first):
         columns = []
         for i in range(count):
             at = pl.ds(pl.multiple_of((y + i) * SIZE, SIZE), SIZE)
             near = pieces[2 * xh + x, at, :]
-            columns.append(
-                jnp.concatenate([near, pieces[2 * (1 - xh) + x, at, :], third(at)], axis=0)
-            )
+            pair = pieces[2 * (1 - xh) + x, at, :]
+            third = pieces[4 + (x ^ xl), at, :]
+            columns.append(jnp.concatenate([near, pair, third], axis=0))
         found = jnp.dot(
             weights[...], jnp.concatenate(columns, axis=1), preferred_element_type=F32
         )
@@ -164,20 +164,12 @@
 
     if second:
         before = (1 - core) * 2
-        project(other_ref, lambda at: other_a_ref[at, :], 0, 0, 8, before)
-        project(other_ref, lambda at: other_b_ref[at, :], 1, 0, 8, before + 8)
-        edge = jnp.where(core == 0, 0, TILES)
-        project(
-            own_ref,
-            lambda at: jnp.where(core == 0, own_b_ref[at, :], own_a_ref[at, :]),
-            1 - core,
-            6 * (1 - core),
-            2,
-            edge,
-        )
+        project(other_ref, 0, 0, 8, before)
+        project(other_ref, 1, 0, 8, before + 8)
+        project(own_ref, 1 - core, 6 * (1 - core), 2, core * TILES)
     else:
-        project(own_ref, lambda at: own_a_ref[at, :], 0, 0, 8, 0)
-        project(own_ref, lambda at: own_b_ref[at, :], 1, 0, 8, 8)
+        project(own_ref, 0, 0, 8, 0)
+        project(own_ref, 1, 0, 8, 8)
 
     def keep(i, at, value):
         v1[i, :, at] = value
@@ -210,7 +202,7 @@
 def smooth(second, *operands):
     wide = (TILES + 2 if second else TILES) * LANES
     whole = pl.BlockSpec(memory_space=pltpu.VMEM)
-    specs = [pl.BlockSpec(memory_space=pltpu.SMEM)] + [whole] * (8 if second else 5)
+    specs = [pl.BlockSpec(memory_space=pltpu.SMEM)] + [whole] * (4 if second else 3)
     if second:
         specs.append(pl.BlockSpec(memory_space=pl.ANY))
     return pl.pallas_call(
@@ -226,7 +218,7 @@
             pltpu.VMEM((HERE, TILE, wide), F32),
             pltpu.SemaphoreType.DMA((HERE,)),
         ],
-        input_output_aliases={9: 0} if second else {},
+        input_output_aliases={5: 0} if second else {},
         cost_estimate=pl.CostEstimate(
             flops=2 * DEEP * ROWS * SPAN * wide,
             bytes_accessed=24 * 1024 * 1024,
@@ -258,9 +250,9 @@
 
 
 def shards(projections, owner, row_offset, band_start, taps):
-    xh, core = lax.axis_index("xh"), lax.axis_index("core")
+    xh, xl, core = (lax.axis_index(a) for a in ("xh", "xl", "core"))
     depth, tile = lax.axis_index(DEPTH), lax.axis_index(("z", "xh"))
-    ids = jnp.stack([depth, tile, xh, core]).astype(I32)
+    ids = jnp.stack([depth, tile, xh, core, xl]).astype(I32)
 
     whole = pl.BlockSpec(memory_space=pltpu.VMEM)
     pieces = pl.pallas_call(
@@ -275,25 +267,31 @@
         [lax.dynamic_index_in_dim(got, owner[v], keepdims=False)[:TILE] for v in range(VIEWS)]
     )
 
+    band = band_start.astype(BF16).reshape(1, SIZE)
+    rest = (band.astype(F32), jnp.pad(band, ((0, 15), (0, 0))), prm, ids)
+    views, (band, band_rows, prm, ids) = lax.optimization_barrier((views, rest))
     near = lax.all_to_all(jnp.broadcast_to(views[None], (8, SIZE, LANES)), "y", 0, 0, tiled=True)
-
-    band = band_start.astype(BF16).reshape(1, SIZE)
-    near = jnp.concatenate([near.reshape(8 * SIZE, LANES), jnp.pad(band, ((0, 15), (0, 0)))])
+    near = jnp.concatenate([near.reshape(8 * SIZE, LANES), band_rows])
+
+    shift = [(2 * i, (2 * i - 2) % 32) for i in range(16)]
+    shift += [(2 * i + 1, (2 * i + 3) % 32) for i in range(16)]
+    foreign = lax.ppermute(near, ("z", "xh"), shift)
     own = lax.all_to_all(
         jnp.broadcast_to(near[None], (4,) + near.shape), ("xh", "xl"), 0, 0, tiled=True
     )
 
-    along = [(2 * i, (2 * i + 2) % 32) for i in range(16)]
-    along += [(2 * i + 1, (2 * i - 1) % 32) for i in range(16)]
-    pair = [lax.dynamic_index_in_dim(own, 2 * (1 - xh) + x, keepdims=False) for x in range(2)]
-    thirds = [lax.ppermute(p, ("z", "xh"), along) for p in pair]
+    own, foreign = lax.optimization_barrier((own, foreign))
+
+    along = [(a, b) for b, a in shift]
+    third = lax.dynamic_index_in_dim(own, 2 * (1 - xh) + xl, keepdims=False)
+    third = lax.ppermute(third, ("z", "xh"), along)
+    third_far = lax.ppermute(foreign, ("xl", "xh"), [(0, 3), (1, 2), (2, 1), (3, 0)])
 
     swap = [(0, 1), (1, 0)]
-    later, thirds[0] = lax.optimization_barrier((own, thirds[0]))
-    other = lax.ppermute(later, "core", swap)
-    other_thirds = [lax.ppermute(t, "core", swap) for t in thirds]
-    first = smooth(False, ids, prm, band.astype(F32), own, *thirds)
-    return smooth(True, ids, prm, band.astype(F32), own, *thirds, other, *other_thirds, first)
+    own = jnp.concatenate([own, third[None], third_far[None]])
+    other = lax.ppermute(own, "core", swap)
+    first = smooth(False, ids, prm, band, own)
+    return smooth(True, ids, prm, band, own, other, first)
 
 
 def solution(mesh):

time: 110 us -> 99.7 us (0.906)
  waiting for transfers between devices: 45.8 us -> 10.9 us
  blocking collectives: 0 us -> 14.5 us
  starting transfers between devices: 40 us -> 49.3 us
    all_to_all x0 -> x1, blocking collectives: none -> 14.5 us  [shards(): lax.all_to_all(jnp.broadcast_to(views[None], (8, SIZE, LANES)), 'y', 0, 0...]
    ppermute x5 -> x4, starting transfers between devices: 15.4 us -> 28.1 us  [the longest x1 10.5 us: shards(): lax.ppermute(foreign, ('xl', 'xh'), [(0, 3), (1, 2), (2, 1), (3, 0)])]
    all_to_all x1, waiting for transfers between devices: 12.2 us -> 0.01 us  [shards(): lax.all_to_all(jnp.broadcast_to(near[None], (4,) + near.shape), ('xh', 'x...]
    ppermute x5 -> x4, waiting for transfers between devices: 19 us -> 7.77 us  [the longest x1 3.68 us: shards(): foreign = lax.ppermute(near, ('z', 'xh'), shift)]
    all_to_all x1 -> x0, waiting for transfers between devices: 9.9 us -> none  [shards(): lax.all_to_all(jnp.broadcast_to(views[None], (8, SIZE, LANES)), 'y', 0, 0...]
    all_to_all x1 -> x0, starting transfers between devices: 3.41 us -> none  [shards(): lax.all_to_all(jnp.broadcast_to(views[None], (8, SIZE, LANES)), 'y', 0, 0...]
    all_to_all x1, waiting for transfers between devices: 4.64 us -> 3.11 us  [shards(): got = lax.all_to_all(pieces, DEPTH, 0, 0, tiled=True)]
  transfers between devices with their start and end apart: 8 -> 6, of which waited for: 5 -> 4; matrix products, arithmetic and copies ran while one was open for 1% -> 2% of each run, Pallas kernels for 5% -> 5%
where the time goes in v4:
time: 99.7 us; the launch traced here: 99.2 us
  starting transfers between devices  49.3 us (49%)
  blocking collectives  14.5 us (15%)
  Pallas kernels  13.2 us (13%)
  waiting for transfers between devices  10.9 us (11%)
  between operations  7.5 us (8%)
  local copies, waits for them, and re-layouts  2.8 us (3%)
    all_to_all x1, starting transfers between devices, shards(): got = lax.all_to_all(pieces, DEPTH, 0, 0, tiled=True)  17.7 us
    all_to_all x1, blocking collectives, shards(): lax.all_to_all(jnp.broadcast_to(views[None], (8, SIZE, LANES)), 'y', 0, 0...  14.5 us
    pallas_call x2, Pallas kernels, smooth(): pl.pallas_call(functools.partial(half, second), out_shape=jax.ShapeDtypeS...  11.4 us
    ppermute x1, starting transfers between devices, shards(): lax.ppermute(foreign, ('xl', 'xh'), [(0, 3), (1, 2), (2, 1), (3, 0)])  10.5 us
    ppermute x1, starting transfers between devices, shards(): foreign = lax.ppermute(near, ('z', 'xh'), shift)  10 us
    ppermute x1, starting transfers between devices, shards(): other = lax.ppermute(own, 'core', swap)  5.66 us
    ppermute x1, waiting for transfers between devices, shards(): foreign = lax.ppermute(near, ('z', 'xh'), shift)  3.68 us
    all_to_all x1, starting transfers between devices, shards(): lax.all_to_all(jnp.broadcast_to(near[None], (4,) + near.shape), ('xh', 'x...  3.52 us
  transfers between devices with their start and end apart: 6, of which 4 were waited for; matrix products, arithmetic and copies ran while one was open for 2% of the time, Pallas kernels for 5%

profile of v4, /device:TPU:1, one launch (start us, length us, event | category | flops | bytes accessed | tf_op | source)
XLA Modules:
  0.0 99.2 jit_solution(13799057863565010886)
XLA Ops:
  0.0 1.8 %shard_map.55 = bf16[32,40,128]{2,1,0:T(8,128)(2,1)} custom-call(bf16[32,4096]{1,0:T(8,128)(2,1)} %bitcast.31, s32[4,4]{1,0:T(4,128)} %offset_ref.1, bf16[4,4,4]{2,1,0:T(4,128)(2,1)} %taps_ref.1), custom_call_target="tpu_custom_call" | custom-call | tf_op jit(solution)/shard_map/pallas_call | solution.py:258
  1.8 17.7 %all-to-all-start = ((bf16[32,40,128]{2,1,0:T(8,128)(2,1)}), bf16[32,40,128]{2,1,0:T(8,128)(2,1)S(1)}, u32[]{:S(2)}, u32[]{:S(2)}) async-start(bf16[32,40,128]{2,1,0:T(8,128)(2,1)} %shard_map.55), calls=%async_computation | async-start | bytes 655360 | tf_op jit(solution)/shard_map/all_to_all | solution.py:264
  19.5 1.4 %fusion.1 = (s32[1]{0:T(128)}, s32[1]{0:T(128)}, s32[1]{0:T(128)}, s32[1]{0:T(128)}) fusion(s32[4]{0:T(128)} %param.6), kind=kLoop, calls=%fused_computation.10 | loop fusion | bytes 32 | tf_op jit(solution)/shard_map/slice | solution.py:267
  25.9 0.7 convert_element_type.22
  26.6 0.1 reshape.26
  29.1 0.1 stack.23.ids
  29.2 3.1 %all-to-all-done = bf16[32,40,128]{2,1,0:T(8,128)(2,1)S(1)} async-done(((bf16[32,40,128]{2,1,0:T(8,128)(2,1)}), bf16[32,40,128]{2,1,0:T(8,128)(2,1)S(1)}, u32[]{:S(2)}, u32[]{:S(2)}) %all-to-all-start) | async-done | bytes 327712 | tf_op jit(solution)/shard_map/all_to_all | solution.py:264
  32.4 14.5 %all_to_all.15 = bf16[8,128,128]{2,1,0:T(8,128)(2,1)S(1)} all-to-all(bf16[8,128,128]{2,1,0:T(8,128)(2,1)S(1)} %broadcast_in_dim.8), channel_id=1, replica_groups=mesh['y'=8,'xl'=2,'core'=2,'z'=16,'xh'=2] {'y'}, dimensions={0} | all-to-all | bytes 524288 | tf_op jit(solution)/shard_map/all_to_all | solution.py:273
  46.9 1.1 %broadcast_in_dim.9 = bf16[4,1040,128]{2,1,0:T(8,128)(2,1)} broadcast(bf16[1040,128]{1,0:T(8,128)(2,1)S(1)} %pad_maximum_fusion.1), dimensions={1,2} | broadcast | bytes 1331200 | tf_op jit(solution)/shard_map/broadcast_in_dim | solution.py:280
  48.0 3.5 %all-to-all-start.2 = ((bf16[4,1040,128]{2,1,0:T(8,128)(2,1)}), bf16[4,1040,128]{2,1,0:T(8,128)(2,1)S(1)}, u32[]{:S(2)}, u32[]{:S(2)}) async-start(bf16[4,1040,128]{2,1,0:T(8,128)(2,1)} %broadcast_in_dim.9), calls=%async_computation.2 | async-start | bytes 2129920 | tf_op jit(solution)/shard_map/all_to_all | solution.py:279
  51.6 10.0 %collective-permute-start = (bf16[1040,128]{1,0:T(8,128)(2,1)S(1)}, bf16[1040,128]{1,0:T(8,128)(2,1)S(1)}, u32[]{:S(2)}, u32[]{:S(2)}) collective-permute-start(bf16[1040,128]{1,0:T(8,128)(2,1)S(1)} %pad_maximum_fusion.1), channel_id=1, source_target_pairs={{0,30},{2,0},{4,2},{6,4},{8,6},{10,8},{12,10},{14,12},{16,14},{18,... | collective-permute-start | bytes 798728 | tf_op jit(solution)/shard_map/ppermute | solution.py:278
  61.6 3.7 %collective-permute-done = bf16[1040,128]{1,0:T(8,128)(2,1)S(1)} collective-permute-done((bf16[1040,128]{1,0:T(8,128)(2,1)S(1)}, bf16[1040,128]{1,0:T(8,128)(2,1)S(1)}, u32[]{:S(2)}, u32[]{:S(2)}) %collective-permute-start) | collective-permute-done | bytes 266272 | tf_op jit(solution)/shard_map/ppermute | solution.py:278
  65.3 0.0 all-to-all-done.2
  65.3 1.9 %collective-permute-start.1 = (bf16[1040,128]{1,0:T(8,128)(2,1)S(1)}, bf16[1040,128]{1,0:T(8,128)(2,1)S(1)}, u32[]{:S(2)}, u32[]{:S(2)}) collective-permute-start(bf16[1040,128]{1,0:T(8,128)(2,1)S(1)} %dynamic-slice_bitcast_fusion), channel_id=1, source_target_pairs={{30,0},{0,2},{2,4},{4,6},{6,8},{8,10},{10,12},{12,14},{14,16},{16,... | collective-permute-start | bytes 798728 | tf_op jit(solution)/shard_map/ppermute | solution.py:287
  67.3 10.5 %collective-permute-start.2 = (bf16[1040,128]{1,0:T(8,128)(2,1)S(1)}, bf16[1040,128]{1,0:T(8,128)(2,1)S(1)}, u32[]{:S(2)}, u32[]{:S(2)}) collective-permute-start(bf16[1040,128]{1,0:T(8,128)(2,1)S(1)} %collective-permute-done), channel_id=1, source_target_pairs={{0,65},{1,64},{64,1},{65,0},{2,67},{3,66},{66,3},{67,2},{4,69},{5,... | collective-permute-start | bytes 798728 | tf_op jit(solution)/shard_map/ppermute | solution.py:288
  77.8 1.0 collective-permute-done.1
  78.8 3.1 %collective-permute-done.2 = bf16[1040,128]{1,0:T(8,128)(2,1)S(1)} collective-permute-done((bf16[1040,128]{1,0:T(8,128)(2,1)S(1)}, bf16[1040,128]{1,0:T(8,128)(2,1)S(1)}, u32[]{:S(2)}, u32[]{:S(2)}) %collective-permute-start.2) | collective-permute-done | bytes 266272 | tf_op jit(solution)/shard_map/ppermute | solution.py:288
  81.9 0.2 pad_maximum_fusion.own_ref
  82.1 5.7 %collective-permute-start.3 = (bf16[6,1040,128]{2,1,0:T(8,128)(2,1)S(1)}, bf16[6,1040,128]{2,1,0:T(8,128)(2,1)S(1)}, u32[]{:S(2)}, u32[]{:S(2)}) collective-permute-start(bf16[6,1040,128]{2,1,0:T(8,128)(2,1)S(1)} %pad_maximum_fusion.own_ref), channel_id=1, source_target_pairs={{0,32},{32,0},{1,33},{33,1},{2,34},{34,2},{3,35},{35,3},{4,36},{36... | collective-permute-start | bytes 4792328 | tf_op jit(solution)/shard_map/ppermute | solution.py:292
  87.7 5.4 %shard_map.56.rest_1_ = f32[4,32,4096]{2,1,0:T(8,128)} custom-call(s32[5]{0:T(128)S(1)} %stack.23.ids, f32[32,128]{1,0:T(8,128)S(1)} %fusion.prm_ref, f32[1,128]{1,0:T(1,128)S(1)} %convert_element_type.23.band_ref, bf16[6,1040,128]{2,1,0:T(8,128)(2,1)S(1)} %pad_maximum_fusion.own_ref), custom_call_target="tpu_custom_call" | custom-call | flops 503316480 | bytes 25165824 | tf_op jit(solution)/shard_map/pallas_call | solution.py:208
  93.1 0.0 collective-permute-done.3.rest_0_
  93.1 6.0 %shard_map.57 = f32[4,32,4096]{2,1,0:T(8,128)} custom-call(s32[5]{0:T(128)S(1)} %stack.23.ids, f32[32,128]{1,0:T(8,128)S(1)} %fusion.prm_ref, f32[1,128]{1,0:T(1,128)S(1)} %convert_element_type.23.band_ref, bf16[6,1040,128]{2,1,0:T(8,128)(2,1)S(1)} %pad_maximum_fusion.own_ref, ...), custom_call_target="tpu_custom_call", output_to_operand_aliasing={{}: (5, {})} | custom-call | flops 566231040 | bytes 25165824 | tf_op jit(solution)/shard_map/pallas_call | solution.py:208
  (9 shorter events, 0.1 us)
Async XLA Ops:
  1.8 30.5 %all-to-all-start = ((bf16[32,40,128]{2,1,0:T(8,128)(2,1)}), bf16[32,40,128]{2,1,0:T(8,128)(2,1)S(1)}, u32[]{:S(2)}, u32[]{:S(2)}) async-start(bf16[32,40,128]{2,1,0:T(8,128)(2,1)} %shard_map.55), calls=%async_computation | async-start | bytes 655360 | tf_op jit(solution)/shard_map/all_to_all | solution.py:264
  48.0 17.3 %all-to-all-start.2 = ((bf16[4,1040,128]{2,1,0:T(8,128)(2,1)}), bf16[4,1040,128]{2,1,0:T(8,128)(2,1)S(1)}, u32[]{:S(2)}, u32[]{:S(2)}) async-start(bf16[4,1040,128]{2,1,0:T(8,128)(2,1)} %broadcast_in_dim.9), calls=%async_computation.2 | async-start | bytes 2129920 | tf_op jit(solution)/shard_map/all_to_all | solution.py:279
  51.6 13.7 %collective-permute-start = (bf16[1040,128]{1,0:T(8,128)(2,1)S(1)}, bf16[1040,128]{1,0:T(8,128)(2,1)S(1)}, u32[]{:S(2)}, u32[]{:S(2)}) collective-permute-start(bf16[1040,128]{1,0:T(8,128)(2,1)S(1)} %pad_maximum_fusion.1), channel_id=1, source_target_pairs={{0,30},{2,0},{4,2},{6,4},{8,6},{10,8},{12,10},{14,12},{16,14},{18,... | collective-permute-start | bytes 798728 | tf_op jit(solution)/shard_map/ppermute | solution.py:278
  65.3 13.4 %collective-permute-start.1 = (bf16[1040,128]{1,0:T(8,128)(2,1)S(1)}, bf16[1040,128]{1,0:T(8,128)(2,1)S(1)}, u32[]{:S(2)}, u32[]{:S(2)}) collective-permute-start(bf16[1040,128]{1,0:T(8,128)(2,1)S(1)} %dynamic-slice_bitcast_fusion), channel_id=1, source_target_pairs={{30,0},{0,2},{2,4},{4,6},{6,8},{8,10},{10,12},{12,14},{14,16},{16,... | collective-permute-start | bytes 798728 | tf_op jit(solution)/shard_map/ppermute | solution.py:287
  67.3 14.6 %collective-permute-start.2 = (bf16[1040,128]{1,0:T(8,128)(2,1)S(1)}, bf16[1040,128]{1,0:T(8,128)(2,1)S(1)}, u32[]{:S(2)}, u32[]{:S(2)}) collective-permute-start(bf16[1040,128]{1,0:T(8,128)(2,1)S(1)} %collective-permute-done), channel_id=1, source_target_pairs={{0,65},{1,64},{64,1},{65,0},{2,67},{3,66},{66,3},{67,2},{4,69},{5,... | collective-permute-start | bytes 798728 | tf_op jit(solution)/shard_map/ppermute | solution.py:288
  82.1 11.1 %collective-permute-start.3 = (bf16[6,1040,128]{2,1,0:T(8,128)(2,1)S(1)}, bf16[6,1040,128]{2,1,0:T(8,128)(2,1)S(1)}, u32[]{:S(2)}, u32[]{:S(2)}) collective-permute-start(bf16[6,1040,128]{2,1,0:T(8,128)(2,1)S(1)} %pad_maximum_fusion.own_ref), channel_id=1, source_target_pairs={{0,32},{32,0},{1,33},{33,1},{2,34},{34,2},{3,35},{35,3},{4,36},{36... | collective-permute-start | bytes 4792328 | tf_op jit(solution)/shard_map/ppermute | solution.py:292

commit v5 on v4

--- a/solution.py
+++ b/solution.py
@@ -69,7 +69,7 @@
     for i in range(DEEP):
         at = depth * HERE + (i - 2)
         at = jnp.where(at < 0, -1 - at, jnp.where(at > last_slice, 2 * last_slice + 1 - at, at))
-        mine = prm_ref[pl.ds(at >> 2, 1), :]
+        mine = prm_ref[pl.ds((at >> 2) - depth + 1, 1), :]
         held.append(jnp.where(lane_slice == (at & 3), mine, 0.0))
     held = jnp.concatenate(held, axis=0)
     stacked = jnp.concatenate([jnp.where(kind, held, 0.0) for kind in kinds], axis=0)
@@ -228,7 +228,7 @@
     )(*operands)
 
 
-def pack(stored_ref, offset_ref, taps_ref, out_ref):
+def pack(stored_ref, offset_ref, taps_ref, out_ref, numbers_ref):
     lane = lax.broadcasted_iota(I32, (1, LANES), 1)
     rest = lane - 4 * VIEWS
     line = lax.broadcasted_iota(I32, (HERE, LANES), 0)
@@ -240,13 +240,12 @@
         spread = jnp.dot(taps_ref[v].astype(F32), pick, preferred_element_type=F32)
         mine = (line == ((rest >> 2) & 3)) & (rest >= 0) & ((rest >> 4) == v)
         numbers += jnp.sum(jnp.where(mine, spread, 0.0), axis=0, keepdims=True)
-    numbers = jnp.broadcast_to(numbers, (8, LANES)).astype(BF16)
+    numbers_ref[...] = jnp.broadcast_to(numbers, (16, LANES)).astype(BF16)
     for y in range(8):
         for xl in range(2):
             for core in range(2):
                 at = ((core * 2 + xl) * 8 + y) * LANES
-                piece = stored_ref[:, at : at + LANES]
-                out_ref[(y * 2 + xl) * 2 + core] = jnp.concatenate([piece, numbers], axis=0)
+                out_ref[(y * 2 + xl) * 2 + core] = stored_ref[:, at : at + LANES]
 
 
 def shards(projections, owner, row_offset, band_start, taps):
@@ -255,17 +254,22 @@
     ids = jnp.stack([depth, tile, xh, core, xl]).astype(I32)
 
     whole = pl.BlockSpec(memory_space=pltpu.VMEM)
-    pieces = pl.pallas_call(
+    pieces, numbers = pl.pallas_call(
         pack,
-        out_shape=jax.ShapeDtypeStruct((32, TILE + 8, LANES), BF16),
+        out_shape=(
+            jax.ShapeDtypeStruct((32, TILE, LANES), BF16),
+            jax.ShapeDtypeStruct((16, LANES), BF16),
+        ),
         in_specs=[whole] * 3,
-        out_specs=whole,
+        out_specs=[whole] * 2,
     )(projections[0], row_offset, taps)
     got = lax.all_to_all(pieces, DEPTH, 0, 0, tiled=True)
-    prm = got[:, TILE, :].astype(F32)
     views = jnp.concatenate(
-        [lax.dynamic_index_in_dim(got, owner[v], keepdims=False)[:TILE] for v in range(VIEWS)]
+        [lax.dynamic_index_in_dim(got, owner[v], keepdims=False) for v in range(VIEWS)]
     )
+    lower = lax.ppermute(numbers, DEPTH, [(i, (i + 1) % 32) for i in range(32)])
+    upper = lax.ppermute(numbers, DEPTH, [((i + 1) % 32, i) for i in range(32)])
+    prm = jnp.concatenate([lower[:1], numbers[:1], upper[:1]]).astype(F32)
 
     band = band_start.astype(BF16).reshape(1, SIZE)
     rest = (band.astype(F32), jnp.pad(band, ((0, 15), (0, 0))), prm, ids)
@@ -273,6 +277,7 @@
     near = lax.all_to_all(jnp.broadcast_to(views[None], (8, SIZE, LANES)), "y", 0, 0, tiled=True)
     near = jnp.concatenate([near.reshape(8 * SIZE, LANES), band_rows])
 
+    swap = [(0, 1), (1, 0)]
     shift = [(2 * i, (2 * i - 2) % 32) for i in range(16)]
     shift += [(2 * i + 1, (2 * i + 3) % 32) for i in range(16)]
     foreign = lax.ppermute(near, ("z", "xh"), shift)
@@ -280,14 +285,10 @@
         jnp.broadcast_to(near[None], (4,) + near.shape), ("xh", "xl"), 0, 0, tiled=True
     )
 
-    own, foreign = lax.optimization_barrier((own, foreign))
-
-    along = [(a, b) for b, a in shift]
-    third = lax.dynamic_index_in_dim(own, 2 * (1 - xh) + xl, keepdims=False)
-    third = lax.ppermute(third, ("z", "xh"), along)
     third_far = lax.ppermute(foreign, ("xl", "xh"), [(0, 3), (1, 2), (2, 1), (3, 0)])
-
-    swap = [(0, 1), (1, 0)]
+    third = lax.ppermute(third_far, "xl", swap)
+    own, third = lax.optimization_barrier((own, third))
+
     own = jnp.concatenate([own, third[None], third_far[None]])
     other = lax.ppermute(own, "core", swap)
     first = smooth(False, ids, prm, band, own)

time: 99.7 us -> 114 us (1.14)
  waiting for transfers between devices: 10.9 us -> 21.5 us
  blocking collectives: 14.5 us -> 18.8 us
  starting transfers between devices: 49.3 us -> 47.7 us
    ppermute x1, waiting for transfers between devices: 3.1 us -> 14.6 us  [shards(): lax.ppermute(foreign, ('xl', 'xh'), [(0, 3), (1, 2), (2, 1), (3, 0)])]
    ppermute x1, starting transfers between devices: 10.5 us -> 4.71 us  [shards(): lax.ppermute(foreign, ('xl', 'xh'), [(0, 3), (1, 2), (2, 1), (3, 0)])]
    ppermute x1 -> x3, starting transfers between devices: 1.92 us -> 7.47 us  [the longest x1 3.31 us: shards(): lower = lax.ppermute(numbers, DEPTH, [(i, (i + 1) % 32) for i in range(32)])]
    ppermute x1 -> x3, waiting for transfers between devices: 0.99 us -> 6.25 us  [the longest x1 6.25 us: shards(): third = lax.ppermute(third_far, 'xl', swap)]
    all_to_all x1, blocking collectives: 14.5 us -> 18.8 us  [shards(): lax.all_to_all(jnp.broadcast_to(views[None], (8, SIZE, LANES)), 'y', 0, 0...]
    all_to_all x1, waiting for transfers between devices: 3.11 us -> 0.01 us  [shards(): got = lax.all_to_all(pieces, DEPTH, 0, 0, tiled=True)]
    ppermute x1, waiting for transfers between devices: 3.68 us -> 0.66 us  [shards(): foreign = lax.ppermute(near, ('z', 'xh'), shift)]
    ppermute x1, starting transfers between devices: 5.66 us -> 4.44 us  [shards(): other = lax.ppermute(own, 'core', swap)]
  transfers between devices with their start and end apart: 6 -> 8, of which waited for: 4 -> 3; matrix products, arithmetic and copies ran while one was open for 2% -> 4% of each run, Pallas kernels for 5% -> 5%
where the time goes in v5:
time: 114 us; the launch traced here: 113 us
  starting transfers between devices  47.7 us (42%)
  waiting for transfers between devices  21.5 us (19%)
  blocking collectives  18.8 us (16%)
  Pallas kernels  13.1 us (11%)
  between operations  7.84 us (7%)
  local copies, waits for them, and re-layouts  3.47 us (3%)
    all_to_all x1, blocking collectives, shards(): lax.all_to_all(jnp.broadcast_to(views[None], (8, SIZE, LANES)), 'y', 0, 0...  18.8 us
    all_to_all x1, starting transfers between devices, shards(): got = lax.all_to_all(pieces, DEPTH, 0, 0, tiled=True)  17.7 us
    ppermute x1, waiting for transfers between devices, shards(): lax.ppermute(foreign, ('xl', 'xh'), [(0, 3), (1, 2), (2, 1), (3, 0)])  14.6 us
    pallas_call x2, Pallas kernels, smooth(): pl.pallas_call(functools.partial(half, second), out_shape=jax.ShapeDtypeS...  11.4 us
    ppermute x1, starting transfers between devices, shards(): foreign = lax.ppermute(near, ('z', 'xh'), shift)  9.86 us
    ppermute x1, waiting for transfers between devices, shards(): third = lax.ppermute(third_far, 'xl', swap)  6.25 us
    ppermute x1, starting transfers between devices, shards(): lax.ppermute(foreign, ('xl', 'xh'), [(0, 3), (1, 2), (2, 1), (3, 0)])  4.71 us
    ppermute x1, starting transfers between devices, shards(): other = lax.ppermute(own, 'core', swap)  4.44 us
  transfers between devices with their start and end apart: 8, of which 3 were waited for; matrix products, arithmetic and copies ran while one was open for 4% of the time, Pallas kernels for 5%

profile of v5, /device:TPU:1, one launch (start us, length us, event | category | flops | bytes accessed | tf_op | source)
XLA Modules:
  0.0 113.4 jit_solution(6516762821710558931)
XLA Ops:
  0.0 1.7 %shard_map.55 = (bf16[32,32,128]{2,1,0:T(8,128)(2,1)}, bf16[16,128]{1,0:T(8,128)(2,1)}) custom-call(bf16[32,4096]{1,0:T(8,128)(2,1)} %bitcast.24, s32[4,4]{1,0:T(4,128)} %offset_ref.1, bf16[4,4,4]{2,1,0:T(4,128)(2,1)} %taps_ref.1), custom_call_target="tpu_custom_call" | custom-call | tf_op jit(solution)/shard_map/pallas_call | solution.py:257
  1.7 17.7 %all-to-all-start = ((bf16[32,32,128]{2,1,0:T(8,128)(2,1)}), bf16[32,32,128]{2,1,0:T(8,128)(2,1)S(1)}, u32[]{:S(2)}, u32[]{:S(2)}) async-start(bf16[32,32,128]{2,1,0:T(8,128)(2,1)} %get-tuple-element.14), calls=%async_computation | async-start | bytes 524288 | tf_op jit(solution)/shard_map/all_to_all | solution.py:266
  19.4 2.3 %collective-permute-start.1 = (bf16[16,128]{1,0:T(8,128)(2,1)}, bf16[16,128]{1,0:T(8,128)(2,1)S(1)}, u32[]{:S(2)}, u32[]{:S(2)}) collective-permute-start(bf16[16,128]{1,0:T(8,128)(2,1)} %get-tuple-element.15), channel_id=1, source_target_pairs={{32,0},{64,32},{96,64},{128,96},{160,128},{192,160},{224,192},{256... | collective-permute-start | bytes 12296 | tf_op jit(solution)/shard_map/ppermute | solution.py:271
  21.7 3.3 %collective-permute-start = (bf16[16,128]{1,0:T(8,128)(2,1)}, bf16[16,128]{1,0:T(8,128)(2,1)S(1)}, u32[]{:S(2)}, u32[]{:S(2)}) collective-permute-start(bf16[16,128]{1,0:T(8,128)(2,1)} %get-tuple-element.15), channel_id=1, source_target_pairs={{0,32},{32,64},{64,96},{96,128},{128,160},{160,192},{192,224},{224... | collective-permute-start | bytes 12296 | tf_op jit(solution)/shard_map/ppermute | solution.py:270
  25.0 1.5 %fusion = (s32[1]{0:T(128)}, s32[1]{0:T(128)}, s32[1]{0:T(128)}, s32[1]{0:T(128)}) fusion(s32[4]{0:T(128)} %param.6), kind=kLoop, calls=%fused_computation.8 | loop fusion | bytes 32 | tf_op jit(solution)/shard_map/slice | solution.py:268
  31.6 0.7 slice.26
  32.2 0.7 convert_element_type.19
  32.9 0.1 reshape.20
  35.6 0.1 stack.23.ids
  35.7 0.0 collective-permute-done.1
  35.7 0.0 collective-permute-done
  35.7 0.0 all-to-all-done
  35.8 18.8 %all_to_all.15 = bf16[8,128,128]{2,1,0:T(8,128)(2,1)S(1)} all-to-all(bf16[8,128,128]{2,1,0:T(8,128)(2,1)S(1)} %broadcast_in_dim.8), channel_id=1, replica_groups=mesh['y'=8,'xl'=2,'core'=2,'z'=16,'xh'=2] {'y'}, dimensions={0} | all-to-all | bytes 524288 | tf_op jit(solution)/shard_map/all_to_all | solution.py:277
  54.7 9.9 %collective-permute-start.2 = (bf16[1040,128]{1,0:T(8,128)(2,1)S(1)}, bf16[1040,128]{1,0:T(8,128)(2,1)S(1)}, u32[]{:S(2)}, u32[]{:S(2)}) collective-permute-start(bf16[1040,128]{1,0:T(8,128)(2,1)S(1)} %pad_maximum_fusion.1), channel_id=1, source_target_pairs={{0,30},{2,0},{4,2},{6,4},{8,6},{10,8},{12,10},{14,12},{16,14},{18,... | collective-permute-start | bytes 798728 | tf_op jit(solution)/shard_map/ppermute | solution.py:283
  64.5 1.1 broadcast_in_dim.9
  65.7 3.5 %all-to-all-start.2 = ((bf16[4,1040,128]{2,1,0:T(8,128)(2,1)}), bf16[4,1040,128]{2,1,0:T(8,128)(2,1)S(1)}, u32[]{:S(2)}, u32[]{:S(2)}) async-start(bf16[4,1040,128]{2,1,0:T(8,128)(2,1)} %broadcast_in_dim.9), calls=%async_computation.2 | async-start | bytes 2129920 | tf_op jit(solution)/shard_map/all_to_all | solution.py:284
  69.2 0.7 collective-permute-done.2
  69.8 4.7 %collective-permute-start.3 = (bf16[1040,128]{1,0:T(8,128)(2,1)S(1)}, bf16[1040,128]{1,0:T(8,128)(2,1)S(1)}, u32[]{:S(2)}, u32[]{:S(2)}) collective-permute-start(bf16[1040,128]{1,0:T(8,128)(2,1)S(1)} %collective-permute-done.2), channel_id=1, source_target_pairs={{0,65},{1,64},{64,1},{65,0},{2,67},{3,66},{66,3},{67,2},{4,69},{5,... | collective-permute-start | bytes 798728 | tf_op jit(solution)/shard_map/ppermute | solution.py:288
  74.6 14.6 %collective-permute-done.3 = bf16[1040,128]{1,0:T(8,128)(2,1)S(1)} collective-permute-done((bf16[1040,128]{1,0:T(8,128)(2,1)S(1)}, bf16[1040,128]{1,0:T(8,128)(2,1)S(1)}, u32[]{:S(2)}, u32[]{:S(2)}) %collective-permute-start.3) | collective-permute-done | bytes 266272 | tf_op jit(solution)/shard_map/ppermute | solution.py:288
  89.2 1.9 %collective-permute-start.4 = (bf16[1040,128]{1,0:T(8,128)(2,1)S(1)}, bf16[1040,128]{1,0:T(8,128)(2,1)S(1)}, u32[]{:S(2)}, u32[]{:S(2)}) collective-permute-start(bf16[1040,128]{1,0:T(8,128)(2,1)S(1)} %collective-permute-done.3), channel_id=1, source_target_pairs={{0,64},{64,0},{1,65},{65,1},{2,66},{66,2},{3,67},{67,3},{4,68},{68... | collective-permute-start | bytes 798728 | tf_op jit(solution)/shard_map/ppermute | solution.py:289
  91.1 6.2 %collective-permute-done.4 = bf16[1040,128]{1,0:T(8,128)(2,1)S(1)} collective-permute-done((bf16[1040,128]{1,0:T(8,128)(2,1)S(1)}, bf16[1040,128]{1,0:T(8,128)(2,1)S(1)}, u32[]{:S(2)}, u32[]{:S(2)}) %collective-permute-start.4) | collective-permute-done | bytes 266272 | tf_op jit(solution)/shard_map/ppermute | solution.py:289
  97.3 0.0 all-to-all-done.2
  97.3 0.2 pad_maximum_fusion.own_ref
  97.5 4.4 %collective-permute-start.5 = (bf16[6,1040,128]{2,1,0:T(8,128)(2,1)S(1)}, bf16[6,1040,128]{2,1,0:T(8,128)(2,1)S(1)}, u32[]{:S(2)}, u32[]{:S(2)}) collective-permute-start(bf16[6,1040,128]{2,1,0:T(8,128)(2,1)S(1)} %pad_maximum_fusion.own_ref), channel_id=1, source_target_pairs={{0,32},{32,0},{1,33},{33,1},{2,34},{34,2},{3,35},{35,3},{4,36},{36... | collective-permute-start | bytes 4792328 | tf_op jit(solution)/shard_map/ppermute | solution.py:293
  102.0 5.4 %shard_map.56.rest_1_ = f32[4,32,4096]{2,1,0:T(8,128)} custom-call(s32[5]{0:T(128)S(1)} %stack.23.ids, f32[3,128]{1,0:T(4,128)S(1)} %maximum_convert_fusion.prm_ref, f32[1,128]{1,0:T(1,128)S(1)} %convert_element_type.20.band_ref, bf16[6,1040,128]{2,1,0:T(8,128)(2,1)S(1)} %pad_maximum_fusion.own_ref), custom_call_target="tpu_custom_call" | custom-call | flops 503316480 | bytes 25165824 | tf_op jit(solution)/shard_map/pallas_call | solution.py:208
  107.4 0.0 collective-permute-done.5.rest_0_
  107.4 6.0 %shard_map.57 = f32[4,32,4096]{2,1,0:T(8,128)} custom-call(s32[5]{0:T(128)S(1)} %stack.23.ids, f32[3,128]{1,0:T(4,128)S(1)} %maximum_convert_fusion.prm_ref, f32[1,128]{1,0:T(1,128)S(1)} %convert_element_type.20.band_ref, bf16[6,1040,128]{2,1,0:T(8,128)(2,1)S(1)} %pad_maximum_fusion.own_ref, ...), custom_call_target="tpu_custom_call", output_to_operand_aliasing={{}: (5, {})} | custom-call | flops 566231040 | bytes 25165824 | tf_op jit(solution)/shard_map/pallas_call | solution.py:208
  (9 shorter events, 0.1 us)
Async XLA Ops:
  1.7 34.0 %all-to-all-start = ((bf16[32,32,128]{2,1,0:T(8,128)(2,1)}), bf16[32,32,128]{2,1,0:T(8,128)(2,1)S(1)}, u32[]{:S(2)}, u32[]{:S(2)}) async-start(bf16[32,32,128]{2,1,0:T(8,128)(2,1)} %get-tuple-element.14), calls=%async_computation | async-start | bytes 524288 | tf_op jit(solution)/shard_map/all_to_all | solution.py:266
  19.4 16.3 %collective-permute-start.1 = (bf16[16,128]{1,0:T(8,128)(2,1)}, bf16[16,128]{1,0:T(8,128)(2,1)S(1)}, u32[]{:S(2)}, u32[]{:S(2)}) collective-permute-start(bf16[16,128]{1,0:T(8,128)(2,1)} %get-tuple-element.15), channel_id=1, source_target_pairs={{32,0},{64,32},{96,64},{128,96},{160,128},{192,160},{224,192},{256... | collective-permute-start | bytes 12296 | tf_op jit(solution)/shard_map/ppermute | solution.py:271
  21.7 14.0 %collective-permute-start = (bf16[16,128]{1,0:T(8,128)(2,1)}, bf16[16,128]{1,0:T(8,128)(2,1)S(1)}, u32[]{:S(2)}, u32[]{:S(2)}) collective-permute-start(bf16[16,128]{1,0:T(8,128)(2,1)} %get-tuple-element.15), channel_id=1, source_target_pairs={{0,32},{32,64},{64,96},{96,128},{128,160},{160,192},{192,224},{224... | collective-permute-start | bytes 12296 | tf_op jit(solution)/shard_map/ppermute | solution.py:270
  54.7 15.2 %collective-permute-start.2 = (bf16[1040,128]{1,0:T(8,128)(2,1)S(1)}, bf16[1040,128]{1,0:T(8,128)(2,1)S(1)}, u32[]{:S(2)}, u32[]{:S(2)}) collective-permute-start(bf16[1040,128]{1,0:T(8,128)(2,1)S(1)} %pad_maximum_fusion.1), channel_id=1, source_target_pairs={{0,30},{2,0},{4,2},{6,4},{8,6},{10,8},{12,10},{14,12},{16,14},{18,... | collective-permute-start | bytes 798728 | tf_op jit(solution)/shard_map/ppermute | solution.py:283
  65.7 31.7 %all-to-all-start.2 = ((bf16[4,1040,128]{2,1,0:T(8,128)(2,1)}), bf16[4,1040,128]{2,1,0:T(8,128)(2,1)S(1)}, u32[]{:S(2)}, u32[]{:S(2)}) async-start(bf16[4,1040,128]{2,1,0:T(8,128)(2,1)} %broadcast_in_dim.9), calls=%async_computation.2 | async-start | bytes 2129920 | tf_op jit(solution)/shard_map/all_to_all | solution.py:284
  69.8 19.3 %collective-permute-start.3 = (bf16[1040,128]{1,0:T(8,128)(2,1)S(1)}, bf16[1040,128]{1,0:T(8,128)(2,1)S(1)}, u32[]{:S(2)}, u32[]{:S(2)}) collective-permute-start(bf16[1040,128]{1,0:T(8,128)(2,1)S(1)} %collective-permute-done.2), channel_id=1, source_target_pairs={{0,65},{1,64},{64,1},{65,0},{2,67},{3,66},{66,3},{67,2},{4,69},{5,... | collective-permute-start | bytes 798728 | tf_op jit(solution)/shard_map/ppermute | solution.py:288
  89.2 8.2 %collective-permute-start.4 = (bf16[1040,128]{1,0:T(8,128)(2,1)S(1)}, bf16[1040,128]{1,0:T(8,128)(2,1)S(1)}, u32[]{:S(2)}, u32[]{:S(2)}) collective-permute-start(bf16[1040,128]{1,0:T(8,128)(2,1)S(1)} %collective-permute-done.3), channel_id=1, source_target_pairs={{0,64},{64,0},{1,65},{65,1},{2,66},{66,2},{3,67},{67,3},{4,68},{68... | collective-permute-start | bytes 798728 | tf_op jit(solution)/shard_map/ppermute | solution.py:289
  97.5 9.8 %collective-permute-start.5 = (bf16[6,1040,128]{2,1,0:T(8,128)(2,1)S(1)}, bf16[6,1040,128]{2,1,0:T(8,128)(2,1)S(1)}, u32[]{:S(2)}, u32[]{:S(2)}) collective-permute-start(bf16[6,1040,128]{2,1,0:T(8,128)(2,1)S(1)} %pad_maximum_fusion.own_ref), channel_id=1, source_target_pairs={{0,32},{32,0},{1,33},{33,1},{2,34},{34,2},{3,35},{35,3},{4,36},{36... | collective-permute-start | bytes 4792328 | tf_op jit(solution)/shard_map/ppermute | solution.py:293

commit v6 on v4

--- a/solution.py
+++ b/solution.py
@@ -264,7 +264,12 @@
     got = lax.all_to_all(pieces, DEPTH, 0, 0, tiled=True)
     prm = got[:, TILE, :].astype(F32)
     views = jnp.concatenate(
-        [lax.dynamic_index_in_dim(got, owner[v], keepdims=False)[:TILE] for v in range(VIEWS)]
+        [
+            lax.dynamic_slice(
+                got, (owner[v], 0, 0), (1, TILE, LANES), allow_negative_indices=False
+            )[0]
+            for v in range(VIEWS)
+        ]
     )
 
     band = band_start.astype(BF16).reshape(1, SIZE)
@@ -273,8 +278,7 @@
     near = lax.all_to_all(jnp.broadcast_to(views[None], (8, SIZE, LANES)), "y", 0, 0, tiled=True)
     near = jnp.concatenate([near.reshape(8 * SIZE, LANES), band_rows])
 
-    shift = [(2 * i, (2 * i - 2) % 32) for i in range(16)]
-    shift += [(2 * i + 1, (2 * i + 3) % 32) for i in range(16)]
+    shift = [(2 * i + 2, 2 * i) for i in range(15)] + [(2 * i + 1, 2 * i + 3) for i in range(15)]
     foreign = lax.ppermute(near, ("z", "xh"), shift)
     own = lax.all_to_all(
         jnp.broadcast_to(near[None], (4,) + near.shape), ("xh", "xl"), 0, 0, tiled=True
@@ -283,7 +287,9 @@
     own, foreign = lax.optimization_barrier((own, foreign))
 
     along = [(a, b) for b, a in shift]
-    third = lax.dynamic_index_in_dim(own, 2 * (1 - xh) + xl, keepdims=False)
+    third = lax.dynamic_slice(
+        own, (2 * (1 - xh) + xl, 0, 0), (1,) + near.shape, allow_negative_indices=False
+    )[0]
     third = lax.ppermute(third, ("z", "xh"), along)
     third_far = lax.ppermute(foreign, ("xl", "xh"), [(0, 3), (1, 2), (2, 1), (3, 0)])
 

time: 99.7 us -> 94.2 us (0.945)
  waiting for transfers between devices: 10.9 us -> 27.9 us
  starting transfers between devices: 49.3 us -> 32.7 us
  between operations: 7.5 us -> 0.14 us
  local copies, waits for them, and re-layouts: 2.8 us -> 5.23 us
    ppermute x1, starting transfers between devices: 10 us -> 1.29 us  [shards(): foreign = lax.ppermute(near, ('z', 'xh'), shift)]
    ppermute x1, starting transfers between devices: 10.5 us -> 2.78 us  [shards(): lax.ppermute(foreign, ('xl', 'xh'), [(0, 3), (1, 2), (2, 1), (3, 0)])]
    all_to_all x1, waiting for transfers between devices: 3.11 us -> 10.5 us  [shards(): got = lax.all_to_all(pieces, DEPTH, 0, 0, tiled=True)]
    all_to_all x1, waiting for transfers between devices: 0.01 us -> 5.49 us  [shards(): lax.all_to_all(jnp.broadcast_to(near[None], (4,) + near.shape), ('xh', 'x...]
    ppermute x1, waiting for transfers between devices: 3.68 us -> 6.33 us  [shards(): foreign = lax.ppermute(near, ('z', 'xh'), shift)]
    squeeze x1 -> x2, local copies, waits for them, and re-layouts: 0.02 us -> 2.47 us  [the longest x1 2.45 us: shards(): lax.dynamic_slice(got, (owner[v], 0, 0), (1, TILE, LANES), allow_negative...]
    ppermute x1, waiting for transfers between devices: 3.1 us -> 5.04 us  [shards(): lax.ppermute(foreign, ('xl', 'xh'), [(0, 3), (1, 2), (2, 1), (3, 0)])]
  transfers between devices with their start and end apart: 6 -> 6, of which waited for: 4 -> 5; matrix products, arithmetic and copies ran while one was open for 2% -> 2% of each run, Pallas kernels for 5% -> 6%
where the time goes in v6:
time: 94.2 us; the launch traced here: 93.8 us
  starting transfers between devices  32.7 us (35%)
  waiting for transfers between devices  27.9 us (30%)
  blocking collectives  13.7 us (15%)
  Pallas kernels  13.2 us (14%)
  local copies, waits for them, and re-layouts  5.23 us (6%)
    all_to_all x1, starting transfers between devices, shards(): got = lax.all_to_all(pieces, DEPTH, 0, 0, tiled=True)  17.7 us
    all_to_all x1, blocking collectives, shards(): lax.all_to_all(jnp.broadcast_to(views[None], (8, SIZE, LANES)), 'y', 0, 0...  13.7 us
    pallas_call x2, Pallas kernels, smooth(): pl.pallas_call(functools.partial(half, second), out_shape=jax.ShapeDtypeS...  11.4 us
    all_to_all x1, waiting for transfers between devices, shards(): got = lax.all_to_all(pieces, DEPTH, 0, 0, tiled=True)  10.5 us
    ppermute x1, waiting for transfers between devices, shards(): foreign = lax.ppermute(near, ('z', 'xh'), shift)  6.33 us
    ppermute x1, starting transfers between devices, shards(): other = lax.ppermute(own, 'core', swap)  6.12 us
    all_to_all x1, waiting for transfers between devices, shards(): lax.all_to_all(jnp.broadcast_to(near[None], (4,) + near.shape), ('xh', 'x...  5.49 us
    ppermute x1, waiting for transfers between devices, shards(): lax.ppermute(foreign, ('xl', 'xh'), [(0, 3), (1, 2), (2, 1), (3, 0)])  5.04 us
  transfers between devices with their start and end apart: 6, of which 5 were waited for; matrix products, arithmetic and copies ran while one was open for 2% of the time, Pallas kernels for 6%

profile of v6, /device:TPU:1, one launch (start us, length us, event | category | flops | bytes accessed | tf_op | source)
XLA Modules:
  0.0 93.8 jit_solution(11816635692740206394)
XLA Ops:
  0.0 1.8 %shard_map.55 = bf16[32,40,128]{2,1,0:T(8,128)(2,1)} custom-call(bf16[32,4096]{1,0:T(8,128)(2,1)} %bitcast.31, s32[4,4]{1,0:T(4,128)} %offset_ref.1, bf16[4,4,4]{2,1,0:T(4,128)(2,1)} %taps_ref.1), custom_call_target="tpu_custom_call" | custom-call | tf_op jit(solution)/shard_map/pallas_call | solution.py:258
  1.8 17.7 %all-to-all-start = ((bf16[32,40,128]{2,1,0:T(8,128)(2,1)}), bf16[32,40,128]{2,1,0:T(8,128)(2,1)S(1)}, u32[]{:S(2)}, u32[]{:S(2)}) async-start(bf16[32,40,128]{2,1,0:T(8,128)(2,1)} %shard_map.55), calls=%async_computation | async-start | bytes 655360 | tf_op jit(solution)/shard_map/all_to_all | solution.py:264
  19.5 0.7 convert_element_type.22
  20.2 0.1 reshape.22
  20.3 0.1 stack.23.ids
  20.4 1.4 %fusion.1 = (s32[1]{0:T(128)}, s32[1]{0:T(128)}, s32[1]{0:T(128)}, s32[1]{0:T(128)}) fusion(s32[4]{0:T(128)} %param.6), kind=kLoop, calls=%fused_computation.10 | loop fusion | bytes 32 | tf_op jit(solution)/shard_map/slice | solution.py:269
  21.8 10.5 %all-to-all-done = bf16[32,40,128]{2,1,0:T(8,128)(2,1)S(1)} async-done(((bf16[32,40,128]{2,1,0:T(8,128)(2,1)}), bf16[32,40,128]{2,1,0:T(8,128)(2,1)S(1)}, u32[]{:S(2)}, u32[]{:S(2)}) %all-to-all-start) | async-done | bytes 327712 | tf_op jit(solution)/shard_map/all_to_all | solution.py:264
  32.3 2.5 %dynamic-slice_bitcast_fusion.4 = (bf16[32,128]{1,0:T(8,128)(2,1)S(1)}, bf16[32,128]{1,0:T(8,128)(2,1)S(1)}, bf16[32,128]{1,0:T(8,128)(2,1)S(1)}, bf16[32,128]{1,0:T(8,128)(2,1)S(1)}) fusion(bf16[32,40,128]{2,1,0:T(8,128)(2,1)S(1)} %all-to-all-done, s32[]{:T(128)} %bitcast.1, s32[]{:T(128)} %bitcast.7, s32[]{:T(128)} %bitcast.5, s32[]{:T(128)} %bitcast.3), kind=kLoop, calls=%fused_computation.9 | loop fusion | bytes 65552 | tf_op jit(solution)/shard_map/squeeze | solution.py:268
  34.8 13.7 %all_to_all.15 = bf16[8,128,128]{2,1,0:T(8,128)(2,1)S(1)} all-to-all(bf16[8,128,128]{2,1,0:T(8,128)(2,1)S(1)} %broadcast_in_dim.8), channel_id=1, replica_groups=mesh['y'=8,'xl'=2,'core'=2,'z'=16,'xh'=2] {'y'}, dimensions={0} | all-to-all | bytes 524288 | tf_op jit(solution)/shard_map/all_to_all | solution.py:278
  48.5 1.1 %broadcast_in_dim.9 = bf16[4,1040,128]{2,1,0:T(8,128)(2,1)} broadcast(bf16[1040,128]{1,0:T(8,128)(2,1)S(1)} %pad_maximum_fusion.1), dimensions={1,2} | broadcast | bytes 1331200 | tf_op jit(solution)/shard_map/broadcast_in_dim | solution.py:284
  49.6 3.5 %all-to-all-start.2 = ((bf16[4,1040,128]{2,1,0:T(8,128)(2,1)}), bf16[4,1040,128]{2,1,0:T(8,128)(2,1)S(1)}, u32[]{:S(2)}, u32[]{:S(2)}) async-start(bf16[4,1040,128]{2,1,0:T(8,128)(2,1)} %broadcast_in_dim.9), calls=%async_computation.2 | async-start | bytes 2129920 | tf_op jit(solution)/shard_map/all_to_all | solution.py:283
  53.2 1.3 %collective-permute-start = (bf16[1040,128]{1,0:T(8,128)(2,1)S(1)}, bf16[1040,128]{1,0:T(8,128)(2,1)S(1)}, u32[]{:S(2)}, u32[]{:S(2)}) collective-permute-start(bf16[1040,128]{1,0:T(8,128)(2,1)S(1)} %pad_maximum_fusion.1), channel_id=1, source_target_pairs={{2,0},{4,2},{6,4},{8,6},{10,8},{12,10},{14,12},{16,14},{18,16},{20... | collective-permute-start | bytes 798728 | tf_op jit(solution)/shard_map/ppermute | solution.py:282
  54.5 6.3 %collective-permute-done = bf16[1040,128]{1,0:T(8,128)(2,1)S(1)} collective-permute-done((bf16[1040,128]{1,0:T(8,128)(2,1)S(1)}, bf16[1040,128]{1,0:T(8,128)(2,1)S(1)}, u32[]{:S(2)}, u32[]{:S(2)}) %collective-permute-start) | collective-permute-done | bytes 266272 | tf_op jit(solution)/shard_map/ppermute | solution.py:282
  60.8 5.5 %all-to-all-done.2 = bf16[4,1040,128]{2,1,0:T(8,128)(2,1)S(1)} async-done(((bf16[4,1040,128]{2,1,0:T(8,128)(2,1)}), bf16[4,1040,128]{2,1,0:T(8,128)(2,1)S(1)}, u32[]{:S(2)}, u32[]{:S(2)}) %all-to-all-start.2) | async-done | bytes 1064992 | tf_op jit(solution)/shard_map/all_to_all | solution.py:283
  66.3 1.3 %collective-permute-start.1 = (bf16[1040,128]{1,0:T(8,128)(2,1)S(1)}, bf16[1040,128]{1,0:T(8,128)(2,1)S(1)}, u32[]{:S(2)}, u32[]{:S(2)}) collective-permute-start(bf16[1040,128]{1,0:T(8,128)(2,1)S(1)} %dynamic-slice_bitcast_fusion), channel_id=1, source_target_pairs={{0,2},{2,4},{4,6},{6,8},{8,10},{10,12},{12,14},{14,16},{16,18},{18... | collective-permute-start | bytes 798728 | tf_op jit(solution)/shard_map/ppermute | solution.py:293
  67.6 2.8 %collective-permute-start.2 = (bf16[1040,128]{1,0:T(8,128)(2,1)S(1)}, bf16[1040,128]{1,0:T(8,128)(2,1)S(1)}, u32[]{:S(2)}, u32[]{:S(2)}) collective-permute-start(bf16[1040,128]{1,0:T(8,128)(2,1)S(1)} %collective-permute-done), channel_id=1, source_target_pairs={{0,65},{1,64},{64,1},{65,0},{2,67},{3,66},{66,3},{67,2},{4,69},{5,... | collective-permute-start | bytes 798728 | tf_op jit(solution)/shard_map/ppermute | solution.py:294
  70.4 0.5 collective-permute-done.1
  71.0 5.0 %collective-permute-done.2 = bf16[1040,128]{1,0:T(8,128)(2,1)S(1)} collective-permute-done((bf16[1040,128]{1,0:T(8,128)(2,1)S(1)}, bf16[1040,128]{1,0:T(8,128)(2,1)S(1)}, u32[]{:S(2)}, u32[]{:S(2)}) %collective-permute-start.2) | collective-permute-done | bytes 266272 | tf_op jit(solution)/shard_map/ppermute | solution.py:294
  76.0 0.2 pad_maximum_fusion.own_ref
  76.2 6.1 %collective-permute-start.3 = (bf16[6,1040,128]{2,1,0:T(8,128)(2,1)S(1)}, bf16[6,1040,128]{2,1,0:T(8,128)(2,1)S(1)}, u32[]{:S(2)}, u32[]{:S(2)}) collective-permute-start(bf16[6,1040,128]{2,1,0:T(8,128)(2,1)S(1)} %pad_maximum_fusion.own_ref), channel_id=1, source_target_pairs={{0,32},{32,0},{1,33},{33,1},{2,34},{34,2},{3,35},{35,3},{4,36},{36... | collective-permute-start | bytes 4792328 | tf_op jit(solution)/shard_map/ppermute | solution.py:298
  82.3 5.4 %shard_map.56.rest_1_ = f32[4,32,4096]{2,1,0:T(8,128)} custom-call(s32[5]{0:T(128)S(1)} %stack.23.ids, f32[32,128]{1,0:T(8,128)S(1)} %fusion.prm_ref, f32[1,128]{1,0:T(1,128)S(1)} %convert_element_type.23.band_ref, bf16[6,1040,128]{2,1,0:T(8,128)(2,1)S(1)} %pad_maximum_fusion.own_ref), custom_call_target="tpu_custom_call" | custom-call | flops 503316480 | bytes 25165824 | tf_op jit(solution)/shard_map/pallas_call | solution.py:208
  87.7 0.0 collective-permute-done.3.rest_0_
  87.7 6.0 %shard_map.57 = f32[4,32,4096]{2,1,0:T(8,128)} custom-call(s32[5]{0:T(128)S(1)} %stack.23.ids, f32[32,128]{1,0:T(8,128)S(1)} %fusion.prm_ref, f32[1,128]{1,0:T(1,128)S(1)} %convert_element_type.23.band_ref, bf16[6,1040,128]{2,1,0:T(8,128)(2,1)S(1)} %pad_maximum_fusion.own_ref, ...), custom_call_target="tpu_custom_call", output_to_operand_aliasing={{}: (5, {})} | custom-call | flops 566231040 | bytes 25165824 | tf_op jit(solution)/shard_map/pallas_call | solution.py:208
  (8 shorter events, 0.1 us)
Async XLA Ops:
  1.8 30.5 %all-to-all-start = ((bf16[32,40,128]{2,1,0:T(8,128)(2,1)}), bf16[32,40,128]{2,1,0:T(8,128)(2,1)S(1)}, u32[]{:S(2)}, u32[]{:S(2)}) async-start(bf16[32,40,128]{2,1,0:T(8,128)(2,1)} %shard_map.55), calls=%async_computation | async-start | bytes 655360 | tf_op jit(solution)/shard_map/all_to_all | solution.py:264
  49.6 16.7 %all-to-all-start.2 = ((bf16[4,1040,128]{2,1,0:T(8,128)(2,1)}), bf16[4,1040,128]{2,1,0:T(8,128)(2,1)S(1)}, u32[]{:S(2)}, u32[]{:S(2)}) async-start(bf16[4,1040,128]{2,1,0:T(8,128)(2,1)} %broadcast_in_dim.9), calls=%async_computation.2 | async-start | bytes 2129920 | tf_op jit(solution)/shard_map/all_to_all | solution.py:283
  53.2 7.6 %collective-permute-start = (bf16[1040,128]{1,0:T(8,128)(2,1)S(1)}, bf16[1040,128]{1,0:T(8,128)(2,1)S(1)}, u32[]{:S(2)}, u32[]{:S(2)}) collective-permute-start(bf16[1040,128]{1,0:T(8,128)(2,1)S(1)} %pad_maximum_fusion.1), channel_id=1, source_target_pairs={{2,0},{4,2},{6,4},{8,6},{10,8},{12,10},{14,12},{16,14},{18,16},{20... | collective-permute-start | bytes 798728 | tf_op jit(solution)/shard_map/ppermute | solution.py:282
  66.3 4.6 %collective-permute-start.1 = (bf16[1040,128]{1,0:T(8,128)(2,1)S(1)}, bf16[1040,128]{1,0:T(8,128)(2,1)S(1)}, u32[]{:S(2)}, u32[]{:S(2)}) collective-permute-start(bf16[1040,128]{1,0:T(8,128)(2,1)S(1)} %dynamic-slice_bitcast_fusion), channel_id=1, source_target_pairs={{0,2},{2,4},{4,6},{6,8},{8,10},{10,12},{12,14},{14,16},{16,18},{18... | collective-permute-start | bytes 798728 | tf_op jit(solution)/shard_map/ppermute | solution.py:293
  67.6 8.4 %collective-permute-start.2 = (bf16[1040,128]{1,0:T(8,128)(2,1)S(1)}, bf16[1040,128]{1,0:T(8,128)(2,1)S(1)}, u32[]{:S(2)}, u32[]{:S(2)}) collective-permute-start(bf16[1040,128]{1,0:T(8,128)(2,1)S(1)} %collective-permute-done), channel_id=1, source_target_pairs={{0,65},{1,64},{64,1},{65,0},{2,67},{3,66},{66,3},{67,2},{4,69},{5,... | collective-permute-start | bytes 798728 | tf_op jit(solution)/shard_map/ppermute | solution.py:294
  76.2 11.5 %collective-permute-start.3 = (bf16[6,1040,128]{2,1,0:T(8,128)(2,1)S(1)}, bf16[6,1040,128]{2,1,0:T(8,128)(2,1)S(1)}, u32[]{:S(2)}, u32[]{:S(2)}) collective-permute-start(bf16[6,1040,128]{2,1,0:T(8,128)(2,1)S(1)} %pad_maximum_fusion.own_ref), channel_id=1, source_target_pairs={{0,32},{32,0},{1,33},{33,1},{2,34},{34,2},{3,35},{35,3},{4,36},{36... | collective-permute-start | bytes 4792328 | tf_op jit(solution)/shard_map/ppermute | solution.py:298

commit v7 on v5

--- a/solution.py
+++ b/solution.py
@@ -267,28 +267,32 @@
     views = jnp.concatenate(
         [lax.dynamic_index_in_dim(got, owner[v], keepdims=False) for v in range(VIEWS)]
     )
-    lower = lax.ppermute(numbers, DEPTH, [(i, (i + 1) % 32) for i in range(32)])
-    upper = lax.ppermute(numbers, DEPTH, [((i + 1) % 32, i) for i in range(32)])
-    prm = jnp.concatenate([lower[:1], numbers[:1], upper[:1]]).astype(F32)
 
     band = band_start.astype(BF16).reshape(1, SIZE)
-    rest = (band.astype(F32), jnp.pad(band, ((0, 15), (0, 0))), prm, ids)
-    views, (band, band_rows, prm, ids) = lax.optimization_barrier((views, rest))
+    rest = (band.astype(F32), jnp.pad(band, ((0, 15), (0, 0))), ids, numbers)
+    views, (band, band_rows, ids, numbers) = lax.optimization_barrier((views, rest))
     near = lax.all_to_all(jnp.broadcast_to(views[None], (8, SIZE, LANES)), "y", 0, 0, tiled=True)
     near = jnp.concatenate([near.reshape(8 * SIZE, LANES), band_rows])
 
-    swap = [(0, 1), (1, 0)]
-    shift = [(2 * i, (2 * i - 2) % 32) for i in range(16)]
-    shift += [(2 * i + 1, (2 * i + 3) % 32) for i in range(16)]
+    shift = [(2 * i + 2, 2 * i) for i in range(15)] + [(2 * i + 1, 2 * i + 3) for i in range(15)]
     foreign = lax.ppermute(near, ("z", "xh"), shift)
     own = lax.all_to_all(
         jnp.broadcast_to(near[None], (4,) + near.shape), ("xh", "xl"), 0, 0, tiled=True
     )
 
+    lower = lax.ppermute(numbers, DEPTH, [(i, i + 1) for i in range(31)])
+    upper = lax.ppermute(numbers, DEPTH, [(i + 1, i) for i in range(31)])
+    own, foreign, lower, upper = lax.optimization_barrier((own, foreign, lower, upper))
+    prm = jnp.concatenate([lower[:1], numbers[:1], upper[:1]]).astype(F32)
+
+    along = [(a, b) for b, a in shift]
+    third = lax.dynamic_slice(
+        own, (2 * (1 - xh) + xl, 0, 0), (1,) + near.shape, allow_negative_indices=False
+    )[0]
+    third = lax.ppermute(third, ("z", "xh"), along)
     third_far = lax.ppermute(foreign, ("xl", "xh"), [(0, 3), (1, 2), (2, 1), (3, 0)])
-    third = lax.ppermute(third_far, "xl", swap)
-    own, third = lax.optimization_barrier((own, third))
-
+
+    swap = [(0, 1), (1, 0)]
     own = jnp.concatenate([own, third[None], third_far[None]])
     other = lax.ppermute(own, "core", swap)
     first = smooth(False, ids, prm, band, own)

time: 114 us -> 93.6 us (0.82)
  starting transfers between devices: 47.7 us -> 37.6 us
  waiting for transfers between devices: 21.5 us -> 14.4 us
  blocking collectives: 18.8 us -> 16.2 us
    ppermute x1, waiting for transfers between devices: 14.6 us -> 5.05 us  [shards(): lax.ppermute(foreign, ('xl', 'xh'), [(0, 3), (1, 2), (2, 1), (3, 0)])]
    ppermute x1, starting transfers between devices: 9.86 us -> 1.29 us  [shards(): foreign = lax.ppermute(near, ('z', 'xh'), shift)]
    ppermute x1, starting transfers between devices: 4.71 us -> 2 us  [shards(): lax.ppermute(foreign, ('xl', 'xh'), [(0, 3), (1, 2), (2, 1), (3, 0)])]
    all_to_all x1, blocking collectives: 18.8 us -> 16.2 us  [shards(): lax.all_to_all(jnp.broadcast_to(views[None], (8, SIZE, LANES)), 'y', 0, 0...]
    ppermute x3, waiting for transfers between devices: 6.25 us -> 7.91 us  [the longest x1 5.9 us: shards(): upper = lax.ppermute(numbers, DEPTH, [(i + 1, i) for i in range(31)])]
    all_to_all x1, waiting for transfers between devices: 0.01 us -> 1.42 us  [shards(): got = lax.all_to_all(pieces, DEPTH, 0, 0, tiled=True)]
  transfers between devices with their start and end apart: 8 -> 8, of which waited for: 3 -> 4; matrix products, arithmetic and copies ran while one was open for 4% -> 3% of each run, Pallas kernels for 5% -> 6%
where the time goes in v7:
time: 93.6 us; the launch traced here: 93 us
  starting transfers between devices  37.6 us (40%)
  blocking collectives  16.2 us (17%)
  waiting for transfers between devices  14.4 us (15%)
  Pallas kernels  13.1 us (14%)
  between operations  7.87 us (8%)
  local copies, waits for them, and re-layouts  2.84 us (3%)
    all_to_all x1, starting transfers between devices, shards(): got = lax.all_to_all(pieces, DEPTH, 0, 0, tiled=True)  17.7 us
    all_to_all x1, blocking collectives, shards(): lax.all_to_all(jnp.broadcast_to(views[None], (8, SIZE, LANES)), 'y', 0, 0...  16.2 us
    pallas_call x2, Pallas kernels, smooth(): pl.pallas_call(functools.partial(half, second), out_shape=jax.ShapeDtypeS...  11.4 us
    ppermute x1, waiting for transfers between devices, shards(): upper = lax.ppermute(numbers, DEPTH, [(i + 1, i) for i in range(31)])  5.9 us
    ppermute x1, waiting for transfers between devices, shards(): lax.ppermute(foreign, ('xl', 'xh'), [(0, 3), (1, 2), (2, 1), (3, 0)])  5.05 us
    ppermute x1, starting transfers between devices, shards(): other = lax.ppermute(own, 'core', swap)  4.76 us
    ppermute x1, starting transfers between devices, shards(): upper = lax.ppermute(numbers, DEPTH, [(i + 1, i) for i in range(31)])  3.6 us
    all_to_all x1, starting transfers between devices, shards(): lax.all_to_all(jnp.broadcast_to(near[None], (4,) + near.shape), ('xh', 'x...  3.52 us
  transfers between devices with their start and end apart: 8, of which 4 were waited for; matrix products, arithmetic and copies ran while one was open for 3% of the time, Pallas kernels for 6%

profile of v7, /device:TPU:1, one launch (start us, length us, event | category | flops | bytes accessed | tf_op | source)
XLA Modules:
  0.0 93.0 jit_solution(12813183532345845230)
XLA Ops:
  0.0 1.7 %shard_map.55 = (bf16[32,32,128]{2,1,0:T(8,128)(2,1)}, bf16[16,128]{1,0:T(8,128)(2,1)}) custom-call(bf16[32,4096]{1,0:T(8,128)(2,1)} %bitcast.26, s32[4,4]{1,0:T(4,128)} %offset_ref.1, bf16[4,4,4]{2,1,0:T(4,128)(2,1)} %taps_ref.1), custom_call_target="tpu_custom_call" | custom-call | tf_op jit(solution)/shard_map/pallas_call | solution.py:257
  1.7 17.7 %all-to-all-start = ((bf16[32,32,128]{2,1,0:T(8,128)(2,1)}), bf16[32,32,128]{2,1,0:T(8,128)(2,1)S(1)}, u32[]{:S(2)}, u32[]{:S(2)}) async-start(bf16[32,32,128]{2,1,0:T(8,128)(2,1)} %get-tuple-element.16), calls=%async_computation | async-start | bytes 524288 | tf_op jit(solution)/shard_map/all_to_all | solution.py:266
  19.4 1.5 %fusion = (s32[1]{0:T(128)}, s32[1]{0:T(128)}, s32[1]{0:T(128)}, s32[1]{0:T(128)}) fusion(s32[4]{0:T(128)} %param.6), kind=kLoop, calls=%fused_computation.9 | loop fusion | bytes 32 | tf_op jit(solution)/shard_map/slice | solution.py:268
  26.0 0.7 convert_element_type.19
  26.7 0.1 reshape.20
  29.4 0.1 stack.23.ids
  29.5 1.4 %all-to-all-done = bf16[32,32,128]{2,1,0:T(8,128)(2,1)S(1)} async-done(((bf16[32,32,128]{2,1,0:T(8,128)(2,1)}), bf16[32,32,128]{2,1,0:T(8,128)(2,1)S(1)}, u32[]{:S(2)}, u32[]{:S(2)}) %all-to-all-start) | async-done | bytes 262176 | tf_op jit(solution)/shard_map/all_to_all | solution.py:266
  30.9 16.2 %all_to_all.15 = bf16[8,128,128]{2,1,0:T(8,128)(2,1)S(1)} all-to-all(bf16[8,128,128]{2,1,0:T(8,128)(2,1)S(1)} %broadcast_in_dim.8), channel_id=1, replica_groups=mesh['y'=8,'xl'=2,'core'=2,'z'=16,'xh'=2] {'y'}, dimensions={0} | all-to-all | bytes 524288 | tf_op jit(solution)/shard_map/all_to_all | solution.py:274
  47.1 0.0 copy-start
  47.2 1.1 %broadcast_in_dim.9 = bf16[4,1040,128]{2,1,0:T(8,128)(2,1)} broadcast(bf16[1040,128]{1,0:T(8,128)(2,1)S(1)} %pad_maximum_fusion.1), dimensions={1,2} | broadcast | bytes 1331200 | tf_op jit(solution)/shard_map/broadcast_in_dim | solution.py:280
  48.3 3.5 %all-to-all-start.2 = ((bf16[4,1040,128]{2,1,0:T(8,128)(2,1)}), bf16[4,1040,128]{2,1,0:T(8,128)(2,1)S(1)}, u32[]{:S(2)}, u32[]{:S(2)}) async-start(bf16[4,1040,128]{2,1,0:T(8,128)(2,1)} %broadcast_in_dim.9), calls=%async_computation.2 | async-start | bytes 2129920 | tf_op jit(solution)/shard_map/all_to_all | solution.py:279
  51.8 1.3 %collective-permute-start = (bf16[1040,128]{1,0:T(8,128)(2,1)S(1)}, bf16[1040,128]{1,0:T(8,128)(2,1)S(1)}, u32[]{:S(2)}, u32[]{:S(2)}) collective-permute-start(bf16[1040,128]{1,0:T(8,128)(2,1)S(1)} %pad_maximum_fusion.1), channel_id=1, source_target_pairs={{2,0},{4,2},{6,4},{8,6},{10,8},{12,10},{14,12},{16,14},{18,16},{20... | collective-permute-start | bytes 798728 | tf_op jit(solution)/shard_map/ppermute | solution.py:278
  53.1 0.0 copy-done
  53.1 3.6 %collective-permute-start.2 = (bf16[16,128]{1,0:T(8,128)(2,1)S(1)}, bf16[16,128]{1,0:T(8,128)(2,1)S(1)}, u32[]{:S(2)}, u32[]{:S(2)}) collective-permute-start(bf16[16,128]{1,0:T(8,128)(2,1)S(1)} %copy-done), channel_id=1, source_target_pairs={{32,0},{64,32},{96,64},{128,96},{160,128},{192,160},{224,192},{256... | collective-permute-start | bytes 12296 | tf_op jit(solution)/shard_map/ppermute | solution.py:284
  56.7 3.5 %collective-permute-start.1 = (bf16[16,128]{1,0:T(8,128)(2,1)S(1)}, bf16[16,128]{1,0:T(8,128)(2,1)S(1)}, u32[]{:S(2)}, u32[]{:S(2)}) collective-permute-start(bf16[16,128]{1,0:T(8,128)(2,1)S(1)} %copy-done), channel_id=1, source_target_pairs={{0,32},{32,64},{64,96},{96,128},{128,160},{160,192},{192,224},{224... | collective-permute-start | bytes 12296 | tf_op jit(solution)/shard_map/ppermute | solution.py:283
  60.2 5.9 %collective-permute-done.2 = bf16[16,128]{1,0:T(8,128)(2,1)S(1)} collective-permute-done((bf16[16,128]{1,0:T(8,128)(2,1)S(1)}, bf16[16,128]{1,0:T(8,128)(2,1)S(1)}, u32[]{:S(2)}, u32[]{:S(2)}) %collective-permute-start.2) | collective-permute-done | bytes 4128 | tf_op jit(solution)/shard_map/ppermute | solution.py:284
  66.1 0.0 collective-permute-done.1
  66.1 0.0 collective-permute-done
  66.1 0.0 all-to-all-done.2
  66.2 1.3 %collective-permute-start.3 = (bf16[1040,128]{1,0:T(8,128)(2,1)S(1)}, bf16[1040,128]{1,0:T(8,128)(2,1)S(1)}, u32[]{:S(2)}, u32[]{:S(2)}) collective-permute-start(bf16[1040,128]{1,0:T(8,128)(2,1)S(1)} %dynamic-slice_bitcast_fusion), channel_id=1, source_target_pairs={{0,2},{2,4},{4,6},{6,8},{8,10},{10,12},{12,14},{14,16},{16,18},{18... | collective-permute-start | bytes 798728 | tf_op jit(solution)/shard_map/ppermute | solution.py:292
  67.5 2.0 %collective-permute-start.4 = (bf16[1040,128]{1,0:T(8,128)(2,1)S(1)}, bf16[1040,128]{1,0:T(8,128)(2,1)S(1)}, u32[]{:S(2)}, u32[]{:S(2)}) collective-permute-start(bf16[1040,128]{1,0:T(8,128)(2,1)S(1)} %collective-permute-done), channel_id=1, source_target_pairs={{0,65},{1,64},{64,1},{65,0},{2,67},{3,66},{66,3},{67,2},{4,69},{5,... | collective-permute-start | bytes 798728 | tf_op jit(solution)/shard_map/ppermute | solution.py:293
  69.5 2.0 %collective-permute-done.3 = bf16[1040,128]{1,0:T(8,128)(2,1)S(1)} collective-permute-done((bf16[1040,128]{1,0:T(8,128)(2,1)S(1)}, bf16[1040,128]{1,0:T(8,128)(2,1)S(1)}, u32[]{:S(2)}, u32[]{:S(2)}) %collective-permute-start.3) | collective-permute-done | bytes 266272 | tf_op jit(solution)/shard_map/ppermute | solution.py:292
  71.5 5.1 %collective-permute-done.4 = bf16[1040,128]{1,0:T(8,128)(2,1)S(1)} collective-permute-done((bf16[1040,128]{1,0:T(8,128)(2,1)S(1)}, bf16[1040,128]{1,0:T(8,128)(2,1)S(1)}, u32[]{:S(2)}, u32[]{:S(2)}) %collective-permute-start.4) | collective-permute-done | bytes 266272 | tf_op jit(solution)/shard_map/ppermute | solution.py:293
  76.6 0.2 pad_maximum_fusion.own_ref
  76.8 4.8 %collective-permute-start.5 = (bf16[6,1040,128]{2,1,0:T(8,128)(2,1)S(1)}, bf16[6,1040,128]{2,1,0:T(8,128)(2,1)S(1)}, u32[]{:S(2)}, u32[]{:S(2)}) collective-permute-start(bf16[6,1040,128]{2,1,0:T(8,128)(2,1)S(1)} %pad_maximum_fusion.own_ref), channel_id=1, source_target_pairs={{0,32},{32,0},{1,33},{33,1},{2,34},{34,2},{3,35},{35,3},{4,36},{36... | collective-permute-start | bytes 4792328 | tf_op jit(solution)/shard_map/ppermute | solution.py:297
  81.6 5.4 %shard_map.56.rest_1_ = f32[4,32,4096]{2,1,0:T(8,128)} custom-call(s32[5]{0:T(128)S(1)} %stack.23.ids, f32[3,128]{1,0:T(4,128)S(1)} %maximum_convert_fusion.prm_ref, f32[1,128]{1,0:T(1,128)S(1)} %convert_element_type.20.band_ref, bf16[6,1040,128]{2,1,0:T(8,128)(2,1)S(1)} %pad_maximum_fusion.own_ref), custom_call_target="tpu_custom_call" | custom-call | flops 503316480 | bytes 25165824 | tf_op jit(solution)/shard_map/pallas_call | solution.py:208
  87.0 0.0 collective-permute-done.5.rest_0_
  87.0 6.0 %shard_map.57 = f32[4,32,4096]{2,1,0:T(8,128)} custom-call(s32[5]{0:T(128)S(1)} %stack.23.ids, f32[3,128]{1,0:T(4,128)S(1)} %maximum_convert_fusion.prm_ref, f32[1,128]{1,0:T(1,128)S(1)} %convert_element_type.20.band_ref, bf16[6,1040,128]{2,1,0:T(8,128)(2,1)S(1)} %pad_maximum_fusion.own_ref, ...), custom_call_target="tpu_custom_call", output_to_operand_aliasing={{}: (5, {})} | custom-call | flops 566231040 | bytes 25165824 | tf_op jit(solution)/shard_map/pallas_call | solution.py:208
  (11 shorter events, 0.1 us)
Async XLA Ops:
  1.7 29.2 %all-to-all-start = ((bf16[32,32,128]{2,1,0:T(8,128)(2,1)}), bf16[32,32,128]{2,1,0:T(8,128)(2,1)S(1)}, u32[]{:S(2)}, u32[]{:S(2)}) async-start(bf16[32,32,128]{2,1,0:T(8,128)(2,1)} %get-tuple-element.16), calls=%async_computation | async-start | bytes 524288 | tf_op jit(solution)/shard_map/all_to_all | solution.py:266
  47.1 6.0 %copy-start = (bf16[16,128]{1,0:T(8,128)(2,1)S(1)}, bf16[16,128]{1,0:T(8,128)(2,1)}, u32[]{:S(2)}) copy-start(bf16[16,128]{1,0:T(8,128)(2,1)} %get-tuple-element.21) | copy-start | bytes 12292
  48.3 17.9 %all-to-all-start.2 = ((bf16[4,1040,128]{2,1,0:T(8,128)(2,1)}), bf16[4,1040,128]{2,1,0:T(8,128)(2,1)S(1)}, u32[]{:S(2)}, u32[]{:S(2)}) async-start(bf16[4,1040,128]{2,1,0:T(8,128)(2,1)} %broadcast_in_dim.9), calls=%async_computation.2 | async-start | bytes 2129920 | tf_op jit(solution)/shard_map/all_to_all | solution.py:279
  51.8 14.3 %collective-permute-start = (bf16[1040,128]{1,0:T(8,128)(2,1)S(1)}, bf16[1040,128]{1,0:T(8,128)(2,1)S(1)}, u32[]{:S(2)}, u32[]{:S(2)}) collective-permute-start(bf16[1040,128]{1,0:T(8,128)(2,1)S(1)} %pad_maximum_fusion.1), channel_id=1, source_target_pairs={{2,0},{4,2},{6,4},{8,6},{10,8},{12,10},{14,12},{16,14},{18,16},{20... | collective-permute-start | bytes 798728 | tf_op jit(solution)/shard_map/ppermute | solution.py:278
  53.1 13.0 %collective-permute-start.2 = (bf16[16,128]{1,0:T(8,128)(2,1)S(1)}, bf16[16,128]{1,0:T(8,128)(2,1)S(1)}, u32[]{:S(2)}, u32[]{:S(2)}) collective-permute-start(bf16[16,128]{1,0:T(8,128)(2,1)S(1)} %copy-done), channel_id=1, source_target_pairs={{32,0},{64,32},{96,64},{128,96},{160,128},{192,160},{224,192},{256... | collective-permute-start | bytes 12296 | tf_op jit(solution)/shard_map/ppermute | solution.py:284
  56.7 9.4 %collective-permute-start.1 = (bf16[16,128]{1,0:T(8,128)(2,1)S(1)}, bf16[16,128]{1,0:T(8,128)(2,1)S(1)}, u32[]{:S(2)}, u32[]{:S(2)}) collective-permute-start(bf16[16,128]{1,0:T(8,128)(2,1)S(1)} %copy-done), channel_id=1, source_target_pairs={{0,32},{32,64},{64,96},{96,128},{128,160},{160,192},{192,224},{224... | collective-permute-start | bytes 12296 | tf_op jit(solution)/shard_map/ppermute | solution.py:283
  66.2 5.3 %collective-permute-start.3 = (bf16[1040,128]{1,0:T(8,128)(2,1)S(1)}, bf16[1040,128]{1,0:T(8,128)(2,1)S(1)}, u32[]{:S(2)}, u32[]{:S(2)}) collective-permute-start(bf16[1040,128]{1,0:T(8,128)(2,1)S(1)} %dynamic-slice_bitcast_fusion), channel_id=1, source_target_pairs={{0,2},{2,4},{4,6},{6,8},{8,10},{10,12},{12,14},{14,16},{16,18},{18... | collective-permute-start | bytes 798728 | tf_op jit(solution)/shard_map/ppermute | solution.py:292
  67.5 9.1 %collective-permute-start.4 = (bf16[1040,128]{1,0:T(8,128)(2,1)S(1)}, bf16[1040,128]{1,0:T(8,128)(2,1)S(1)}, u32[]{:S(2)}, u32[]{:S(2)}) collective-permute-start(bf16[1040,128]{1,0:T(8,128)(2,1)S(1)} %collective-permute-done), channel_id=1, source_target_pairs={{0,65},{1,64},{64,1},{65,0},{2,67},{3,66},{66,3},{67,2},{4,69},{5,... | collective-permute-start | bytes 798728 | tf_op jit(solution)/shard_map/ppermute | solution.py:293
  76.8 10.2 %collective-permute-start.5 = (bf16[6,1040,128]{2,1,0:T(8,128)(2,1)S(1)}, bf16[6,1040,128]{2,1,0:T(8,128)(2,1)S(1)}, u32[]{:S(2)}, u32[]{:S(2)}) collective-permute-start(bf16[6,1040,128]{2,1,0:T(8,128)(2,1)S(1)} %pad_maximum_fusion.own_ref), channel_id=1, source_target_pairs={{0,32},{32,0},{1,33},{33,1},{2,34},{34,2},{3,35},{35,3},{4,36},{36... | collective-permute-start | bytes 4792328 | tf_op jit(solution)/shard_map/ppermute | solution.py:297

commit v8 on v4

--- a/solution.py
+++ b/solution.py
@@ -139,23 +139,21 @@
         other_ref, _, out_ref, weights, v0, v1, flow, done, sems = rest
     else:
         out_ref, weights, v0, v1, flow, done, sems = rest
-    xh, core, xl = ids[2], ids[3], ids[4]
+    core, xl = ids[3], ids[4]
     tiles = TILES + 2 if second else TILES
 
     def band(ref):
         return ref[8 * SIZE :, :].astype(F32)[:1, :]
 
-    pair_band = band(own_ref.at[2 * (1 - xh)])
-    weights[...] = interpolation(ids, prm_ref, band_ref[...], pair_band, band(own_ref.at[4]))
+    pair_band = band(own_ref.at[3])
+    weights[...] = interpolation(ids, prm_ref, band_ref[...], pair_band, band(own_ref.at[5]))
 
     def project(pieces, x, y, count, first):
         columns = []
         for i in range(count):
             at = pl.ds(pl.multiple_of((y + i) * SIZE, SIZE), SIZE)
-            near = pieces[2 * xh + x, at, :]
-            pair = pieces[2 * (1 - xh) + x, at, :]
-            third = pieces[4 + (x ^ xl), at, :]
-            columns.append(jnp.concatenate([near, pair, third], axis=0))
+            from_tiles = [pieces[2 * n + (x ^ xl), at, :] for n in range(3)]
+            columns.append(jnp.concatenate(from_tiles, axis=0))
         found = jnp.dot(
             weights[...], jnp.concatenate(columns, axis=1), preferred_element_type=F32
         )
@@ -273,22 +271,22 @@
     near = lax.all_to_all(jnp.broadcast_to(views[None], (8, SIZE, LANES)), "y", 0, 0, tiled=True)
     near = jnp.concatenate([near.reshape(8 * SIZE, LANES), band_rows])
 
-    shift = [(2 * i, (2 * i - 2) % 32) for i in range(16)]
-    shift += [(2 * i + 1, (2 * i + 3) % 32) for i in range(16)]
-    foreign = lax.ppermute(near, ("z", "xh"), shift)
-    own = lax.all_to_all(
-        jnp.broadcast_to(near[None], (4,) + near.shape), ("xh", "xl"), 0, 0, tiled=True
-    )
-
-    own, foreign = lax.optimization_barrier((own, foreign))
-
-    along = [(a, b) for b, a in shift]
-    third = lax.dynamic_index_in_dim(own, 2 * (1 - xh) + xl, keepdims=False)
-    third = lax.ppermute(third, ("z", "xh"), along)
-    third_far = lax.ppermute(foreign, ("xl", "xh"), [(0, 3), (1, 2), (2, 1), (3, 0)])
-
     swap = [(0, 1), (1, 0)]
-    own = jnp.concatenate([own, third[None], third_far[None]])
+    across = [(0, 3), (1, 2), (2, 1), (3, 0)]
+    pair_far = lax.ppermute(near, ("xl", "xh"), across)
+    on = [((x * 16 + i + 1) * 2, ((1 - x) * 16 + i) * 2) for i in range(15) for x in range(2)]
+    on += [(a + 1 - 2, b + 1 + 2) for a, b in on]
+    foreign = lax.ppermute(near, ("xl", "z", "xh"), on)
+    near_far = lax.ppermute(near, "xl", swap)
+
+    along = [(2 * i, 2 * i + 2) for i in range(15)] + [(2 * i + 3, 2 * i + 1) for i in range(15)]
+    third_far = lax.ppermute(pair_far, ("z", "xh"), along)
+    third = lax.ppermute(foreign, ("xl", "xh"), across)
+    upper = lax.ppermute(near_far[: 4 * SIZE], ("xl", "xh"), across)
+    lower = lax.ppermute(pair_far[4 * SIZE :], "xl", swap)
+
+    pair = jnp.concatenate([upper, lower])
+    own = jnp.stack([near, near_far, pair, pair_far, third, third_far])
     other = lax.ppermute(own, "core", swap)
     first = smooth(False, ids, prm, band, own)
     return smooth(True, ids, prm, band, own, other, first)

time: 99.7 us -> 93.9 us (0.942)
  starting transfers between devices: 49.3 us -> 44.2 us
    ppermute x3 -> x7, starting transfers between devices: 22.5 us -> 16 us  [the longest x1 3.43 us: shards(): third = lax.ppermute(foreign, ('xl', 'xh'), across)]
    ppermute x1, starting transfers between devices: 5.66 us -> 10.5 us  [shards(): other = lax.ppermute(own, 'core', swap)]
    all_to_all x1 -> x0, starting transfers between devices: 3.52 us -> none  [shards(): lax.all_to_all(jnp.broadcast_to(near[None], (4,) + near.shape), ('xh', 'x...]
    broadcast_in_dim x1 -> x0, local copies, waits for them, and re-layouts: 1.11 us -> none  [shards(): jnp.broadcast_to(near[None], (4,) + near.shape)]
    ppermute x3 -> x7, waiting for transfers between devices: 7.77 us -> 7.74 us  [the longest x1 4.63 us: shards(): third = lax.ppermute(foreign, ('xl', 'xh'), across)]
  transfers between devices with their start and end apart: 6 -> 9, of which waited for: 4 -> 4; matrix products, arithmetic and copies ran while one was open for 2% -> 3% of each run, Pallas kernels for 5% -> 6%
where the time goes in v8:
time: 93.9 us; the launch traced here: 93.3 us
  starting transfers between devices  44.2 us (47%)
  blocking collectives  14.9 us (16%)
  Pallas kernels  13.2 us (14%)
  waiting for transfers between devices  10.5 us (11%)
  between operations  7.92 us (8%)
  local copies, waits for them, and re-layouts  1.88 us (2%)
    all_to_all x1, starting transfers between devices, shards(): got = lax.all_to_all(pieces, DEPTH, 0, 0, tiled=True)  17.7 us
    all_to_all x1, blocking collectives, shards(): lax.all_to_all(jnp.broadcast_to(views[None], (8, SIZE, LANES)), 'y', 0, 0...  14.9 us
    pallas_call x2, Pallas kernels, smooth(): pl.pallas_call(functools.partial(half, second), out_shape=jax.ShapeDtypeS...  11.4 us
    ppermute x1, starting transfers between devices, shards(): other = lax.ppermute(own, 'core', swap)  10.5 us
    ppermute x1, waiting for transfers between devices, shards(): third = lax.ppermute(foreign, ('xl', 'xh'), across)  4.63 us
    ppermute x1, starting transfers between devices, shards(): third = lax.ppermute(foreign, ('xl', 'xh'), across)  3.43 us
    ppermute x1, starting transfers between devices, shards(): near_far = lax.ppermute(near, 'xl', swap)  3.1 us
    ppermute x1, starting transfers between devices, shards(): upper = lax.ppermute(near_far[:4 * SIZE], ('xl', 'xh'), across)  3.05 us
  transfers between devices with their start and end apart: 9, of which 4 were waited for; matrix products, arithmetic and copies ran while one was open for 3% of the time, Pallas kernels for 6%

profile of v8, /device:TPU:1, one launch (start us, length us, event | category | flops | bytes accessed | tf_op | source)
XLA Modules:
  0.0 93.3 jit_solution(3032495652400920535)
XLA Ops:
  0.0 1.8 %shard_map.55 = bf16[32,40,128]{2,1,0:T(8,128)(2,1)} custom-call(bf16[32,4096]{1,0:T(8,128)(2,1)} %bitcast.40, s32[4,4]{1,0:T(4,128)} %offset_ref.1, bf16[4,4,4]{2,1,0:T(4,128)(2,1)} %taps_ref.1), custom_call_target="tpu_custom_call" | custom-call | tf_op jit(solution)/shard_map/pallas_call | solution.py:256
  1.8 17.7 %all-to-all-start = ((bf16[32,40,128]{2,1,0:T(8,128)(2,1)}), bf16[32,40,128]{2,1,0:T(8,128)(2,1)S(1)}, u32[]{:S(2)}, u32[]{:S(2)}) async-start(bf16[32,40,128]{2,1,0:T(8,128)(2,1)} %shard_map.55), calls=%async_computation | async-start | bytes 655360 | tf_op jit(solution)/shard_map/all_to_all | solution.py:262
  19.5 1.5 %fusion.2 = (s32[1]{0:T(128)}, s32[1]{0:T(128)}, s32[1]{0:T(128)}, s32[1]{0:T(128)}) fusion(s32[4]{0:T(128)} %param.6), kind=kLoop, calls=%fused_computation.15 | loop fusion | bytes 32 | tf_op jit(solution)/shard_map/slice | solution.py:265
  26.1 0.7 convert_element_type.22
  26.8 0.1 reshape.25
  29.5 0.1 stack.44.ids
  29.6 2.7 %all-to-all-done = bf16[32,40,128]{2,1,0:T(8,128)(2,1)S(1)} async-done(((bf16[32,40,128]{2,1,0:T(8,128)(2,1)}), bf16[32,40,128]{2,1,0:T(8,128)(2,1)S(1)}, u32[]{:S(2)}, u32[]{:S(2)}) %all-to-all-start) | async-done | bytes 327712 | tf_op jit(solution)/shard_map/all_to_all | solution.py:262
  32.4 14.9 %all_to_all.10 = bf16[8,128,128]{2,1,0:T(8,128)(2,1)S(1)} all-to-all(bf16[8,128,128]{2,1,0:T(8,128)(2,1)S(1)} %broadcast_in_dim.2), channel_id=1, replica_groups=mesh['y'=8,'xl'=2,'core'=2,'z'=16,'xh'=2] {'y'}, dimensions={0} | all-to-all | bytes 524288 | tf_op jit(solution)/shard_map/all_to_all | solution.py:271
  47.3 1.9 %collective-permute-start.2 = (bf16[1040,128]{1,0:T(8,128)(2,1)S(1)}, bf16[1040,128]{1,0:T(8,128)(2,1)S(1)}, u32[]{:S(2)}, u32[]{:S(2)}) collective-permute-start(bf16[1040,128]{1,0:T(8,128)(2,1)S(1)} %pad_maximum_fusion), channel_id=1, source_target_pairs={{0,65},{1,64},{64,1},{65,0},{2,67},{3,66},{66,3},{67,2},{4,69},{5,... | collective-permute-start | bytes 798728 | tf_op jit(solution)/shard_map/ppermute | solution.py:276
  49.2 3.1 %collective-permute-start = (bf16[1040,128]{1,0:T(8,128)(2,1)S(1)}, bf16[1040,128]{1,0:T(8,128)(2,1)S(1)}, u32[]{:S(2)}, u32[]{:S(2)}) collective-permute-start(bf16[1040,128]{1,0:T(8,128)(2,1)S(1)} %pad_maximum_fusion), channel_id=1, source_target_pairs={{0,64},{64,0},{1,65},{65,1},{2,66},{66,2},{3,67},{67,3},{4,68},{68... | collective-permute-start | bytes 798728 | tf_op jit(solution)/shard_map/ppermute | solution.py:280
  52.4 1.3 %collective-permute-start.4 = (bf16[1040,128]{1,0:T(8,128)(2,1)S(1)}, bf16[1040,128]{1,0:T(8,128)(2,1)S(1)}, u32[]{:S(2)}, u32[]{:S(2)}) collective-permute-start(bf16[1040,128]{1,0:T(8,128)(2,1)S(1)} %pad_maximum_fusion), channel_id=1, source_target_pairs={{2,64},{66,0},{4,66},{68,2},{6,68},{70,4},{8,70},{72,6},{10,72},{7... | collective-permute-start | bytes 798728 | tf_op jit(solution)/shard_map/ppermute | solution.py:279
  53.7 2.9 %collective-permute-done.2 = bf16[1040,128]{1,0:T(8,128)(2,1)S(1)} collective-permute-done((bf16[1040,128]{1,0:T(8,128)(2,1)S(1)}, bf16[1040,128]{1,0:T(8,128)(2,1)S(1)}, u32[]{:S(2)}, u32[]{:S(2)}) %collective-permute-start.2) | collective-permute-done | bytes 266272 | tf_op jit(solution)/shard_map/ppermute | solution.py:276
  56.6 1.9 %collective-permute-start.3 = (bf16[528,128]{1,0:T(8,128)(2,1)S(1)}, bf16[528,128]{1,0:T(8,128)(2,1)S(1)}, u32[]{:S(2)}, u32[]{:S(2)}) collective-permute-start(bf16[528,128]{1,0:T(8,128)(2,1)S(1)} %slice.62), channel_id=1, source_target_pairs={{0,64},{64,0},{1,65},{65,1},{2,66},{66,2},{3,67},{67,3},{4,68},{68... | collective-permute-start | bytes 405512 | tf_op jit(solution)/shard_map/ppermute | solution.py:286
  58.6 0.0 collective-permute-done
  58.6 3.1 %collective-permute-start.1 = (bf16[512,128]{1,0:T(8,128)(2,1)S(1)}, bf16[512,128]{1,0:T(8,128)(2,1)S(1)}, u32[]{:S(2)}, u32[]{:S(2)}) collective-permute-start(bf16[512,128]{1,0:T(8,128)(2,1)S(1)} %slice.61), channel_id=1, source_target_pairs={{0,65},{1,64},{64,1},{65,0},{2,67},{3,66},{66,3},{67,2},{4,69},{5,... | collective-permute-start | bytes 393224 | tf_op jit(solution)/shard_map/ppermute | solution.py:285
  61.6 1.3 %collective-permute-start.6 = (bf16[1040,128]{1,0:T(8,128)(2,1)S(1)}, bf16[1040,128]{1,0:T(8,128)(2,1)S(1)}, u32[]{:S(2)}, u32[]{:S(2)}) collective-permute-start(bf16[1040,128]{1,0:T(8,128)(2,1)S(1)} %collective-permute-done.2), channel_id=1, source_target_pairs={{0,2},{2,4},{4,6},{6,8},{8,10},{10,12},{12,14},{14,16},{16,18},{18... | collective-permute-start | bytes 798728 | tf_op jit(solution)/shard_map/ppermute | solution.py:283
  63.0 0.0 collective-permute-done.4
  63.0 3.4 %collective-permute-start.5 = (bf16[1040,128]{1,0:T(8,128)(2,1)S(1)}, bf16[1040,128]{1,0:T(8,128)(2,1)S(1)}, u32[]{:S(2)}, u32[]{:S(2)}) collective-permute-start(bf16[1040,128]{1,0:T(8,128)(2,1)S(1)} %collective-permute-done.4), channel_id=1, source_target_pairs={{0,65},{1,64},{64,1},{65,0},{2,67},{3,66},{66,3},{67,2},{4,69},{5,... | collective-permute-start | bytes 798728 | tf_op jit(solution)/shard_map/ppermute | solution.py:284
  66.4 0.0 collective-permute-done.1
  66.5 0.2 collective-permute-done.3
  66.7 4.6 %collective-permute-done.5 = bf16[1040,128]{1,0:T(8,128)(2,1)S(1)} collective-permute-done((bf16[1040,128]{1,0:T(8,128)(2,1)S(1)}, bf16[1040,128]{1,0:T(8,128)(2,1)S(1)}, u32[]{:S(2)}, u32[]{:S(2)}) %collective-permute-start.5) | collective-permute-done | bytes 266272 | tf_op jit(solution)/shard_map/ppermute | solution.py:284
  71.4 0.0 collective-permute-done.6
  71.4 10.5 %collective-permute-start.7 = (bf16[6,1040,128]{2,1,0:T(8,128)(2,1)S(1)}, bf16[6,1040,128]{2,1,0:T(8,128)(2,1)S(1)}, u32[]{:S(2)}, u32[]{:S(2)}) collective-permute-start(bf16[6,1040,128]{2,1,0:T(8,128)(2,1)S(1)} %bitcast_dynamic-update-slice_fusion.own_ref), channel_id=1, source_target_pairs={{0,32},{32,0},{1,33},{33,1},{2,34},{34,2},{3,35},{35,3},{4,36},{36... | collective-permute-start | bytes 4792328 | tf_op jit(solution)/shard_map/ppermute | solution.py:290
  81.9 5.4 %shard_map.56.rest_1_ = f32[4,32,4096]{2,1,0:T(8,128)} custom-call(s32[5]{0:T(128)S(1)} %stack.44.ids, f32[32,128]{1,0:T(8,128)S(1)} %fusion.1.prm_ref, f32[1,128]{1,0:T(1,128)S(1)} %convert_element_type.23.band_ref, bf16[6,1040,128]{2,1,0:T(8,128)(2,1)S(1)} %bitcast_dynamic-update-slice_fusion.own_ref), custom_call_target="tpu_custom_call" | custom-call | flops 503316480 | bytes 25165824 | tf_op jit(solution)/shard_map/pallas_call | solution.py:206
  87.3 0.0 collective-permute-done.7.rest_0_
  87.3 6.0 %shard_map.57 = f32[4,32,4096]{2,1,0:T(8,128)} custom-call(s32[5]{0:T(128)S(1)} %stack.44.ids, f32[32,128]{1,0:T(8,128)S(1)} %fusion.1.prm_ref, f32[1,128]{1,0:T(1,128)S(1)} %convert_element_type.23.band_ref, bf16[6,1040,128]{2,1,0:T(8,128)(2,1)S(1)} %bitcast_dynamic-update-slice_fusion.own_ref, ...), custom_call_target="tpu_custom_call", output_to_operand_aliasing={{}: (5, {})} | custom-call | flops 566231040 | bytes 25165824 | tf_op jit(solution)/shard_map/pallas_call | solution.py:206
  (16 shorter events, 0.3 us)
Async XLA Ops:
  1.8 30.5 %all-to-all-start = ((bf16[32,40,128]{2,1,0:T(8,128)(2,1)}), bf16[32,40,128]{2,1,0:T(8,128)(2,1)S(1)}, u32[]{:S(2)}, u32[]{:S(2)}) async-start(bf16[32,40,128]{2,1,0:T(8,128)(2,1)} %shard_map.55), calls=%async_computation | async-start | bytes 655360 | tf_op jit(solution)/shard_map/all_to_all | solution.py:262
  47.3 9.3 %collective-permute-start.2 = (bf16[1040,128]{1,0:T(8,128)(2,1)S(1)}, bf16[1040,128]{1,0:T(8,128)(2,1)S(1)}, u32[]{:S(2)}, u32[]{:S(2)}) collective-permute-start(bf16[1040,128]{1,0:T(8,128)(2,1)S(1)} %pad_maximum_fusion), channel_id=1, source_target_pairs={{0,65},{1,64},{64,1},{65,0},{2,67},{3,66},{66,3},{67,2},{4,69},{5,... | collective-permute-start | bytes 798728 | tf_op jit(solution)/shard_map/ppermute | solution.py:276
  49.2 9.3 %collective-permute-start = (bf16[1040,128]{1,0:T(8,128)(2,1)S(1)}, bf16[1040,128]{1,0:T(8,128)(2,1)S(1)}, u32[]{:S(2)}, u32[]{:S(2)}) collective-permute-start(bf16[1040,128]{1,0:T(8,128)(2,1)S(1)} %pad_maximum_fusion), channel_id=1, source_target_pairs={{0,64},{64,0},{1,65},{65,1},{2,66},{66,2},{3,67},{67,3},{4,68},{68... | collective-permute-start | bytes 798728 | tf_op jit(solution)/shard_map/ppermute | solution.py:280
  52.4 10.6 %collective-permute-start.4 = (bf16[1040,128]{1,0:T(8,128)(2,1)S(1)}, bf16[1040,128]{1,0:T(8,128)(2,1)S(1)}, u32[]{:S(2)}, u32[]{:S(2)}) collective-permute-start(bf16[1040,128]{1,0:T(8,128)(2,1)S(1)} %pad_maximum_fusion), channel_id=1, source_target_pairs={{2,64},{66,0},{4,66},{68,2},{6,68},{70,4},{8,70},{72,6},{10,72},{7... | collective-permute-start | bytes 798728 | tf_op jit(solution)/shard_map/ppermute | solution.py:279
  56.6 10.0 %collective-permute-start.3 = (bf16[528,128]{1,0:T(8,128)(2,1)S(1)}, bf16[528,128]{1,0:T(8,128)(2,1)S(1)}, u32[]{:S(2)}, u32[]{:S(2)}) collective-permute-start(bf16[528,128]{1,0:T(8,128)(2,1)S(1)} %slice.62), channel_id=1, source_target_pairs={{0,64},{64,0},{1,65},{65,1},{2,66},{66,2},{3,67},{67,3},{4,68},{68... | collective-permute-start | bytes 405512 | tf_op jit(solution)/shard_map/ppermute | solution.py:286
  58.6 7.9 %collective-permute-start.1 = (bf16[512,128]{1,0:T(8,128)(2,1)S(1)}, bf16[512,128]{1,0:T(8,128)(2,1)S(1)}, u32[]{:S(2)}, u32[]{:S(2)}) collective-permute-start(bf16[512,128]{1,0:T(8,128)(2,1)S(1)} %slice.61), channel_id=1, source_target_pairs={{0,65},{1,64},{64,1},{65,0},{2,67},{3,66},{66,3},{67,2},{4,69},{5,... | collective-permute-start | bytes 393224 | tf_op jit(solution)/shard_map/ppermute | solution.py:285
  61.6 9.7 %collective-permute-start.6 = (bf16[1040,128]{1,0:T(8,128)(2,1)S(1)}, bf16[1040,128]{1,0:T(8,128)(2,1)S(1)}, u32[]{:S(2)}, u32[]{:S(2)}) collective-permute-start(bf16[1040,128]{1,0:T(8,128)(2,1)S(1)} %collective-permute-done.2), channel_id=1, source_target_pairs={{0,2},{2,4},{4,6},{6,8},{8,10},{10,12},{12,14},{14,16},{16,18},{18... | collective-permute-start | bytes 798728 | tf_op jit(solution)/shard_map/ppermute | solution.py:283
  63.0 8.4 %collective-permute-start.5 = (bf16[1040,128]{1,0:T(8,128)(2,1)S(1)}, bf16[1040,128]{1,0:T(8,128)(2,1)S(1)}, u32[]{:S(2)}, u32[]{:S(2)}) collective-permute-start(bf16[1040,128]{1,0:T(8,128)(2,1)S(1)} %collective-permute-done.4), channel_id=1, source_target_pairs={{0,65},{1,64},{64,1},{65,0},{2,67},{3,66},{66,3},{67,2},{4,69},{5,... | collective-permute-start | bytes 798728 | tf_op jit(solution)/shard_map/ppermute | solution.py:284
  71.4 15.9 %collective-permute-start.7 = (bf16[6,1040,128]{2,1,0:T(8,128)(2,1)S(1)}, bf16[6,1040,128]{2,1,0:T(8,128)(2,1)S(1)}, u32[]{:S(2)}, u32[]{:S(2)}) collective-permute-start(bf16[6,1040,128]{2,1,0:T(8,128)(2,1)S(1)} %bitcast_dynamic-update-slice_fusion.own_ref), channel_id=1, source_target_pairs={{0,32},{32,0},{1,33},{33,1},{2,34},{34,2},{3,35},{35,3},{4,36},{36... | collective-permute-start | bytes 4792328 | tf_op jit(solution)/shard_map/ppermute | solution.py:290

commit v9 on v7

--- a/solution.py
+++ b/solution.py
@@ -24,7 +24,8 @@
 ROWS = 40
 DEEP = HERE + 4
 BATCH = 16
-DEPTH = ("y", "xl", "core")
+ALONG_Y = ("ya", "yb")
+DEPTH = ALONG_Y + ("xl", "core")
 
 
 def half_conduct(diff):
@@ -35,9 +36,9 @@
     depth, tile, xh = ids[0], ids[1], ids[2]
     lane = lax.broadcasted_iota(I32, (1, LANES), 1)
     col = lax.broadcasted_iota(I32, (1, SPAN), 1)
-    view_of_col = (col >> 5) & 3
+    row_of_col = ((col >> 5) & 3) * 8 + (col & 7)
     lane_c = lax.broadcasted_iota(I32, (LANES, SPAN), 0)
-    view_c = (lax.broadcasted_iota(I32, (LANES, SPAN), 1) >> 5) & 3
+    view_c = (lax.broadcasted_iota(I32, (LANES, SPAN), 1) >> 3) & 3
 
     row = lax.broadcasted_iota(I32, (ROWS, 1), 0)
     row = tile * TILE + jnp.where(row < 36, row, row - ROWS)
@@ -56,7 +57,7 @@
     third = jnp.where(first_half, tile - 1, tile + 1)
     pair = jnp.where(first_half, tile + 1, tile - 1)
     source = jnp.where(slot == 0, tile, jnp.where(slot == 1, pair, third))
-    col_row = jnp.where((source >= 0) & (source < 32), source * TILE + (col & 31), -100000)
+    col_row = jnp.where((source >= 0) & (source < 32), source * TILE + row_of_col, -100000)
     reach = (col_row - row).astype(F32) - bands
 
     rest = lane - 4 * VIEWS
@@ -148,14 +149,17 @@
     pair_band = band(own_ref.at[2 * (1 - xh)])
     weights[...] = interpolation(ids, prm_ref, band_ref[...], pair_band, band(own_ref.at[4]))
 
-    def project(pieces, x, y, count, first):
+    def project(pieces, start, count, first):
         columns = []
         for i in range(count):
-            at = pl.ds(pl.multiple_of((y + i) * SIZE, SIZE), SIZE)
-            near = pieces[2 * xh + x, at, :]
-            pair = pieces[2 * (1 - xh) + x, at, :]
-            third = pieces[4 + (x ^ xl), at, :]
-            columns.append(jnp.concatenate([near, pair, third], axis=0))
+            tile = start + i
+            yb, x = tile >> 3, (tile >> 2) & 1
+            parts = []
+            for part in (2 * xh + x, 2 * (1 - xh) + x, 4 + (x ^ xl)):
+                for ya in range(4):
+                    at = pl.multiple_of((2 * ya + yb) * SIZE + (tile & 3) * TILE, TILE)
+                    parts.append(pieces[part, pl.ds(at, TILE), :])
+            columns.append(jnp.concatenate(parts, axis=0))
         found = jnp.dot(
             weights[...], jnp.concatenate(columns, axis=1), preferred_element_type=F32
         )
@@ -164,12 +168,12 @@
 
     if second:
         before = (1 - core) * 2
-        project(other_ref, 0, 0, 8, before)
-        project(other_ref, 1, 0, 8, before + 8)
-        project(own_ref, 1 - core, 6 * (1 - core), 2, core * TILES)
+        project(other_ref, 0, 8, before)
+        project(other_ref, 8, 8, before + 8)
+        project(own_ref, 14 * (1 - core), 2, core * TILES)
     else:
-        project(own_ref, 0, 0, 8, 0)
-        project(own_ref, 1, 0, 8, 8)
+        project(own_ref, 0, 8, 0)
+        project(own_ref, 8, 8, 8)
 
     def keep(i, at, value):
         v1[i, :, at] = value
@@ -228,7 +232,7 @@
     )(*operands)
 
 
-def pack(stored_ref, offset_ref, taps_ref, out_ref, numbers_ref):
+def line_up(offset_ref, taps_ref, numbers_ref):
     lane = lax.broadcasted_iota(I32, (1, LANES), 1)
     rest = lane - 4 * VIEWS
     line = lax.broadcasted_iota(I32, (HERE, LANES), 0)
@@ -241,11 +245,6 @@
         mine = (line == ((rest >> 2) & 3)) & (rest >= 0) & ((rest >> 4) == v)
         numbers += jnp.sum(jnp.where(mine, spread, 0.0), axis=0, keepdims=True)
     numbers_ref[...] = jnp.broadcast_to(numbers, (16, LANES)).astype(BF16)
-    for y in range(8):
-        for xl in range(2):
-            for core in range(2):
-                at = ((core * 2 + xl) * 8 + y) * LANES
-                out_ref[(y * 2 + xl) * 2 + core] = stored_ref[:, at : at + LANES]
 
 
 def shards(projections, owner, row_offset, band_start, taps):
@@ -253,25 +252,26 @@
     depth, tile = lax.axis_index(DEPTH), lax.axis_index(("z", "xh"))
     ids = jnp.stack([depth, tile, xh, core, xl]).astype(I32)
 
+    order = ("ya", "core", "yb", "xl")
+    pieces = projections[0].reshape(4, 8, 8, 4, LANES).transpose(0, 2, 3, 1, 4)
+    got = lax.all_to_all(pieces.reshape(32, TILE, LANES), order, 0, 0, tiled=True)
+    place = (owner & 24) + (owner & 1) * 4 + ((owner >> 1) & 3)
+    views = jnp.stack(
+        [lax.dynamic_index_in_dim(got, place[v], keepdims=False) for v in range(VIEWS)]
+    )
+    views = views.reshape(VIEWS, 4, 8, LANES).transpose(1, 0, 2, 3).reshape(SIZE, LANES)
     whole = pl.BlockSpec(memory_space=pltpu.VMEM)
-    pieces, numbers = pl.pallas_call(
-        pack,
-        out_shape=(
-            jax.ShapeDtypeStruct((32, TILE, LANES), BF16),
-            jax.ShapeDtypeStruct((16, LANES), BF16),
-        ),
-        in_specs=[whole] * 3,
-        out_specs=[whole] * 2,
-    )(projections[0], row_offset, taps)
-    got = lax.all_to_all(pieces, DEPTH, 0, 0, tiled=True)
-    views = jnp.concatenate(
-        [lax.dynamic_index_in_dim(got, owner[v], keepdims=False) for v in range(VIEWS)]
-    )
+    numbers = pl.pallas_call(
+        line_up,
+        out_shape=jax.ShapeDtypeStruct((16, LANES), BF16),
+        in_specs=[whole] * 2,
+        out_specs=whole,
+    )(row_offset, taps)
 
     band = band_start.astype(BF16).reshape(1, SIZE)
     rest = (band.astype(F32), jnp.pad(band, ((0, 15), (0, 0))), ids, numbers)
     views, (band, band_rows, ids, numbers) = lax.optimization_barrier((views, rest))
-    near = lax.all_to_all(jnp.broadcast_to(views[None], (8, SIZE, LANES)), "y", 0, 0, tiled=True)
+    near = lax.all_to_all(jnp.broadcast_to(views[None], (8, SIZE, LANES)), ALONG_Y, 0, 0, tiled=True)
     near = jnp.concatenate([near.reshape(8 * SIZE, LANES), band_rows])
 
     shift = [(2 * i + 2, 2 * i) for i in range(15)] + [(2 * i + 1, 2 * i + 3) for i in range(15)]
@@ -300,7 +300,7 @@
 
 
 def solution(mesh):
-    parted = Mesh(mesh.devices.reshape(8, 2, 2, 16, 2), DEPTH + ("z", "xh"))
+    parted = Mesh(mesh.devices.reshape(4, 2, 2, 2, 16, 2), DEPTH + ("z", "xh"))
     rows = ("z", "xh")
     placed = (
         P(DEPTH, rows, None),

time: 93.6 us -> 92.8 us (level)
    all_to_all x1, blocking collectives: 16.2 us -> 17.1 us  [shards(): lax.all_to_all(jnp.broadcast_to(views[None], (8, SIZE, LANES)), ALONG_Y,...]
    all_to_all x1, waiting for transfers between devices: 1.42 us -> 0.48 us  [shards(): lax.all_to_all(pieces.reshape(32, TILE, LANES), order, 0, 0, tiled=True)]
  transfers between devices with their start and end apart: 8 -> 8, of which waited for: 4 -> 4; matrix products, arithmetic and copies ran while one was open for 3% -> 2% of each run, Pallas kernels for 6% -> 7%
where the time goes in v9:
time: 92.8 us; the launch traced here: 92.2 us
  starting transfers between devices  37.7 us (41%)
  blocking collectives  17.1 us (18%)
  waiting for transfers between devices  13.5 us (15%)
  Pallas kernels  12.9 us (14%)
  between operations  7.52 us (8%)
  local copies, waits for them, and re-layouts  2.02 us (2%)
  other arithmetic  1.59 us (2%)
    all_to_all x1, starting transfers between devices, shards(): lax.all_to_all(pieces.reshape(32, TILE, LANES), order, 0, 0, tiled=True)  17.7 us
    all_to_all x1, blocking collectives, shards(): lax.all_to_all(jnp.broadcast_to(views[None], (8, SIZE, LANES)), ALONG_Y,...  17.1 us
    pallas_call x2, Pallas kernels, smooth(): pl.pallas_call(functools.partial(half, second), out_shape=jax.ShapeDtypeS...  11.4 us
    ppermute x1, waiting for transfers between devices, shards(): upper = lax.ppermute(numbers, DEPTH, [(i + 1, i) for i in range(31)])  5.92 us
    ppermute x1, waiting for transfers between devices, shards(): lax.ppermute(foreign, ('xl', 'xh'), [(0, 3), (1, 2), (2, 1), (3, 0)])  5.05 us
    ppermute x1, starting transfers between devices, shards(): other = lax.ppermute(own, 'core', swap)  4.76 us
    ppermute x1, starting transfers between devices, shards(): upper = lax.ppermute(numbers, DEPTH, [(i + 1, i) for i in range(31)])  3.58 us
    all_to_all x1, starting transfers between devices, shards(): lax.all_to_all(jnp.broadcast_to(near[None], (4,) + near.shape), ('xh', 'x...  3.52 us
  transfers between devices with their start and end apart: 8, of which 4 were waited for; matrix products, arithmetic and copies ran while one was open for 2% of the time, Pallas kernels for 7%

profile of v9, /device:TPU:1, one launch (start us, length us, event | category | flops | bytes accessed | tf_op | source)
XLA Modules:
  0.0 92.2 jit_solution(7325317938318151640)
XLA Ops:
  0.0 17.7 %all-to-all-start = ((bf16[32,32,128]{2,1,0:T(8,128)(2,1)}), bf16[32,32,128]{2,1,0:T(8,128)(2,1)S(1)}, u32[]{:S(2)}, u32[]{:S(2)}) async-start(bf16[32,32,128]{2,1,0:T(8,128)(2,1)} %bitcast.27), calls=%async_computation | async-start | bytes 524288 | tf_op jit(solution)/shard_map/all_to_all | solution.py:257
  17.7 0.7 and_add_fusion
  18.4 0.6 fusion
  23.9 0.7 convert_element_type.19
  24.6 0.1 reshape.32
  27.1 1.4 %shard_map.55 = bf16[16,128]{1,0:T(8,128)(2,1)} custom-call(s32[4,4]{1,0:T(4,128)} %offset_ref.1, bf16[4,4,4]{2,1,0:T(4,128)(2,1)} %taps_ref.1), custom_call_target="tpu_custom_call" | custom-call | tf_op jit(solution)/shard_map/pallas_call | solution.py:264
  28.6 0.1 stack.31.ids
  28.7 0.5 all-to-all-done
  29.2 17.1 %all_to_all.15 = bf16[8,128,128]{2,1,0:T(8,128)(2,1)S(1)} all-to-all(bf16[8,128,128]{2,1,0:T(8,128)(2,1)S(1)} %broadcast_in_dim.8), channel_id=1, replica_groups=mesh['ya'=4,'yb'=2,'xl'=2,'core'=2,'z'=16,'xh'=2] {'ya','yb'}, dimensions={0} | all-to-all | bytes 524288 | tf_op jit(solution)/shard_map/all_to_all | solution.py:274
  46.4 0.0 copy-start
  46.4 1.1 %broadcast_in_dim.9 = bf16[4,1040,128]{2,1,0:T(8,128)(2,1)} broadcast(bf16[1040,128]{1,0:T(8,128)(2,1)S(1)} %pad_maximum_fusion.1), dimensions={1,2} | broadcast | bytes 1331200 | tf_op jit(solution)/shard_map/broadcast_in_dim | solution.py:280
  47.5 3.5 %all-to-all-start.2 = ((bf16[4,1040,128]{2,1,0:T(8,128)(2,1)}), bf16[4,1040,128]{2,1,0:T(8,128)(2,1)S(1)}, u32[]{:S(2)}, u32[]{:S(2)}) async-start(bf16[4,1040,128]{2,1,0:T(8,128)(2,1)} %broadcast_in_dim.9), calls=%async_computation.2 | async-start | bytes 2129920 | tf_op jit(solution)/shard_map/all_to_all | solution.py:279
  51.0 1.3 %collective-permute-start = (bf16[1040,128]{1,0:T(8,128)(2,1)S(1)}, bf16[1040,128]{1,0:T(8,128)(2,1)S(1)}, u32[]{:S(2)}, u32[]{:S(2)}) collective-permute-start(bf16[1040,128]{1,0:T(8,128)(2,1)S(1)} %pad_maximum_fusion.1), channel_id=1, source_target_pairs={{2,0},{4,2},{6,4},{8,6},{10,8},{12,10},{14,12},{16,14},{18,16},{20... | collective-permute-start | bytes 798728 | tf_op jit(solution)/shard_map/ppermute | solution.py:278
  52.3 0.0 copy-done
  52.3 3.6 %collective-permute-start.2 = (bf16[16,128]{1,0:T(8,128)(2,1)S(1)}, bf16[16,128]{1,0:T(8,128)(2,1)S(1)}, u32[]{:S(2)}, u32[]{:S(2)}) collective-permute-start(bf16[16,128]{1,0:T(8,128)(2,1)S(1)} %copy-done), channel_id=1, source_target_pairs={{32,0},{64,32},{96,64},{128,96},{160,128},{192,160},{224,192},{256... | collective-permute-start | bytes 12296 | tf_op jit(solution)/shard_map/ppermute | solution.py:284
  55.9 3.5 %collective-permute-start.1 = (bf16[16,128]{1,0:T(8,128)(2,1)S(1)}, bf16[16,128]{1,0:T(8,128)(2,1)S(1)}, u32[]{:S(2)}, u32[]{:S(2)}) collective-permute-start(bf16[16,128]{1,0:T(8,128)(2,1)S(1)} %copy-done), channel_id=1, source_target_pairs={{0,32},{32,64},{64,96},{96,128},{128,160},{160,192},{192,224},{224... | collective-permute-start | bytes 12296 | tf_op jit(solution)/shard_map/ppermute | solution.py:283
  59.4 5.9 %collective-permute-done.2 = bf16[16,128]{1,0:T(8,128)(2,1)S(1)} collective-permute-done((bf16[16,128]{1,0:T(8,128)(2,1)S(1)}, bf16[16,128]{1,0:T(8,128)(2,1)S(1)}, u32[]{:S(2)}, u32[]{:S(2)}) %collective-permute-start.2) | collective-permute-done | bytes 4128 | tf_op jit(solution)/shard_map/ppermute | solution.py:284
  65.4 0.0 collective-permute-done.1
  65.4 0.0 collective-permute-done
  65.4 0.0 all-to-all-done.2
  65.4 1.3 %collective-permute-start.3 = (bf16[1040,128]{1,0:T(8,128)(2,1)S(1)}, bf16[1040,128]{1,0:T(8,128)(2,1)S(1)}, u32[]{:S(2)}, u32[]{:S(2)}) collective-permute-start(bf16[1040,128]{1,0:T(8,128)(2,1)S(1)} %dynamic-slice_bitcast_fusion), channel_id=1, source_target_pairs={{0,2},{2,4},{4,6},{6,8},{8,10},{10,12},{12,14},{14,16},{16,18},{18... | collective-permute-start | bytes 798728 | tf_op jit(solution)/shard_map/ppermute | solution.py:292
  66.7 2.0 %collective-permute-start.4 = (bf16[1040,128]{1,0:T(8,128)(2,1)S(1)}, bf16[1040,128]{1,0:T(8,128)(2,1)S(1)}, u32[]{:S(2)}, u32[]{:S(2)}) collective-permute-start(bf16[1040,128]{1,0:T(8,128)(2,1)S(1)} %collective-permute-done), channel_id=1, source_target_pairs={{0,65},{1,64},{64,1},{65,0},{2,67},{3,66},{66,3},{67,2},{4,69},{5,... | collective-permute-start | bytes 798728 | tf_op jit(solution)/shard_map/ppermute | solution.py:293
  68.7 2.0 %collective-permute-done.3 = bf16[1040,128]{1,0:T(8,128)(2,1)S(1)} collective-permute-done((bf16[1040,128]{1,0:T(8,128)(2,1)S(1)}, bf16[1040,128]{1,0:T(8,128)(2,1)S(1)}, u32[]{:S(2)}, u32[]{:S(2)}) %collective-permute-start.3) | collective-permute-done | bytes 266272 | tf_op jit(solution)/shard_map/ppermute | solution.py:292
  70.7 5.1 %collective-permute-done.4 = bf16[1040,128]{1,0:T(8,128)(2,1)S(1)} collective-permute-done((bf16[1040,128]{1,0:T(8,128)(2,1)S(1)}, bf16[1040,128]{1,0:T(8,128)(2,1)S(1)}, u32[]{:S(2)}, u32[]{:S(2)}) %collective-permute-start.4) | collective-permute-done | bytes 266272 | tf_op jit(solution)/shard_map/ppermute | solution.py:293
  75.8 0.2 pad_maximum_fusion.own_ref
  76.0 4.8 %collective-permute-start.5 = (bf16[6,1040,128]{2,1,0:T(8,128)(2,1)S(1)}, bf16[6,1040,128]{2,1,0:T(8,128)(2,1)S(1)}, u32[]{:S(2)}, u32[]{:S(2)}) collective-permute-start(bf16[6,1040,128]{2,1,0:T(8,128)(2,1)S(1)} %pad_maximum_fusion.own_ref), channel_id=1, source_target_pairs={{0,32},{32,0},{1,33},{33,1},{2,34},{34,2},{3,35},{35,3},{4,36},{36... | collective-permute-start | bytes 4792328 | tf_op jit(solution)/shard_map/ppermute | solution.py:297
  80.8 5.4 %shard_map.56.rest_1_ = f32[4,32,4096]{2,1,0:T(8,128)} custom-call(s32[5]{0:T(128)S(1)} %stack.31.ids, f32[3,128]{1,0:T(4,128)S(1)} %maximum_convert_fusion.prm_ref, f32[1,128]{1,0:T(1,128)S(1)} %convert_element_type.20.band_ref, bf16[6,1040,128]{2,1,0:T(8,128)(2,1)S(1)} %pad_maximum_fusion.own_ref), custom_call_target="tpu_custom_call" | custom-call | flops 503316480 | bytes 25165824 | tf_op jit(solution)/shard_map/pallas_call | solution.py:212
  86.2 0.0 collective-permute-done.5.rest_0_
  86.2 6.0 %shard_map.57 = f32[4,32,4096]{2,1,0:T(8,128)} custom-call(s32[5]{0:T(128)S(1)} %stack.31.ids, f32[3,128]{1,0:T(4,128)S(1)} %maximum_convert_fusion.prm_ref, f32[1,128]{1,0:T(1,128)S(1)} %convert_element_type.20.band_ref, bf16[6,1040,128]{2,1,0:T(8,128)(2,1)S(1)} %pad_maximum_fusion.own_ref, ...), custom_call_target="tpu_custom_call", output_to_operand_aliasing={{}: (5, {})} | custom-call | flops 566231040 | bytes 25165824 | tf_op jit(solution)/shard_map/pallas_call | solution.py:212
  (12 shorter events, 0.1 us)
Async XLA Ops:
  0.0 29.1 %all-to-all-start = ((bf16[32,32,128]{2,1,0:T(8,128)(2,1)}), bf16[32,32,128]{2,1,0:T(8,128)(2,1)S(1)}, u32[]{:S(2)}, u32[]{:S(2)}) async-start(bf16[32,32,128]{2,1,0:T(8,128)(2,1)} %bitcast.27), calls=%async_computation | async-start | bytes 524288 | tf_op jit(solution)/shard_map/all_to_all | solution.py:257
  46.4 6.0 %copy-start = (bf16[16,128]{1,0:T(8,128)(2,1)S(1)}, bf16[16,128]{1,0:T(8,128)(2,1)}, u32[]{:S(2)}) copy-start(bf16[16,128]{1,0:T(8,128)(2,1)} %shard_map.55) | copy-start | bytes 12292
  47.5 17.9 %all-to-all-start.2 = ((bf16[4,1040,128]{2,1,0:T(8,128)(2,1)}), bf16[4,1040,128]{2,1,0:T(8,128)(2,1)S(1)}, u32[]{:S(2)}, u32[]{:S(2)}) async-start(bf16[4,1040,128]{2,1,0:T(8,128)(2,1)} %broadcast_in_dim.9), calls=%async_computation.2 | async-start | bytes 2129920 | tf_op jit(solution)/shard_map/all_to_all | solution.py:279
  51.0 14.3 %collective-permute-start = (bf16[1040,128]{1,0:T(8,128)(2,1)S(1)}, bf16[1040,128]{1,0:T(8,128)(2,1)S(1)}, u32[]{:S(2)}, u32[]{:S(2)}) collective-permute-start(bf16[1040,128]{1,0:T(8,128)(2,1)S(1)} %pad_maximum_fusion.1), channel_id=1, source_target_pairs={{2,0},{4,2},{6,4},{8,6},{10,8},{12,10},{14,12},{16,14},{18,16},{20... | collective-permute-start | bytes 798728 | tf_op jit(solution)/shard_map/ppermute | solution.py:278
  52.3 13.0 %collective-permute-start.2 = (bf16[16,128]{1,0:T(8,128)(2,1)S(1)}, bf16[16,128]{1,0:T(8,128)(2,1)S(1)}, u32[]{:S(2)}, u32[]{:S(2)}) collective-permute-start(bf16[16,128]{1,0:T(8,128)(2,1)S(1)} %copy-done), channel_id=1, source_target_pairs={{32,0},{64,32},{96,64},{128,96},{160,128},{192,160},{224,192},{256... | collective-permute-start | bytes 12296 | tf_op jit(solution)/shard_map/ppermute | solution.py:284
  55.9 9.4 %collective-permute-start.1 = (bf16[16,128]{1,0:T(8,128)(2,1)S(1)}, bf16[16,128]{1,0:T(8,128)(2,1)S(1)}, u32[]{:S(2)}, u32[]{:S(2)}) collective-permute-start(bf16[16,128]{1,0:T(8,128)(2,1)S(1)} %copy-done), channel_id=1, source_target_pairs={{0,32},{32,64},{64,96},{96,128},{128,160},{160,192},{192,224},{224... | collective-permute-start | bytes 12296 | tf_op jit(solution)/shard_map/ppermute | solution.py:283
  65.4 5.3 %collective-permute-start.3 = (bf16[1040,128]{1,0:T(8,128)(2,1)S(1)}, bf16[1040,128]{1,0:T(8,128)(2,1)S(1)}, u32[]{:S(2)}, u32[]{:S(2)}) collective-permute-start(bf16[1040,128]{1,0:T(8,128)(2,1)S(1)} %dynamic-slice_bitcast_fusion), channel_id=1, source_target_pairs={{0,2},{2,4},{4,6},{6,8},{8,10},{10,12},{12,14},{14,16},{16,18},{18... | collective-permute-start | bytes 798728 | tf_op jit(solution)/shard_map/ppermute | solution.py:292
  66.7 9.1 %collective-permute-start.4 = (bf16[1040,128]{1,0:T(8,128)(2,1)S(1)}, bf16[1040,128]{1,0:T(8,128)(2,1)S(1)}, u32[]{:S(2)}, u32[]{:S(2)}) collective-permute-start(bf16[1040,128]{1,0:T(8,128)(2,1)S(1)} %collective-permute-done), channel_id=1, source_target_pairs={{0,65},{1,64},{64,1},{65,0},{2,67},{3,66},{66,3},{67,2},{4,69},{5,... | collective-permute-start | bytes 798728 | tf_op jit(solution)/shard_map/ppermute | solution.py:293
  76.0 10.2 %collective-permute-start.5 = (bf16[6,1040,128]{2,1,0:T(8,128)(2,1)S(1)}, bf16[6,1040,128]{2,1,0:T(8,128)(2,1)S(1)}, u32[]{:S(2)}, u32[]{:S(2)}) collective-permute-start(bf16[6,1040,128]{2,1,0:T(8,128)(2,1)S(1)} %pad_maximum_fusion.own_ref), channel_id=1, source_target_pairs={{0,32},{32,0},{1,33},{33,1},{2,34},{34,2},{3,35},{35,3},{4,36},{36... | collective-permute-start | bytes 4792328 | tf_op jit(solution)/shard_map/ppermute | solution.py:297

commit v10 on v9

--- a/solution.py
+++ b/solution.py
@@ -260,26 +260,26 @@
         [lax.dynamic_index_in_dim(got, place[v], keepdims=False) for v in range(VIEWS)]
     )
     views = views.reshape(VIEWS, 4, 8, LANES).transpose(1, 0, 2, 3).reshape(SIZE, LANES)
+    band = band_start.astype(BF16).reshape(1, SIZE)
+    rest = (band.astype(F32), jnp.pad(band, ((0, 15), (0, 0))), ids)
+    views, (band, band_rows, ids) = lax.optimization_barrier((views, rest))
+    near = lax.all_to_all(jnp.broadcast_to(views[None], (8, SIZE, LANES)), ALONG_Y, 0, 0, tiled=True)
+    near = jnp.concatenate([near.reshape(8 * SIZE, LANES), band_rows])
+
+    shift = [(2 * i + 2, 2 * i) for i in range(15)] + [(2 * i + 1, 2 * i + 3) for i in range(15)]
+    foreign = lax.ppermute(near, ("z", "xh"), shift)
+    own = lax.all_to_all(
+        jnp.broadcast_to(near[None], (4,) + near.shape), ("xh", "xl"), 0, 0, tiled=True
+    )
+
+    _, offsets = lax.optimization_barrier((near, row_offset))
     whole = pl.BlockSpec(memory_space=pltpu.VMEM)
     numbers = pl.pallas_call(
         line_up,
         out_shape=jax.ShapeDtypeStruct((16, LANES), BF16),
         in_specs=[whole] * 2,
         out_specs=whole,
-    )(row_offset, taps)
-
-    band = band_start.astype(BF16).reshape(1, SIZE)
-    rest = (band.astype(F32), jnp.pad(band, ((0, 15), (0, 0))), ids, numbers)
-    views, (band, band_rows, ids, numbers) = lax.optimization_barrier((views, rest))
-    near = lax.all_to_all(jnp.broadcast_to(views[None], (8, SIZE, LANES)), ALONG_Y, 0, 0, tiled=True)
-    near = jnp.concatenate([near.reshape(8 * SIZE, LANES), band_rows])
-
-    shift = [(2 * i + 2, 2 * i) for i in range(15)] + [(2 * i + 1, 2 * i + 3) for i in range(15)]
-    foreign = lax.ppermute(near, ("z", "xh"), shift)
-    own = lax.all_to_all(
-        jnp.broadcast_to(near[None], (4,) + near.shape), ("xh", "xl"), 0, 0, tiled=True
-    )
-
+    )(offsets, taps)
     lower = lax.ppermute(numbers, DEPTH, [(i, i + 1) for i in range(31)])
     upper = lax.ppermute(numbers, DEPTH, [(i + 1, i) for i in range(31)])
     own, foreign, lower, upper = lax.optimization_barrier((own, foreign, lower, upper))

time: 92.8 us -> 92.3 us (level)
  blocking collectives: 17.1 us -> 15.9 us
    ppermute x1, waiting for transfers between devices: 5.92 us -> 4.52 us  [shards(): upper = lax.ppermute(numbers, DEPTH, [(i + 1, i) for i in range(31)])]
    all_to_all x1, waiting for transfers between devices: 0.48 us -> 1.69 us  [shards(): lax.all_to_all(pieces.reshape(32, TILE, LANES), order, 0, 0, tiled=True)]
    all_to_all x1, blocking collectives: 17.1 us -> 15.9 us  [shards(): lax.all_to_all(jnp.broadcast_to(views[None], (8, SIZE, LANES)), ALONG_Y,...]
  transfers between devices with their start and end apart: 8 -> 8, of which waited for: 4 -> 4; matrix products, arithmetic and copies ran while one was open for 2% -> 3% of each run, Pallas kernels for 7% -> 7%
where the time goes in v10:
time: 92.3 us; the launch traced here: 91.7 us
  starting transfers between devices  37.7 us (41%)
  blocking collectives  15.9 us (17%)
  waiting for transfers between devices  13.3 us (14%)
  Pallas kernels  12.8 us (14%)
  between operations  7.69 us (8%)
  local copies, waits for them, and re-layouts  2.69 us (3%)
  other arithmetic  1.59 us (2%)
    all_to_all x1, starting transfers between devices, shards(): lax.all_to_all(pieces.reshape(32, TILE, LANES), order, 0, 0, tiled=True)  17.7 us
    all_to_all x1, blocking collectives, shards(): lax.all_to_all(jnp.broadcast_to(views[None], (8, SIZE, LANES)), ALONG_Y,...  15.9 us
    pallas_call x2, Pallas kernels, smooth(): pl.pallas_call(functools.partial(half, second), out_shape=jax.ShapeDtypeS...  11.4 us
    ppermute x1, waiting for transfers between devices, shards(): lax.ppermute(foreign, ('xl', 'xh'), [(0, 3), (1, 2), (2, 1), (3, 0)])  5.05 us
    ppermute x1, starting transfers between devices, shards(): other = lax.ppermute(own, 'core', swap)  4.76 us
    ppermute x1, waiting for transfers between devices, shards(): upper = lax.ppermute(numbers, DEPTH, [(i + 1, i) for i in range(31)])  4.52 us
    ppermute x1, starting transfers between devices, shards(): upper = lax.ppermute(numbers, DEPTH, [(i + 1, i) for i in range(31)])  3.57 us
    all_to_all x1, starting transfers between devices, shards(): lax.all_to_all(jnp.broadcast_to(near[None], (4,) + near.shape), ('xh', 'x...  3.52 us
  transfers between devices with their start and end apart: 8, of which 4 were waited for; matrix products, arithmetic and copies ran while one was open for 3% of the time, Pallas kernels for 7%

profile of v10, /device:TPU:1, one launch (start us, length us, event | category | flops | bytes accessed | tf_op | source)
XLA Modules:
  0.0 91.7 jit_solution(3361769781000700799)
XLA Ops:
  0.0 17.7 %all-to-all-start = ((bf16[32,32,128]{2,1,0:T(8,128)(2,1)}), bf16[32,32,128]{2,1,0:T(8,128)(2,1)S(1)}, u32[]{:S(2)}, u32[]{:S(2)}) async-start(bf16[32,32,128]{2,1,0:T(8,128)(2,1)} %bitcast.27), calls=%async_computation | async-start | bytes 524288 | tf_op jit(solution)/shard_map/all_to_all | solution.py:257
  17.7 0.7 and_add_fusion
  18.4 0.7 fusion
  24.1 0.7 convert_element_type.19
  24.7 0.1 reshape.32
  27.4 0.1 stack.31.ids
  27.5 1.7 %all-to-all-done = bf16[32,32,128]{2,1,0:T(8,128)(2,1)S(1)} async-done(((bf16[32,32,128]{2,1,0:T(8,128)(2,1)}), bf16[32,32,128]{2,1,0:T(8,128)(2,1)S(1)}, u32[]{:S(2)}, u32[]{:S(2)}) %all-to-all-start) | async-done | bytes 262176 | tf_op jit(solution)/shard_map/all_to_all | solution.py:257
  29.2 15.9 %all_to_all.15 = bf16[8,128,128]{2,1,0:T(8,128)(2,1)S(1)} all-to-all(bf16[8,128,128]{2,1,0:T(8,128)(2,1)S(1)} %broadcast_in_dim.8), channel_id=1, replica_groups=mesh['ya'=4,'yb'=2,'xl'=2,'core'=2,'z'=16,'xh'=2] {'ya','yb'}, dimensions={0} | all-to-all | bytes 524288 | tf_op jit(solution)/shard_map/all_to_all | solution.py:266
  45.2 1.1 %broadcast_in_dim.9 = bf16[4,1040,128]{2,1,0:T(8,128)(2,1)} broadcast(bf16[1040,128]{1,0:T(8,128)(2,1)S(1)} %pad_maximum_fusion.1), dimensions={1,2} | broadcast | bytes 1331200 | tf_op jit(solution)/shard_map/broadcast_in_dim | solution.py:272
  46.3 3.5 %all-to-all-start.2 = ((bf16[4,1040,128]{2,1,0:T(8,128)(2,1)}), bf16[4,1040,128]{2,1,0:T(8,128)(2,1)S(1)}, u32[]{:S(2)}, u32[]{:S(2)}) async-start(bf16[4,1040,128]{2,1,0:T(8,128)(2,1)} %broadcast_in_dim.9), calls=%async_computation.2 | async-start | bytes 2129920 | tf_op jit(solution)/shard_map/all_to_all | solution.py:271
  49.8 1.3 %collective-permute-start = (bf16[1040,128]{1,0:T(8,128)(2,1)S(1)}, bf16[1040,128]{1,0:T(8,128)(2,1)S(1)}, u32[]{:S(2)}, u32[]{:S(2)}) collective-permute-start(bf16[1040,128]{1,0:T(8,128)(2,1)S(1)} %pad_maximum_fusion.1), channel_id=1, source_target_pairs={{2,0},{4,2},{6,4},{8,6},{10,8},{12,10},{14,12},{16,14},{18,16},{20... | collective-permute-start | bytes 798728 | tf_op jit(solution)/shard_map/ppermute | solution.py:270
  51.1 1.4 %shard_map.55 = bf16[16,128]{1,0:T(8,128)(2,1)} custom-call(s32[4,4]{1,0:T(4,128)} %offset_ref, bf16[4,4,4]{2,1,0:T(4,128)(2,1)} %taps_ref.1), custom_call_target="tpu_custom_call" | custom-call | tf_op jit(solution)/shard_map/pallas_call | solution.py:277
  52.5 3.6 %collective-permute-start.2 = (bf16[16,128]{1,0:T(8,128)(2,1)}, bf16[16,128]{1,0:T(8,128)(2,1)S(1)}, u32[]{:S(2)}, u32[]{:S(2)}) collective-permute-start(bf16[16,128]{1,0:T(8,128)(2,1)} %shard_map.55), channel_id=1, source_target_pairs={{32,0},{64,32},{96,64},{128,96},{160,128},{192,160},{224,192},{256... | collective-permute-start | bytes 12296 | tf_op jit(solution)/shard_map/ppermute | solution.py:284
  56.1 3.5 %collective-permute-start.1 = (bf16[16,128]{1,0:T(8,128)(2,1)}, bf16[16,128]{1,0:T(8,128)(2,1)S(1)}, u32[]{:S(2)}, u32[]{:S(2)}) collective-permute-start(bf16[16,128]{1,0:T(8,128)(2,1)} %shard_map.55), channel_id=1, source_target_pairs={{0,32},{32,64},{64,96},{96,128},{128,160},{160,192},{192,224},{224... | collective-permute-start | bytes 12296 | tf_op jit(solution)/shard_map/ppermute | solution.py:283
  59.6 4.5 %collective-permute-done.2 = bf16[16,128]{1,0:T(8,128)(2,1)S(1)} collective-permute-done((bf16[16,128]{1,0:T(8,128)(2,1)}, bf16[16,128]{1,0:T(8,128)(2,1)S(1)}, u32[]{:S(2)}, u32[]{:S(2)}) %collective-permute-start.2) | collective-permute-done | bytes 4128 | tf_op jit(solution)/shard_map/ppermute | solution.py:284
  64.1 0.0 collective-permute-done.1
  64.1 0.0 collective-permute-done
  64.2 0.0 all-to-all-done.2
  64.2 1.3 %collective-permute-start.3 = (bf16[1040,128]{1,0:T(8,128)(2,1)S(1)}, bf16[1040,128]{1,0:T(8,128)(2,1)S(1)}, u32[]{:S(2)}, u32[]{:S(2)}) collective-permute-start(bf16[1040,128]{1,0:T(8,128)(2,1)S(1)} %dynamic-slice_bitcast_fusion), channel_id=1, source_target_pairs={{0,2},{2,4},{4,6},{6,8},{8,10},{10,12},{12,14},{14,16},{16,18},{18... | collective-permute-start | bytes 798728 | tf_op jit(solution)/shard_map/ppermute | solution.py:292
  65.5 2.0 %collective-permute-start.4 = (bf16[1040,128]{1,0:T(8,128)(2,1)S(1)}, bf16[1040,128]{1,0:T(8,128)(2,1)S(1)}, u32[]{:S(2)}, u32[]{:S(2)}) collective-permute-start(bf16[1040,128]{1,0:T(8,128)(2,1)S(1)} %collective-permute-done), channel_id=1, source_target_pairs={{0,65},{1,64},{64,1},{65,0},{2,67},{3,66},{66,3},{67,2},{4,69},{5,... | collective-permute-start | bytes 798728 | tf_op jit(solution)/shard_map/ppermute | solution.py:293
  67.5 2.0 %collective-permute-done.3 = bf16[1040,128]{1,0:T(8,128)(2,1)S(1)} collective-permute-done((bf16[1040,128]{1,0:T(8,128)(2,1)S(1)}, bf16[1040,128]{1,0:T(8,128)(2,1)S(1)}, u32[]{:S(2)}, u32[]{:S(2)}) %collective-permute-start.3) | collective-permute-done | bytes 266272 | tf_op jit(solution)/shard_map/ppermute | solution.py:292
  69.5 5.1 %collective-permute-done.4 = bf16[1040,128]{1,0:T(8,128)(2,1)S(1)} collective-permute-done((bf16[1040,128]{1,0:T(8,128)(2,1)S(1)}, bf16[1040,128]{1,0:T(8,128)(2,1)S(1)}, u32[]{:S(2)}, u32[]{:S(2)}) %collective-permute-start.4) | collective-permute-done | bytes 266272 | tf_op jit(solution)/shard_map/ppermute | solution.py:293
  74.6 0.2 pad_maximum_fusion.own_ref
  74.8 4.8 %collective-permute-start.5 = (bf16[6,1040,128]{2,1,0:T(8,128)(2,1)S(1)}, bf16[6,1040,128]{2,1,0:T(8,128)(2,1)S(1)}, u32[]{:S(2)}, u32[]{:S(2)}) collective-permute-start(bf16[6,1040,128]{2,1,0:T(8,128)(2,1)S(1)} %pad_maximum_fusion.own_ref), channel_id=1, source_target_pairs={{0,32},{32,0},{1,33},{33,1},{2,34},{34,2},{3,35},{35,3},{4,36},{36... | collective-permute-start | bytes 4792328 | tf_op jit(solution)/shard_map/ppermute | solution.py:297
  79.5 0.7 slice.28
  80.2 5.4 %shard_map.56.rest_1_ = f32[4,32,4096]{2,1,0:T(8,128)} custom-call(s32[5]{0:T(128)S(1)} %stack.31.ids, f32[3,128]{1,0:T(4,128)S(1)} %maximum_convert_fusion.prm_ref, f32[1,128]{1,0:T(1,128)S(1)} %convert_element_type.20.band_ref, bf16[6,1040,128]{2,1,0:T(8,128)(2,1)S(1)} %pad_maximum_fusion.own_ref), custom_call_target="tpu_custom_call" | custom-call | flops 503316480 | bytes 25165824 | tf_op jit(solution)/shard_map/pallas_call | solution.py:212
  85.6 0.0 collective-permute-done.5.rest_0_
  85.6 6.0 %shard_map.57 = f32[4,32,4096]{2,1,0:T(8,128)} custom-call(s32[5]{0:T(128)S(1)} %stack.31.ids, f32[3,128]{1,0:T(4,128)S(1)} %maximum_convert_fusion.prm_ref, f32[1,128]{1,0:T(1,128)S(1)} %convert_element_type.20.band_ref, bf16[6,1040,128]{2,1,0:T(8,128)(2,1)S(1)} %pad_maximum_fusion.own_ref, ...), custom_call_target="tpu_custom_call", output_to_operand_aliasing={{}: (5, {})} | custom-call | flops 566231040 | bytes 25165824 | tf_op jit(solution)/shard_map/pallas_call | solution.py:212
  (11 shorter events, 0.1 us)
Async XLA Ops:
  0.0 29.1 %all-to-all-start = ((bf16[32,32,128]{2,1,0:T(8,128)(2,1)}), bf16[32,32,128]{2,1,0:T(8,128)(2,1)S(1)}, u32[]{:S(2)}, u32[]{:S(2)}) async-start(bf16[32,32,128]{2,1,0:T(8,128)(2,1)} %bitcast.27), calls=%async_computation | async-start | bytes 524288 | tf_op jit(solution)/shard_map/all_to_all | solution.py:257
  46.3 17.9 %all-to-all-start.2 = ((bf16[4,1040,128]{2,1,0:T(8,128)(2,1)}), bf16[4,1040,128]{2,1,0:T(8,128)(2,1)S(1)}, u32[]{:S(2)}, u32[]{:S(2)}) async-start(bf16[4,1040,128]{2,1,0:T(8,128)(2,1)} %broadcast_in_dim.9), calls=%async_computation.2 | async-start | bytes 2129920 | tf_op jit(solution)/shard_map/all_to_all | solution.py:271
  49.8 14.3 %collective-permute-start = (bf16[1040,128]{1,0:T(8,128)(2,1)S(1)}, bf16[1040,128]{1,0:T(8,128)(2,1)S(1)}, u32[]{:S(2)}, u32[]{:S(2)}) collective-permute-start(bf16[1040,128]{1,0:T(8,128)(2,1)S(1)} %pad_maximum_fusion.1), channel_id=1, source_target_pairs={{2,0},{4,2},{6,4},{8,6},{10,8},{12,10},{14,12},{16,14},{18,16},{20... | collective-permute-start | bytes 798728 | tf_op jit(solution)/shard_map/ppermute | solution.py:270
  52.5 11.6 %collective-permute-start.2 = (bf16[16,128]{1,0:T(8,128)(2,1)}, bf16[16,128]{1,0:T(8,128)(2,1)S(1)}, u32[]{:S(2)}, u32[]{:S(2)}) collective-permute-start(bf16[16,128]{1,0:T(8,128)(2,1)} %shard_map.55), channel_id=1, source_target_pairs={{32,0},{64,32},{96,64},{128,96},{160,128},{192,160},{224,192},{256... | collective-permute-start | bytes 12296 | tf_op jit(solution)/shard_map/ppermute | solution.py:284
  56.1 8.0 %collective-permute-start.1 = (bf16[16,128]{1,0:T(8,128)(2,1)}, bf16[16,128]{1,0:T(8,128)(2,1)S(1)}, u32[]{:S(2)}, u32[]{:S(2)}) collective-permute-start(bf16[16,128]{1,0:T(8,128)(2,1)} %shard_map.55), channel_id=1, source_target_pairs={{0,32},{32,64},{64,96},{96,128},{128,160},{160,192},{192,224},{224... | collective-permute-start | bytes 12296 | tf_op jit(solution)/shard_map/ppermute | solution.py:283
  64.2 5.3 %collective-permute-start.3 = (bf16[1040,128]{1,0:T(8,128)(2,1)S(1)}, bf16[1040,128]{1,0:T(8,128)(2,1)S(1)}, u32[]{:S(2)}, u32[]{:S(2)}) collective-permute-start(bf16[1040,128]{1,0:T(8,128)(2,1)S(1)} %dynamic-slice_bitcast_fusion), channel_id=1, source_target_pairs={{0,2},{2,4},{4,6},{6,8},{8,10},{10,12},{12,14},{14,16},{16,18},{18... | collective-permute-start | bytes 798728 | tf_op jit(solution)/shard_map/ppermute | solution.py:292
  65.5 9.1 %collective-permute-start.4 = (bf16[1040,128]{1,0:T(8,128)(2,1)S(1)}, bf16[1040,128]{1,0:T(8,128)(2,1)S(1)}, u32[]{:S(2)}, u32[]{:S(2)}) collective-permute-start(bf16[1040,128]{1,0:T(8,128)(2,1)S(1)} %collective-permute-done), channel_id=1, source_target_pairs={{0,65},{1,64},{64,1},{65,0},{2,67},{3,66},{66,3},{67,2},{4,69},{5,... | collective-permute-start | bytes 798728 | tf_op jit(solution)/shard_map/ppermute | solution.py:293
  74.8 10.9 %collective-permute-start.5 = (bf16[6,1040,128]{2,1,0:T(8,128)(2,1)S(1)}, bf16[6,1040,128]{2,1,0:T(8,128)(2,1)S(1)}, u32[]{:S(2)}, u32[]{:S(2)}) collective-permute-start(bf16[6,1040,128]{2,1,0:T(8,128)(2,1)S(1)} %pad_maximum_fusion.own_ref), channel_id=1, source_target_pairs={{0,32},{32,0},{1,33},{33,1},{2,34},{34,2},{3,35},{35,3},{4,36},{36... | collective-permute-start | bytes 4792328 | tf_op jit(solution)/shard_map/ppermute | solution.py:297
